TPU v7x, 128 devices: a whole 4x4x4 slice. The times are simulated.
128 devices in a mesh: label: 32 (over z, y, x_lo), dp: 4 (over x_hi, core).
Axes of the slice: x: 4 (x_hi: 2, x_lo: 2; x = x_hi * 2 + x_lo), y: 4, z: 4, core: 2. Of those that a mesh axis runs over, the one named last changes fastest.
Arguments:
- queries: bfloat16 [16384, 1024], P(('label', 'dp')), may hold values from -6 to 6
- label_ids: int32 [16384, 8], P(('label', 'dp')), may hold values from 0 to 32767
- label_counts: int32 [16384], P(('label', 'dp')), may hold values from 1 to 8
- weights: bfloat16 [32768, 1024], P('label'), may hold values from -0.1875 to 0.1875
- encoder: bfloat16 [1024, 192], replicated, may hold values from -0.1875 to 0.1875
- decoder: bfloat16 [192, 1024], replicated, may hold values from -6 to 6
Outputs:
- query_grad: bfloat16 [16384, 1024], P(('label', 'dp'))
- weight_grad: bfloat16 [32768, 1024], P('label', 'dp')
Inputs may be any that keep to these rules, and one draw needn't show every extreme that they name: `label_ids`: entries of a row past that row's count are ignored; a row may name a label more than once.
All inputs are finite; a program needn't handle non-finite values.
Results may differ from a plain program's by a relative error of at most 0.0033.
Values may be sent and summed in bfloat16 or wider, within the bound.
No kernel may reach another device: no remote copies, remote signals or barrier semaphores. Data moves between devices by JAX's collectives and lax.ppermute only.
A program may use at most 192 MiB of HBM per device.

v0:
```python
import jax
import jax.numpy as jnp
from jax import lax
from jax.sharding import PartitionSpec as P


def shards(queries, label_ids, label_counts, weights, encoder, decoder):
    num_label = lax.axis_size("label")
    num_groups = lax.axis_size("dp")
    scale = float(queries.shape[0] * num_label * num_groups) ** (-0.5)
    shard_len = weights.shape[0]
    offset = lax.axis_index("label") * shard_len
    rows_all, ids_all, counts_all = (
        lax.all_gather(queries, "label", axis=0, tiled=True),
        lax.all_gather(label_ids, "label", axis=0, tiled=True),
        lax.all_gather(label_counts, "label", axis=0, tiled=True),
    )
    logits = lax.dot_general(
        rows_all, weights, (((1,), (1,)), ((), ())), preferred_element_type=jnp.float32
    )
    local = ids_all - offset
    live = jnp.arange(ids_all.shape[1], dtype=jnp.int32)[None, :] < counts_all[:, None]
    labels_here = jnp.arange(shard_len, dtype=jnp.int32)
    hit = (local[:, :, None] == labels_here[None, None, :]) & live[:, :, None]
    target = jnp.any(hit, axis=1).astype(jnp.float32)
    grad = ((jax.nn.sigmoid(logits) - target) * scale).astype(jnp.bfloat16)
    partial_value = jnp.dot(grad, weights, preferred_element_type=jnp.float32)
    encoded = jnp.dot(partial_value, encoder.astype(jnp.float32), precision=lax.Precision.HIGHEST)
    summed = lax.psum_scatter(encoded, "label", scatter_dimension=0, tiled=True)
    query_grad = jnp.dot(
        summed, decoder.astype(jnp.float32), precision=lax.Precision.HIGHEST
    ).astype(jnp.bfloat16)
    wpart = lax.dot_general(
        grad, rows_all, (((0,), (0,)), ((), ())), preferred_element_type=jnp.float32
    )
    weight_grad = lax.psum_scatter(wpart, "dp", scatter_dimension=1, tiled=True).astype(
        jnp.bfloat16
    )
    return (query_grad, weight_grad)


def solution(mesh):
    placed = (
        P(("label", "dp"), None),
        P(("label", "dp"), None),
        P(("label", "dp")),
        P("label", None),
        P(),
        P(),
    )
    return jax.shard_map(
        shards,
        mesh=mesh,
        in_specs=placed,
        out_specs=(P(("label", "dp"), None), P("label", "dp")),
        check_vma=False,
    )
```

profile of v0, /device:TPU:1, one launch (start us, length us, event | category | flops | bytes accessed | tf_op | source)
XLA Modules:
  0.0 490.2 jit_solution(4182407581739229832)
XLA Ops:
  7.2 0.0 copy-start
  7.2 0.0 all-gather.3.cloned.1.call-start
  7.2 0.7 all-gather.3.cloned.1.call-update
  7.9 0.0 reduce-scatter.3.cloned.1.call-start
  8.0 73.4 %all-gather = s32[32,1,128]{2,1,0:T(1,128)S(1)} all-gather(s32[1,1,128]{2,1,0:T(1,128)} %bitcast.13), channel_id=1, replica_groups=mesh['label'=32,'dp'=4] {'label'}, dimensions={0}, use_global_device_ids=true | all-gather | bytes 16896 | tf_op jit(solution)/shard_map/all_gather | solution.py:16
  81.4 0.8 copy.11
  82.3 67.6 %all_gather.10 = s32[4096,8]{0,1:T(8,128)S(1)} all-gather(s32[128,8]{0,1:T(8,128)} %param.7), channel_id=1, replica_groups=mesh['label'=32,'dp'=4] {'label'}, dimensions={0}, use_global_device_ids=true | all-gather | bytes 135168 | tf_op jit(solution)/shard_map/all_gather | solution.py:15
  149.9 2.0 copy.10
  151.8 52.0 %fusion.1 = pred[4096,1024]{1,0:T(8,128)(4,1)} fusion(s32[4096,8]{1,0:T(8,128)} %copy.10, pred[4096,8]{1,0:T(8,128)(4,1)S(1)} %copy.11), kind=kLoop, calls=%fused_computation.2 | loop fusion | flops 96468992 | bytes 4358144 | tf_op jit(solution)/shard_map/reduce_or | solution.py:25
  203.8 2.1 all-gather.3.cloned.1.call-done
  206.0 0.0 copy-done
  206.0 18.4 %multiply_convert_fusion = bf16[4096,1024]{1,0:T(8,128)(2,1)} fusion(pred[4096,1024]{1,0:T(8,128)(4,1)} %fusion.1, bf16[4096,1024]{1,0:T(8,128)(2,1)} %all-gather.3.cloned.1.call-done, bf16[1024,1024]{1,0:T(8,128)(2,1)S(1)} %copy-done), kind=kOutput, calls=%fused_computation.3 | convolution fusion | flops 8619294720 | bytes 23068672 | tf_op jit(solution)/shard_map/dot_general | solution.py:18
  224.4 0.0 copy-start.1
  224.4 11.3 %fusion.2 = f32[4096,1024]{1,0:T(8,128)S(1)} fusion(bf16[4096,1024]{1,0:T(8,128)(2,1)} %multiply_convert_fusion, bf16[1024,1024]{1,0:T(8,128)(2,1)S(1)} %copy-done), kind=kOutput, calls=%fused_computation.7 | convolution fusion | flops 8589934592 | bytes 27262976 | tf_op jit(solution)/shard_map/dot_general | solution.py:27
  235.8 0.0 copy-done.1
  235.8 11.5 %fusion.3 = f32[4096,192]{0,1:T(8,128)} fusion(f32[4096,1024]{1,0:T(8,128)S(1)} %fusion.2, bf16[1024,192]{0,1:T(8,128)(2,1)S(1)} %copy-done.1), kind=kOutput, calls=%fused_computation.8 | convolution fusion | flops 9663676416 | bytes 20316160 | tf_op jit(solution)/shard_map/dot_general | solution.py:28
  247.3 0.0 reduce-scatter.3.cloned.1.call-update
  247.3 0.0 copy-start.2
  247.3 0.0 reduce-scatter.5.cloned.1.call-start
  247.4 15.1 %fusion.4 = f32[1024,1024]{1,0:T(8,128)} fusion(bf16[4096,1024]{1,0:T(8,128)(2,1)} %multiply_convert_fusion, bf16[4096,1024]{1,0:T(8,128)(2,1)} %all-gather.3.cloned.1.call-done), kind=kOutput, calls=%fused_computation.9 | convolution fusion | flops 8589934592 | bytes 20971520 | tf_op jit(solution)/shard_map/dot_general | solution.py:33
  262.5 0.0 reduce-scatter.5.cloned.1.call-update
  262.5 148.0 %reduce-scatter.3.cloned.1.call-done = f32[128,192]{0,1:T(8,128)} async-done(((f32[4096,192]{0,1:T(8,128)}), f32[128,192]{0,1:T(8,128)}) %reduce-scatter.3.cloned.1.call-update) | async-done | bytes 98320 | tf_op jit(solution)/shard_map/reduce_scatter | solution.py:29
  410.4 0.0 copy-done.2
  410.4 2.0 convolution_convert_fusion
  412.5 69.1 %reduce-scatter.5.cloned.1.call-done = f32[1024,256]{1,0:T(8,128)} async-done(((f32[1024,1024]{1,0:T(8,128)}), f32[1024,256]{1,0:T(8,128)}) %reduce-scatter.5.cloned.1.call-update) | async-done | bytes 1048592 | tf_op jit(solution)/shard_map/reduce_scatter | solution.py:36
  481.6 2.1 convert_element_type.17
  (2 shorter events, 0.0 us)
Async XLA Ops:
  7.2 198.8 %copy-start = (bf16[1024,1024]{1,0:T(8,128)(2,1)S(1)}, bf16[1024,1024]{1,0:T(8,128)(2,1)}, u32[]{:S(2)}) copy-start(bf16[1024,1024]{1,0:T(8,128)(2,1)} %param.9) | copy-start | bytes 6291460
  7.2 198.8 %all-gather.3.cloned.1.call-start = ((), (), s32[]{:S(2)}) async-start(), calls=%async_computation.2 | async-start | bytes 8650752 | tf_op jit(solution)/shard_map/all_gather | solution.py:14
  7.9 402.5 %reduce-scatter.3.cloned.1.call-start = ((), (), s32[]{:S(2)}) async-start(), calls=%async_computation.3 | async-start | bytes 3244032 | tf_op jit(solution)/shard_map/reduce_scatter | solution.py:29
  224.4 11.3 %copy-start.1 = (bf16[1024,192]{0,1:T(8,128)(2,1)S(1)}, bf16[1024,192]{0,1:T(8,128)(2,1)}, u32[]{:S(2)}) copy-start(bf16[1024,192]{0,1:T(8,128)(2,1)} %param.10) | copy-start | bytes 1179652
  247.3 163.1 %copy-start.2 = (bf16[192,1024]{1,0:T(8,128)(2,1)S(1)}, bf16[192,1024]{1,0:T(8,128)(2,1)}, u32[]{:S(2)}) copy-start(bf16[192,1024]{1,0:T(8,128)(2,1)} %param.11) | copy-start | bytes 1179652
  247.3 234.3 %reduce-scatter.5.cloned.1.call-start = ((), (), s32[]{:S(2)}) async-start(), calls=%async_computation.4 | async-start | bytes 5242880 | tf_op jit(solution)/shard_map/reduce_scatter | solution.py:36
Sparse Core Ops, SparseCore 0:
  9.7 196.2 all-gather.2
  247.4 162.9 reduce-scatter.2
  413.3 68.2 reduce-scatter.4
where the time goes:
time: 490 us
  waiting for transfers between devices  220 us (45%)
  blocking collectives  141 us (29%)
  matrix products  58.4 us (12%)
  other arithmetic  54.1 us (11%)
  between operations  13.8 us (3%)
    reduce_scatter x1, waiting for transfers between devices, shards(): summed = lax.psum_scatter(encoded, 'label', scatter_dimension=0, tiled=True)  148 us
    all_gather x1, blocking collectives, shards(): lax.all_gather(label_counts, 'label', axis=0, tiled=True)  73.4 us
    reduce_scatter x1, waiting for transfers between devices, shards(): lax.psum_scatter(wpart, 'dp', scatter_dimension=1, tiled=True)  69.1 us
    all_gather x1, blocking collectives, shards(): lax.all_gather(label_ids, 'label', axis=0, tiled=True)  67.6 us
    reduce_or x1, other arithmetic, shards(): target = jnp.any(hit, axis=1).astype(jnp.float32)  52 us
    dot_general x1, matrix products, shards(): lax.dot_general(rows_all, weights, (((1,), (1,)), ((), ())), preferred_el...  18.4 us
    dot_general x1, matrix products, shards(): lax.dot_general(grad, rows_all, (((0,), (0,)), ((), ())), preferred_eleme...  15.1 us
    dot_general x1, matrix products, shards(): jnp.dot(partial_value, encoder.astype(jnp.float32), precision=lax.Precisi...  11.5 us
  transfers between devices with their start and end apart: 3, of which 3 were waited for; matrix products, arithmetic and copies ran while one was open for 15% of the time, Pallas kernels for 0%

commit v1 on v0

v1 whole, which is shorter than its diff:
```python
import functools
import itertools

import jax
import jax.numpy as jnp
from jax import lax
from jax.experimental import pallas as pl
from jax.experimental.pallas import tpu as pltpu
from jax.sharding import Mesh, PartitionSpec as P

AXES = ("z", "y", "xl", "xh", "core")
BF16, F32, I32 = jnp.bfloat16, jnp.float32, jnp.int32
TAIL = 16
BLOCK = 256


def pairs(target):
    flat = lambda z, y, x, c: (((z % 4 * 4 + y % 4) * 2 + x % 2) * 2 + x % 4 // 2) * 2 + c
    places = itertools.product(range(4), range(4), range(4), range(2))
    return [(flat(*at), flat(*target(*at))) for at in places if target(*at) is not None]


def move(array, target):
    return lax.ppermute(array, AXES, pairs(target))


def hop(phase, step):
    return lambda z, y, x, c: (z + step, y, x, c) if c == phase else (z, y + step, x, c)


def to_sibling(z, y, x, c):
    return z, y, x, 1 - c


def weights_from(step):
    return lambda z, y, x, c: (z, y, x + step, c) if c == x % 2 else (z, y, x, 1 - c)


def encode_kernel(w_ref, enc_ref, out_ref):
    we = lax.dot_general(
        enc_ref[...], w_ref[...], (((1,), (1,)), ((), ())), preferred_element_type=F32
    )
    high = we.astype(BF16)
    out_ref[:192, :] = high
    out_ref[192:, :] = (we - high.astype(F32)).astype(BF16)


def target_bits(tail, block, base, step):
    digits = tail[2 * block : 2 * block + 2, :]
    local = (digits[0:1] * 256 + digits[1:2]) - base
    word = jnp.where((local >> 8) == step, jnp.left_shift(1, (local >> 3) & 31), 0)
    low = local & 7
    row = lax.broadcasted_iota(I32, (8, 128), 0)
    bits = jnp.zeros((8, 128), I32)
    for slot in range(8):
        lanes = slice(slot * 128, (slot + 1) * 128)
        here = jnp.broadcast_to(low[:, lanes], (8, 128)) == row
        bits = bits | jnp.where(here, jnp.broadcast_to(word[:, lanes], (8, 128)), 0)
    return bits


def chunk_kernel(pieces, n_q, enc_widths, first, last, scale, *refs):
    place = refs[0]
    q_refs = refs[1 : 1 + n_q]
    w_ref, wet_ref = refs[1 + n_q : 3 + n_q]
    rest = refs[3 + n_q :]
    if not first:
        total_ref, rest = rest[0], rest[1:]
    enc_refs, outs = rest[: len(enc_widths)], rest[len(enc_widths) :]
    step = pl.program_id(0)
    base = place[0]
    w = w_ref[...]
    wet = wet_ref[...]

    @pl.when(step == 0)
    def _():
        for ref in enc_refs:
            ref[...] = jnp.zeros_like(ref)

    group = lax.broadcasted_iota(I32, (BLOCK // 8, 1, 1), 0)
    total = None if first else total_ref[...]
    tails = {}
    for q, rows, t, offset, block, out, column in pieces:
        if t not in tails:
            tails[t] = q_refs[t][offset : offset + TAIL, :].astype(F32).astype(I32)
        queries = q_refs[q][:rows, :]
        logits = lax.dot_general(
            w, queries, (((1,), (1,)), ((), ())), preferred_element_type=F32
        )
        bits = jnp.concatenate(
            [target_bits(tails[t], block + b, base, step) for b in range(rows // 128)], axis=1
        )
        hit = (bits[None] >> group) & 1
        target = hit.reshape(BLOCK, rows).astype(F32)
        grad = ((jax.nn.sigmoid(logits) - target) * scale).astype(BF16)
        encoded = jnp.dot(wet, grad, preferred_element_type=F32)
        enc_refs[out][:, column : column + rows] += encoded[:192] + encoded[192:]
        part = jnp.dot(grad, queries, preferred_element_type=F32)
        total = part if total is None else total + part
    if last:
        left, right = total[:, :512], total[:, 512:]
        swap = place[1] == 0
        outs[0][...] = jnp.where(swap, left, right).astype(BF16)
        other = jnp.where(swap, right, left)
        outs[1][...] = other.astype(BF16)
        outs[2][...] = other
    else:
        outs[0][...] = total


def chunk(place, q_bufs, pieces, w, wet, total, enc_widths, last, scale):
    labels, width = w.shape
    first = total is None
    whole = lambda a: pl.BlockSpec(a.shape, lambda i: (0,) * a.ndim)
    rows = lambda n: pl.BlockSpec((BLOCK, n), lambda i: (i, 0))
    in_specs = [pl.BlockSpec(memory_space=pltpu.SMEM)]
    in_specs += [whole(a) for a in q_bufs]
    in_specs += [rows(width), pl.BlockSpec((2 * 192, BLOCK), lambda i: (0, i))]
    args = [place, *q_bufs, w, wet]
    if not first:
        in_specs.append(rows(width))
        args.append(total)
    shapes = [jax.ShapeDtypeStruct((192, n), F32) for n in enc_widths]
    out_specs = [whole(s) for s in shapes]
    if last:
        shapes += [jax.ShapeDtypeStruct((labels, 512), d) for d in (BF16, BF16, F32)]
        out_specs += [rows(512)] * 3
    else:
        shapes.append(jax.ShapeDtypeStruct((labels, width), F32))
        out_specs.append(rows(width))
    n = sum(p[1] for p in pieces)
    return pl.pallas_call(
        functools.partial(chunk_kernel, pieces, len(q_bufs), enc_widths, first, last, scale),
        grid=(labels // BLOCK,),
        in_specs=in_specs,
        out_specs=out_specs,
        out_shape=shapes,
        compiler_params=pltpu.CompilerParams(vmem_limit_bytes=40 * 2**20),
        cost_estimate=pl.CostEstimate(
            flops=2 * n * labels * (2 * width + 384), bytes_accessed=8 * 2**20, transcendentals=0
        ),
        name="chunk",
    )(*args)


def pack_kernel(index_ref, *refs):
    own, sib, out = refs[:4], refs[4:8], refs[8]
    for part in range(4):
        for block in range(4):
            lanes = slice(block * 128, block * 128 + 128)
            value = own[part][:, lanes] + sib[part][:, lanes]
            out[index_ref[part * 4 + block]] = value.astype(BF16)


def decode_kernel(parts_ref, dec_ref, out_ref):
    total = parts_ref[0].astype(F32)
    for i in range(1, 16):
        total += parts_ref[i].astype(F32)
    dec = dec_ref[...]
    rest, result = total, None
    for _ in range(3):
        digit = rest.astype(BF16)
        rest = rest - digit.astype(F32)
        part = lax.dot_general(digit, dec, (((0,), (0,)), ((), ())), preferred_element_type=F32)
        result = part if result is None else result + part
    out_ref[...] = result.astype(BF16)


def join_kernel(flag_ref, own_ref, a_ref, b_ref, c_ref, mine_ref, sib_ref):
    total = own_ref[...] + a_ref[...].astype(F32) + b_ref[...].astype(F32) + c_ref[...].astype(F32)
    total = total.astype(BF16)
    left, right = total[:, :256], total[:, 256:]
    first = flag_ref[0] == 0
    mine_ref[...] = jnp.where(first, left, right)
    sib_ref[...] = jnp.where(first, right, left)


def shards(queries, label_ids, label_counts, weights, encoder, decoder):
    z, y, xl, xh, core = (lax.axis_index(a) for a in AXES)
    x = 2 * xh + xl
    scale = float(queries.shape[0] * 128) ** (-0.5)
    labels = weights.shape[0]

    slot = lax.broadcasted_iota(I32, (8, 128), 0)
    ids = jnp.where(slot < label_counts[None, :], label_ids.T, 255 * 256).reshape(1, 1024)
    tail = jnp.concatenate([ids >> 8, ids & 255, jnp.zeros((TAIL - 2, 1024), I32)], axis=0)
    own = jnp.concatenate([queries, tail.astype(BF16)], axis=0)

    back, ahead = move(own, hop(0, 1)), move(own, hop(0, -1))
    w = jnp.concatenate(
        [move(weights[: labels // 2], weights_from(1)), move(weights[labels // 2 :], weights_from(-1))], axis=0
    )
    far0, far1 = move(back[:64], hop(0, 1)), move(ahead[64:], hop(0, -1))
    row = jnp.concatenate(
        [own[:128], back[:128], ahead[:128], far0, far1[:64]]
        + [own[128:130], back[128:130], ahead[128:130], far1[64:66], own[136:144]],
        axis=0,
    )
    row_back, row_ahead = move(row, hop(1, 1)), move(row, hop(1, -1))
    row_far0, row_far1 = move(row_back[:256], hop(1, 1)), move(row_ahead[256:], hop(1, -1))

    shard = (z * 4 + y) * 2 + core
    away = jnp.where(core == xl, 1 - xh, (x + 1) % 4 // 2)
    place = jnp.stack([shard * labels, away]).astype(I32)
    wet = pl.pallas_call(
        encode_kernel, out_shape=jax.ShapeDtypeStruct((384, labels), BF16), name="encode"
    )(w, encoder.T)

    whole = lambda q, out, column: (q, 512, q, 512, 0, out, column)
    enc_a, enc_sa, total = chunk(
        place, [row, move(row, to_sibling)], [whole(0, 0, 0), whole(1, 1, 0)],
        w, wet, None, (512, 512), False, scale,
    )
    enc_b, total = chunk(
        place, [row_back, row_ahead], [whole(0, 0, 0), whole(1, 0, 512)],
        w, wet, total, (1024,), False, scale,
    )
    enc_sb, total = chunk(
        place, [move(row_back, to_sibling), move(row_ahead, to_sibling)], [whole(0, 0, 0), whole(1, 0, 512)],
        w, wet, total, (1024,), False, scale,
    )
    half = lambda q, t, block, out: (q, 256, t, 256, block, out, block * 128)
    enc_c, enc_sc, out_a, out_b, kept = chunk(
        place, [row_far0, row_far1, move(row_far0, to_sibling), move(row_far1, to_sibling)],
        [half(0, 1, 0, 0), half(1, 1, 2, 0), half(2, 3, 0, 1), half(3, 3, 2, 1)],
        w, wet, total, (512, 512), True, scale,
    )

    other = lambda step: lambda z, y, x, c: (z, y, x + step, c) if c != x % 2 else None
    same = lambda z, y, x, c: (z, y, x + 2, c) if c == x % 2 else None
    got = [move(out_a, other(1)), move(out_b, other(-1)), move(out_a, same)]

    got_a, got_b, got_c = move(enc_sa, to_sibling), move(enc_sb, to_sibling), move(enc_sc, to_sibling)
    shift = jnp.array([0, 3, 1, 2], I32)
    first, second = jnp.where(core == 0, z, y), jnp.where(core == 0, y, z)
    first, second = (first + shift[None, :]) % 4, (second + shift[:, None]) % 4
    index = jnp.where(core == 0, first * 4 + second, second * 4 + first).reshape(16).astype(I32)
    vmem = pl.BlockSpec(memory_space=pltpu.VMEM)
    smem = pl.BlockSpec(memory_space=pltpu.SMEM)
    part = lambda j: pl.BlockSpec((192, 512), lambda i: (0, j))
    packed = pl.pallas_call(
        pack_kernel,
        grid=(1,),
        in_specs=[smem, part(0), part(0), part(1), part(0), part(0), part(0), part(1), part(0)],
        out_specs=pl.BlockSpec((16, 192, 128), lambda i: (0, 0, 0)),
        out_shape=jax.ShapeDtypeStruct((16, 192, 128), BF16),
        name="pack",
    )(index, enc_a, enc_b, enc_b, enc_c, got_a, got_b, got_b, got_c)
    parts = lax.all_to_all(packed, ("z", "y"), split_axis=0, concat_axis=0, tiled=True)
    query_grad = pl.pallas_call(
        decode_kernel, out_shape=jax.ShapeDtypeStruct((128, 1024), BF16), name="decode"
    )(parts, decoder)

    wide = pl.BlockSpec((256, 512), lambda i: (i, 0))
    narrow = pl.BlockSpec((256, 256), lambda i: (i, 0))
    mine, sib = pl.pallas_call(
        join_kernel,
        grid=(labels // 256,),
        in_specs=[smem, wide, wide, wide, wide],
        out_specs=[narrow, narrow],
        out_shape=[jax.ShapeDtypeStruct((labels, 256), BF16)] * 2,
        name="join",
    )(core.astype(I32).reshape(1), kept, *got)
    sib = move(sib, lambda z, y, x, c: (z, y, x, 1 - c) if c == x % 2 else None)
    weight_grad = jnp.where(core == xl, mine, sib)
    return query_grad, weight_grad


def solution(mesh):
    fine = Mesh(mesh.devices.reshape(4, 4, 2, 2, 2), AXES)
    label, dp = AXES[:3], AXES[3:]
    return jax.shard_map(
        shards,
        mesh=fine,
        in_specs=(P(AXES, None), P(AXES, None), P(AXES), P(label, None), P(), P()),
        out_specs=(P(AXES, None), P(label, dp)),
        check_vma=False,
    )
```

time: 490 us -> 138 us (0.28)
  waiting for transfers between devices: 220 us -> 25 us
  blocking collectives: 141 us -> 0 us
  matrix products: 58.4 us -> 0 us
  Pallas kernels: 0 us -> 52.6 us
  other arithmetic: 54.1 us -> 2.78 us
  starting transfers between devices: 0.12 us -> 35.7 us
  local copies, waits for them, and re-layouts: 2.8 us -> 19 us
  between operations: 13.8 us -> 0.89 us
    reduce_scatter x2 -> x0, waiting for transfers between devices: 217 us -> none  [the longest x1 148 us: shards(): summed = lax.psum_scatter(encoded, 'label', scatter_dimension=0, tiled=True)]
    all_gather x2 -> x0, blocking collectives: 141 us -> none  [the longest x1 73.4 us: shards(): lax.all_gather(label_counts, 'label', axis=0, tiled=True)]
    dot_general x5 -> x0, matrix products: 58.4 us -> none  [the longest x1 18.4 us: shards(): lax.dot_general(rows_all, weights, (((1,), (1,)), ((), ())), preferred_el...]
    pallas_call x0 -> x8, Pallas kernels: none -> 52.6 us  [the longest x4 39.5 us: chunk(): pl.pallas_call(functools.partial(chunk_kernel, pieces, len(q_bufs), enc_w...]
    reduce_or x1 -> x0, other arithmetic: 52 us -> none  [shards(): target = jnp.any(hit, axis=1).astype(jnp.float32)]
    ppermute x0 -> x22, starting transfers between devices: none -> 31 us  [move(): return lax.ppermute(array, AXES, pairs(target))]
    ppermute x0 -> x22, waiting for transfers between devices: none -> 25 us  [move(): return lax.ppermute(array, AXES, pairs(target))]
    unnamed x6 -> x21, local copies, waits for them, and re-layouts: 0.02 us -> 10 us
  transfers between devices with their start and end apart: 3 -> 23, of which waited for: 3 -> 7; matrix products, arithmetic and copies ran while one was open for 15% -> 8% of each run, Pallas kernels for 0% -> 39%
where the time goes in v1:
time: 138 us; the launch traced here: 136 us
  Pallas kernels  52.6 us (38%)
  starting transfers between devices  35.7 us (26%)
  waiting for transfers between devices  25 us (18%)
  local copies, waits for them, and re-layouts  19 us (14%)
  other arithmetic  2.78 us (2%)
    pallas_call x4, Pallas kernels, chunk(): pl.pallas_call(functools.partial(chunk_kernel, pieces, len(q_bufs), enc_w...  39.5 us
    ppermute x22, starting transfers between devices, move(): return lax.ppermute(array, AXES, pairs(target))  31 us
    ppermute x22, waiting for transfers between devices, move(): return lax.ppermute(array, AXES, pairs(target))  25 us
    unnamed x21, local copies, waits for them, and re-layouts  10 us
    all_to_all x1, starting transfers between devices, shards(): lax.all_to_all(packed, ('z', 'y'), split_axis=0, concat_axis=0, tiled=True)  4.66 us
    pallas_call x1, Pallas kernels, shards(): pl.pallas_call(join_kernel, grid=(labels // 256,), in_specs=[smem, wide,...  4.26 us
    pallas_call x1, Pallas kernels, shards(): pl.pallas_call(encode_kernel, out_shape=jax.ShapeDtypeStruct((384, labels...  3.39 us
    pallas_call x1, Pallas kernels, shards(): pl.pallas_call(pack_kernel, grid=(1,), in_specs=[smem, part(0), part(0),...  3.04 us
  transfers between devices with their start and end apart: 23, of which 7 were waited for; matrix products, arithmetic and copies ran while one was open for 8% of the time, Pallas kernels for 39%

profile of v1, /device:TPU:1, one launch (start us, length us, event | category | flops | bytes accessed | tf_op | source)
XLA Modules:
  0.0 135.9 jit_solution(864435824921685261)
XLA Ops:
  0.6 0.7 fusion
  1.3 0.1 pad.3.clone
  1.4 1.1 maximum_maximum_fusion
  2.5 2.2 %collective-permute-start = (bf16[144,1024]{1,0:T(8,128)(2,1)S(1)}, bf16[144,1024]{1,0:T(8,128)(2,1)S(1)}, u32[]{:S(2)}, u32[]{:S(2)}) collective-permute-start(bf16[144,1024]{1,0:T(8,128)(2,1)S(1)} %maximum_maximum_fusion), channel_id=1, source_target_pairs={{0,32},{1,9},{4,36},{5,13},{2,34},{3,11},{6,38},{7,15},{8,40},{9,1... | collective-permute-start | bytes 884744 | tf_op jit(solution)/shard_map/ppermute | solution.py:24
  4.7 1.5 %collective-permute-start.1 = (bf16[144,1024]{1,0:T(8,128)(2,1)S(1)}, bf16[144,1024]{1,0:T(8,128)(2,1)S(1)}, u32[]{:S(2)}, u32[]{:S(2)}) collective-permute-start(bf16[144,1024]{1,0:T(8,128)(2,1)S(1)} %maximum_maximum_fusion), channel_id=1, source_target_pairs={{0,96},{1,25},{4,100},{5,29},{2,98},{3,27},{6,102},{7,31},{8,104},... | collective-permute-start | bytes 884744 | tf_op jit(solution)/shard_map/ppermute | solution.py:24
  6.2 4.3 %collective-permute-done = bf16[144,1024]{1,0:T(8,128)(2,1)S(1)} collective-permute-done((bf16[144,1024]{1,0:T(8,128)(2,1)S(1)}, bf16[144,1024]{1,0:T(8,128)(2,1)S(1)}, u32[]{:S(2)}, u32[]{:S(2)}) %collective-permute-start) | collective-permute-done | bytes 294944 | tf_op jit(solution)/shard_map/ppermute | solution.py:24
  10.5 0.1 collective-permute-start.2
  10.7 0.0 copy-start.8
  10.7 2.7 %collective-permute-start.3 = (bf16[80,1024]{1,0:T(8,128)(2,1)S(1)}, bf16[80,1024]{1,0:T(8,128)(2,1)S(1)}, u32[]{:S(2)}, u32[]{:S(2)}) collective-permute-start(bf16[80,1024]{1,0:T(8,128)(2,1)S(1)} %slice.58), channel_id=1, source_target_pairs={{0,96},{1,25},{4,100},{5,29},{2,98},{3,27},{6,102},{7,31},{8,104},... | collective-permute-start | bytes 491528 | tf_op jit(solution)/shard_map/ppermute | solution.py:24
  13.4 2.7 %fusion.4 = (bf16[512,1024]{1,0:T(8,128)(2,1)}, bf16[512,1024]{1,0:T(8,128)(2,1)S(1)}) fusion(bf16[1024,1024]{1,0:T(8,128)(2,1)} %param.10), kind=kLoop, calls=%fused_computation.24 | loop fusion | bytes 4194304 | tf_op jit(solution)/shard_map/slice | solution.py:191
  16.1 2.8 %collective-permute-start.5 = (bf16[512,1024]{1,0:T(8,128)(2,1)S(1)}, bf16[512,1024]{1,0:T(8,128)(2,1)}, u32[]{:S(2)}, u32[]{:S(2)}) collective-permute-start(bf16[512,1024]{1,0:T(8,128)(2,1)S(1)} %get-tuple-element.35), channel_id=1, source_target_pairs={{0,4},{1,0},{4,5},{5,3},{2,6},{3,2},{6,7},{7,1},{8,12},{9,8},{12,1... | collective-permute-start | bytes 3145736 | tf_op jit(solution)/shard_map/ppermute | solution.py:24
  19.1 0.3 concatenate.15.refs_1_
  19.4 0.1 collective-permute-start.7
  19.5 2.7 %collective-permute-start.8 = (bf16[528,1024]{1,0:T(8,128)(2,1)S(1)}, bf16[528,1024]{1,0:T(8,128)(2,1)}, u32[]{:S(2)}, u32[]{:S(2)}) collective-permute-start(bf16[528,1024]{1,0:T(8,128)(2,1)S(1)} %concatenate.15.refs_1_), channel_id=1, source_target_pairs={{0,24},{1,97},{4,28},{5,101},{2,26},{3,99},{6,30},{7,103},{8,0},{9... | collective-permute-start | bytes 3244040 | tf_op jit(solution)/shard_map/ppermute | solution.py:24
  22.2 2.1 %collective-permute-start.6 = (bf16[512,1024]{1,0:T(8,128)(2,1)}, bf16[512,1024]{1,0:T(8,128)(2,1)}, u32[]{:S(2)}, u32[]{:S(2)}) collective-permute-start(bf16[512,1024]{1,0:T(8,128)(2,1)} %get-tuple-element.34), channel_id=1, source_target_pairs={{0,6},{1,0},{4,5},{5,1},{2,4},{3,2},{6,7},{7,3},{8,14},{9,8},{12,1... | collective-permute-start | bytes 3145736 | tf_op jit(solution)/shard_map/ppermute | solution.py:24
  24.2 1.3 collective-permute-start.4
  25.5 0.1 pad_add_fusion.refs_0_
  25.6 5.7 %collective-permute-done.5 = bf16[512,1024]{1,0:T(8,128)(2,1)} collective-permute-done((bf16[512,1024]{1,0:T(8,128)(2,1)S(1)}, bf16[512,1024]{1,0:T(8,128)(2,1)}, u32[]{:S(2)}, u32[]{:S(2)}) %collective-permute-start.5) | collective-permute-done | bytes 1048608 | tf_op jit(solution)/shard_map/ppermute | solution.py:24
  31.4 1.3 constant_dynamic-update-slice_fusion.1
  32.6 2.5 %collective-permute-done.7.refs_1_ = bf16[528,1024]{1,0:T(8,128)(2,1)} collective-permute-done((bf16[528,1024]{1,0:T(8,128)(2,1)S(1)}, bf16[528,1024]{1,0:T(8,128)(2,1)}, u32[]{:S(2)}, u32[]{:S(2)}) %collective-permute-start.7) | collective-permute-done | bytes 1081376 | tf_op jit(solution)/shard_map/ppermute | solution.py:24
  35.1 1.9 %slice.63 = bf16[256,1024]{1,0:T(8,128)(2,1)} slice(bf16[528,1024]{1,0:T(8,128)(2,1)} %collective-permute-done.7.refs_1_), slice={[0:256], [0:1024]} | slice | bytes 1048576 | tf_op jit(solution)/shard_map/slice | solution.py:200
  37.0 0.0 collective-permute-start.9
  37.0 0.0 collective-permute-done.8.refs_2_
  37.0 1.9 %slice.64 = bf16[272,1024]{1,0:T(8,128)(2,1)} slice(bf16[528,1024]{1,0:T(8,128)(2,1)} %collective-permute-done.8.refs_2_), slice={[256:528], [0:1024]} | slice | bytes 1114112 | tf_op jit(solution)/shard_map/slice | solution.py:200
  38.9 2.7 %collective-permute-start.10 = (bf16[272,1024]{1,0:T(8,128)(2,1)}, bf16[272,1024]{1,0:T(8,128)(2,1)}, u32[]{:S(2)}, u32[]{:S(2)}) collective-permute-start(bf16[272,1024]{1,0:T(8,128)(2,1)} %slice.64), channel_id=1, source_target_pairs={{0,24},{1,97},{4,28},{5,101},{2,26},{3,99},{6,30},{7,103},{8,0},{9... | collective-permute-start | bytes 1671176 | tf_op jit(solution)/shard_map/ppermute | solution.py:24
  41.6 2.9 %collective-permute-start.13 = (bf16[528,1024]{1,0:T(8,128)(2,1)}, bf16[528,1024]{1,0:T(8,128)(2,1)}, u32[]{:S(2)}, u32[]{:S(2)}) collective-permute-start(bf16[528,1024]{1,0:T(8,128)(2,1)} %collective-permute-done.7.refs_1_), channel_id=1, source_target_pairs={{0,1},{1,0},{4,5},{5,4},{2,3},{3,2},{6,7},{7,6},{8,9},{9,8},{12,13... | collective-permute-start | bytes 3244040 | tf_op jit(solution)/shard_map/ppermute | solution.py:24
  44.5 0.0 collective-permute-start.14
  44.5 1.3 constant_dynamic-update-slice_fusion.w_ref.refs_3_.refs_5_
  45.8 1.4 %copy-done = bf16[1024,1024]{1,0:T(8,128)(2,1)} copy-done((bf16[1024,1024]{1,0:T(8,128)(2,1)}, bf16[1024,1024]{1,0:T(8,128)(2,1)S(1)}, u32[]{:S(2)}) %copy-start) | copy-done | bytes 2097176
  47.2 3.4 %encode.1.refs_4_.refs_6_ = bf16[384,1024]{1,0:T(8,128)(2,1)} custom-call(bf16[1024,1024]{1,0:T(8,128)(2,1)} %copy-done, bf16[192,1024]{1,0:T(8,128)(2,1)} %bitcast.24), custom_call_target="tpu_custom_call" | custom-call | tf_op jit(solution)/shard_map/encode/pallas_call | solution.py:205
  50.6 0.0 collective-permute-done.4.refs_2_
  50.6 1.6 %copy-done.1 = bf16[1024,1024]{1,0:T(8,128)(2,1)S(1)} copy-done((bf16[1024,1024]{1,0:T(8,128)(2,1)S(1)}, bf16[1024,1024]{1,0:T(8,128)(2,1)}, u32[]{:S(2)}) %copy-start.1) | copy-done | bytes 2097176
  52.2 1.1 copy-done.4
  53.3 9.3 %chunk.4 = (f32[192,512]{1,0:T(8,128)S(1)}, f32[192,512]{1,0:T(8,128)}, f32[1024,1024]{1,0:T(8,128)S(1)}) custom-call(s32[2]{0:T(128)S(1)} %pad_add_fusion.refs_0_, bf16[528,1024]{1,0:T(8,128)(2,1)S(1)} %concatenate.15.refs_1_, bf16[528,1024]{1,0:T(8,128)(2,1)} %collective-permute-done.4.refs_2_, bf16[1024,1024]{1,0:T(8,128)(2,1)S(1)} %copy-done.1, ...), custom_call_target="tpu_custom_call" | custom-call | flops 5100273664 | bytes 8388608 | tf_op jit(solution)/shard_map/chunk/pallas_call | solution.py:132
  62.6 0.7 copy-done.5
  63.3 0.5 collective-permute-start.15
  63.8 0.0 collective-permute-done.9.refs_1_
  63.8 0.0 collective-permute-start.11
  63.8 0.5 collective-permute-start.12
  64.3 9.4 %chunk.5 = (f32[192,1024]{1,0:T(8,128)S(1)}, f32[1024,1024]{1,0:T(8,128)S(1)}) custom-call(s32[2]{0:T(128)S(1)} %pad_add_fusion.refs_0_, bf16[528,1024]{1,0:T(8,128)(2,1)} %collective-permute-done.7.refs_1_, bf16[528,1024]{1,0:T(8,128)(2,1)} %collective-permute-done.8.refs_2_, bf16[1024,1024]{1,0:T(8,128)(2,1)S(1)} %copy-done.1, ...), custom_call_target="tpu_custom_call" | custom-call | flops 5100273664 | bytes 8388608 | tf_op jit(solution)/shard_map/chunk/pallas_call | solution.py:132
  73.7 0.9 copy-done.2
  74.6 9.5 %chunk.6 = (f32[192,1024]{1,0:T(8,128)S(1)}, f32[1024,1024]{1,0:T(8,128)S(1)}) custom-call(s32[2]{0:T(128)S(1)} %pad_add_fusion.refs_0_, bf16[528,1024]{1,0:T(8,128)(2,1)} %collective-permute-done.13.refs_1_, bf16[528,1024]{1,0:T(8,128)(2,1)} %collective-permute-done.14.refs_2_, bf16[1024,1024]{1,0:T(8,128)(2,1)S(1)} %copy-done.1, ...), custom_call_target="tpu_custom_call" | custom-call | flops 5100273664 | bytes 8388608 | tf_op jit(solution)/shard_map/chunk/pallas_call | solution.py:132
  84.1 0.0 copy-start.9
  84.1 11.3 %chunk.7 = (f32[192,512]{1,0:T(8,128)S(1)}, f32[192,512]{1,0:T(8,128)S(1)}, bf16[1024,512]{1,0:T(8,128)(2,1)S(1)}, bf16[1024,512]{1,0:T(8,128)(2,1)S(1)}, f32[1024,512]{1,0:T(8,128)S(1)}) custom-call(s32[2]{0:T(128)S(1)} %pad_add_fusion.refs_0_, bf16[256,1024]{1,0:T(8,128)(2,1)} %collective-permute-done.9.refs_1_, ...), custom_call_target="tpu_custom_call" | custom-call | flops 5100273664 | bytes 8388608 | tf_op jit(solution)/shard_map/chunk/pallas_call | solution.py:132
  95.5 1.4 copy-done.3
  96.9 0.7 copy-done.6
  97.6 2.7 %collective-permute-start.18 = (bf16[1024,512]{1,0:T(8,128)(2,1)S(1)}, bf16[1024,512]{1,0:T(8,128)(2,1)}, u32[]{:S(2)}, u32[]{:S(2)}) collective-permute-start(bf16[1024,512]{1,0:T(8,128)(2,1)S(1)} %get-tuple-element.26), channel_id=1, source_target_pairs={{1,5},{4,2},{3,7},{6,0},{9,13},{12,10},{11,15},{14,8},{17,21},{20,... | collective-permute-start | bytes 3145736 | tf_op jit(solution)/shard_map/ppermute | solution.py:24
  100.3 2.6 %collective-permute-start.19 = (bf16[1024,512]{1,0:T(8,128)(2,1)S(1)}, bf16[1024,512]{1,0:T(8,128)(2,1)}, u32[]{:S(2)}, u32[]{:S(2)}) collective-permute-start(bf16[1024,512]{1,0:T(8,128)(2,1)S(1)} %get-tuple-element.27), channel_id=1, source_target_pairs={{1,7},{4,0},{3,5},{6,2},{9,15},{12,8},{11,13},{14,10},{17,23},{20,... | collective-permute-start | bytes 3145736 | tf_op jit(solution)/shard_map/ppermute | solution.py:24
  102.8 1.6 %collective-permute-start.20 = (bf16[1024,512]{1,0:T(8,128)(2,1)S(1)}, bf16[1024,512]{1,0:T(8,128)(2,1)}, u32[]{:S(2)}, u32[]{:S(2)}) collective-permute-start(bf16[1024,512]{1,0:T(8,128)(2,1)S(1)} %get-tuple-element.26), channel_id=1, source_target_pairs={{0,2},{5,7},{2,0},{7,5},{8,10},{13,15},{10,8},{15,13},{16,18},{21,... | collective-permute-start | bytes 3145736 | tf_op jit(solution)/shard_map/ppermute | solution.py:24
  104.5 0.7 collective-permute-start.16
  105.2 0.1 collective-permute-start.17
  105.3 0.1 add_select_fusion
  105.4 0.6 select_n.64.index_ref
  106.0 1.8 %collective-permute-done.17.refs_7_ = f32[192,512]{1,0:T(8,128)} collective-permute-done((f32[192,512]{1,0:T(8,128)S(1)}, f32[192,512]{1,0:T(8,128)}, u32[]{:S(2)}, u32[]{:S(2)}) %collective-permute-start.17) | collective-permute-done | bytes 393248 | tf_op jit(solution)/shard_map/ppermute | solution.py:24
  107.8 3.0 %pack.1 = bf16[16,192,128]{2,1,0:T(8,128)(2,1)} custom-call(s32[16]{0:T(128)} %select_n.64.index_ref, f32[192,512]{1,0:T(8,128)} %copy-done.5, f32[192,1024]{1,0:T(8,128)} %copy-done.2, f32[192,1024]{1,0:T(8,128)} %copy-done.2, f32[192,512]{1,0:T(8,128)} %copy-done.6, f32[192,512]{1,0:T(8,128)} %collective-permute-done.15.refs_4_, ...), custom_call_target="tpu_custom_call" | custom-call | tf_op jit(solution)/shard_map/pack/pallas_call | solution.py:241
  110.8 4.7 %all-to-all-start = ((bf16[16,192,128]{2,1,0:T(8,128)(2,1)}), bf16[16,192,128]{2,1,0:T(8,128)(2,1)S(1)}, u32[]{:S(2)}, u32[]{:S(2)}) async-start(bf16[16,192,128]{2,1,0:T(8,128)(2,1)} %pack.1), calls=%async_computation | async-start | bytes 1572864 | tf_op jit(solution)/shard_map/all_to_all | solution.py:249
  115.5 0.6 collective-permute-done.18.a_ref
  116.2 7.8 %collective-permute-done.19.b_ref = bf16[1024,512]{1,0:T(8,128)(2,1)} collective-permute-done((bf16[1024,512]{1,0:T(8,128)(2,1)S(1)}, bf16[1024,512]{1,0:T(8,128)(2,1)}, u32[]{:S(2)}, u32[]{:S(2)}) %collective-permute-start.19) | collective-permute-done | bytes 1048608 | tf_op jit(solution)/shard_map/ppermute | solution.py:24
  124.0 4.3 %join.1 = (bf16[1024,256]{1,0:T(8,128)(2,1)}, bf16[1024,256]{1,0:T(8,128)(2,1)}) custom-call(s32[1]{0:T(128)} %bitcast.4.flag_ref, f32[1024,512]{1,0:T(8,128)} %copy-done.3, bf16[1024,512]{1,0:T(8,128)(2,1)} %collective-permute-done.18.a_ref, bf16[1024,512]{1,0:T(8,128)(2,1)} %collective-permute-done.19.b_ref, bf16[1024,512]{1,0:T(8,128)(2,1)} %collective-permute-done.20.c_ref), custom_call_target="tpu_custom_call" | custom-call | tf_op jit(solution)/shard_map/join/pallas_call | solution.py:256
  128.3 1.3 collective-permute-start.21
  129.6 0.9 copy-done.7
  130.5 2.4 %decode.1 = bf16[128,1024]{1,0:T(8,128)(2,1)} custom-call(bf16[16,192,128]{2,1,0:T(8,128)(2,1)} %copy-done.7, bf16[192,1024]{1,0:T(8,128)(2,1)} %dec_ref.1), custom_call_target="tpu_custom_call" | custom-call | tf_op jit(solution)/shard_map/decode/pallas_call | solution.py:250
  132.9 2.2 %collective-permute-done.21 = bf16[1024,256]{1,0:T(8,128)(2,1)S(1)} collective-permute-done((bf16[1024,256]{1,0:T(8,128)(2,1)}, bf16[1024,256]{1,0:T(8,128)(2,1)S(1)}, u32[]{:S(2)}, u32[]{:S(2)}) %collective-permute-start.21) | collective-permute-done | bytes 524320 | tf_op jit(solution)/shard_map/ppermute | solution.py:24
  135.1 0.9 broadcast_select_fusion
  (35 shorter events, 0.2 us)
Async XLA Ops:
  2.5 8.0 %collective-permute-start = (bf16[144,1024]{1,0:T(8,128)(2,1)S(1)}, bf16[144,1024]{1,0:T(8,128)(2,1)S(1)}, u32[]{:S(2)}, u32[]{:S(2)}) collective-permute-start(bf16[144,1024]{1,0:T(8,128)(2,1)S(1)} %maximum_maximum_fusion), channel_id=1, source_target_pairs={{0,32},{1,9},{4,36},{5,13},{2,34},{3,11},{6,38},{7,15},{8,40},{9,1... | collective-permute-start | bytes 884744 | tf_op jit(solution)/shard_map/ppermute | solution.py:24
  4.7 6.0 %collective-permute-start.1 = (bf16[144,1024]{1,0:T(8,128)(2,1)S(1)}, bf16[144,1024]{1,0:T(8,128)(2,1)S(1)}, u32[]{:S(2)}, u32[]{:S(2)}) collective-permute-start(bf16[144,1024]{1,0:T(8,128)(2,1)S(1)} %maximum_maximum_fusion), channel_id=1, source_target_pairs={{0,96},{1,25},{4,100},{5,29},{2,98},{3,27},{6,102},{7,31},{8,104},... | collective-permute-start | bytes 884744 | tf_op jit(solution)/shard_map/ppermute | solution.py:24
  10.5 8.5 %collective-permute-start.2 = (bf16[64,1024]{1,0:T(8,128)(2,1)S(1)}, bf16[64,1024]{1,0:T(8,128)(2,1)S(1)}, u32[]{:S(2)}, u32[]{:S(2)}) collective-permute-start(bf16[64,1024]{1,0:T(8,128)(2,1)S(1)} %slice.57), channel_id=1, source_target_pairs={{0,32},{1,9},{4,36},{5,13},{2,34},{3,11},{6,38},{7,15},{8,40},{9,1... | collective-permute-start | bytes 393224 | tf_op jit(solution)/shard_map/ppermute | solution.py:24
  10.7 8.4 %copy-start.8 = (bf16[128,1024]{1,0:T(8,128)(2,1)S(1)}, bf16[128,1024]{1,0:T(8,128)(2,1)}, u32[]{:S(2)}) copy-start(bf16[128,1024]{1,0:T(8,128)(2,1)} %param.7) | copy-start | bytes 786436
  10.7 8.3 %collective-permute-start.3 = (bf16[80,1024]{1,0:T(8,128)(2,1)S(1)}, bf16[80,1024]{1,0:T(8,128)(2,1)S(1)}, u32[]{:S(2)}, u32[]{:S(2)}) collective-permute-start(bf16[80,1024]{1,0:T(8,128)(2,1)S(1)} %slice.58), channel_id=1, source_target_pairs={{0,96},{1,25},{4,100},{5,29},{2,98},{3,27},{6,102},{7,31},{8,104},... | collective-permute-start | bytes 491528 | tf_op jit(solution)/shard_map/ppermute | solution.py:24
  16.1 15.3 %collective-permute-start.5 = (bf16[512,1024]{1,0:T(8,128)(2,1)S(1)}, bf16[512,1024]{1,0:T(8,128)(2,1)}, u32[]{:S(2)}, u32[]{:S(2)}) collective-permute-start(bf16[512,1024]{1,0:T(8,128)(2,1)S(1)} %get-tuple-element.35), channel_id=1, source_target_pairs={{0,4},{1,0},{4,5},{5,3},{2,6},{3,2},{6,7},{7,1},{8,12},{9,8},{12,1... | collective-permute-start | bytes 3145736 | tf_op jit(solution)/shard_map/ppermute | solution.py:24
  19.4 15.7 %collective-permute-start.7 = (bf16[528,1024]{1,0:T(8,128)(2,1)S(1)}, bf16[528,1024]{1,0:T(8,128)(2,1)}, u32[]{:S(2)}, u32[]{:S(2)}) collective-permute-start(bf16[528,1024]{1,0:T(8,128)(2,1)S(1)} %concatenate.15.refs_1_), channel_id=1, source_target_pairs={{0,8},{1,33},{4,12},{5,37},{2,10},{3,35},{6,14},{7,39},{8,16},{9,4... | collective-permute-start | bytes 3244040 | tf_op jit(solution)/shard_map/ppermute | solution.py:24
  19.5 17.5 %collective-permute-start.8 = (bf16[528,1024]{1,0:T(8,128)(2,1)S(1)}, bf16[528,1024]{1,0:T(8,128)(2,1)}, u32[]{:S(2)}, u32[]{:S(2)}) collective-permute-start(bf16[528,1024]{1,0:T(8,128)(2,1)S(1)} %concatenate.15.refs_1_), channel_id=1, source_target_pairs={{0,24},{1,97},{4,28},{5,101},{2,26},{3,99},{6,30},{7,103},{8,0},{9... | collective-permute-start | bytes 3244040 | tf_op jit(solution)/shard_map/ppermute | solution.py:24
  22.2 22.3 %collective-permute-start.6 = (bf16[512,1024]{1,0:T(8,128)(2,1)}, bf16[512,1024]{1,0:T(8,128)(2,1)}, u32[]{:S(2)}, u32[]{:S(2)}) collective-permute-start(bf16[512,1024]{1,0:T(8,128)(2,1)} %get-tuple-element.34), channel_id=1, source_target_pairs={{0,6},{1,0},{4,5},{5,1},{2,4},{3,2},{6,7},{7,3},{8,14},{9,8},{12,1... | collective-permute-start | bytes 3145736 | tf_op jit(solution)/shard_map/ppermute | solution.py:24
  24.2 26.4 %collective-permute-start.4 = (bf16[528,1024]{1,0:T(8,128)(2,1)S(1)}, bf16[528,1024]{1,0:T(8,128)(2,1)}, u32[]{:S(2)}, u32[]{:S(2)}) collective-permute-start(bf16[528,1024]{1,0:T(8,128)(2,1)S(1)} %concatenate.15.refs_1_), channel_id=1, source_target_pairs={{0,1},{1,0},{4,5},{5,4},{2,3},{3,2},{6,7},{7,6},{8,9},{9,8},{12,13... | collective-permute-start | bytes 3244040 | tf_op jit(solution)/shard_map/ppermute | solution.py:24
  37.0 26.9 %collective-permute-start.9 = (bf16[256,1024]{1,0:T(8,128)(2,1)}, bf16[256,1024]{1,0:T(8,128)(2,1)}, u32[]{:S(2)}, u32[]{:S(2)}) collective-permute-start(bf16[256,1024]{1,0:T(8,128)(2,1)} %slice.63), channel_id=1, source_target_pairs={{0,8},{1,33},{4,12},{5,37},{2,10},{3,35},{6,14},{7,39},{8,16},{9,4... | collective-permute-start | bytes 1572872 | tf_op jit(solution)/shard_map/ppermute | solution.py:24
  38.9 24.9 %collective-permute-start.10 = (bf16[272,1024]{1,0:T(8,128)(2,1)}, bf16[272,1024]{1,0:T(8,128)(2,1)}, u32[]{:S(2)}, u32[]{:S(2)}) collective-permute-start(bf16[272,1024]{1,0:T(8,128)(2,1)} %slice.64), channel_id=1, source_target_pairs={{0,24},{1,97},{4,28},{5,101},{2,26},{3,99},{6,30},{7,103},{8,0},{9... | collective-permute-start | bytes 1671176 | tf_op jit(solution)/shard_map/ppermute | solution.py:24
  41.6 33.0 %collective-permute-start.13 = (bf16[528,1024]{1,0:T(8,128)(2,1)}, bf16[528,1024]{1,0:T(8,128)(2,1)}, u32[]{:S(2)}, u32[]{:S(2)}) collective-permute-start(bf16[528,1024]{1,0:T(8,128)(2,1)} %collective-permute-done.7.refs_1_), channel_id=1, source_target_pairs={{0,1},{1,0},{4,5},{5,4},{2,3},{3,2},{6,7},{7,6},{8,9},{9,8},{12,13... | collective-permute-start | bytes 3244040 | tf_op jit(solution)/shard_map/ppermute | solution.py:24
  44.5 30.1 %collective-permute-start.14 = (bf16[528,1024]{1,0:T(8,128)(2,1)}, bf16[528,1024]{1,0:T(8,128)(2,1)}, u32[]{:S(2)}, u32[]{:S(2)}) collective-permute-start(bf16[528,1024]{1,0:T(8,128)(2,1)} %collective-permute-done.8.refs_2_), channel_id=1, source_target_pairs={{0,1},{1,0},{4,5},{5,4},{2,3},{3,2},{6,7},{7,6},{8,9},{9,8},{12,13... | collective-permute-start | bytes 3244040 | tf_op jit(solution)/shard_map/ppermute | solution.py:24
  45.8 1.4 %copy-start = (bf16[1024,1024]{1,0:T(8,128)(2,1)}, bf16[1024,1024]{1,0:T(8,128)(2,1)S(1)}, u32[]{:S(2)}) copy-start(bf16[1024,1024]{1,0:T(8,128)(2,1)S(1)} %constant_dynamic-update-slice_fusion.w_ref.refs_3_.refs_5_) | copy-start | bytes 6291460
  50.6 1.6 %copy-start.1 = (bf16[1024,1024]{1,0:T(8,128)(2,1)S(1)}, bf16[1024,1024]{1,0:T(8,128)(2,1)}, u32[]{:S(2)}) copy-start(bf16[1024,1024]{1,0:T(8,128)(2,1)} %copy-done) | copy-start | bytes 6291460
  52.2 1.1 copy-start.4
  62.6 0.7 copy-start.5
  63.3 41.9 %collective-permute-start.15 = (f32[192,512]{1,0:T(8,128)}, f32[192,512]{1,0:T(8,128)}, u32[]{:S(2)}, u32[]{:S(2)}) collective-permute-start(f32[192,512]{1,0:T(8,128)} %get-tuple-element.22), channel_id=1, source_target_pairs={{0,1},{1,0},{4,5},{5,4},{2,3},{3,2},{6,7},{7,6},{8,9},{9,8},{12,13... | collective-permute-start | bytes 1179656 | tf_op jit(solution)/shard_map/ppermute | solution.py:24
  63.8 20.3 %collective-permute-start.11 = (bf16[256,1024]{1,0:T(8,128)(2,1)}, bf16[256,1024]{1,0:T(8,128)(2,1)S(1)}, u32[]{:S(2)}, u32[]{:S(2)}) collective-permute-start(bf16[256,1024]{1,0:T(8,128)(2,1)} %collective-permute-done.9.refs_1_), channel_id=1, source_target_pairs={{0,1},{1,0},{4,5},{5,4},{2,3},{3,2},{6,7},{7,6},{8,9},{9,8},{12,13... | collective-permute-start | bytes 1572872 | tf_op jit(solution)/shard_map/ppermute | solution.py:24
  63.8 20.3 %collective-permute-start.12 = (bf16[272,1024]{1,0:T(8,128)(2,1)}, bf16[272,1024]{1,0:T(8,128)(2,1)S(1)}, u32[]{:S(2)}, u32[]{:S(2)}) collective-permute-start(bf16[272,1024]{1,0:T(8,128)(2,1)} %collective-permute-done.10.refs_2_), channel_id=1, source_target_pairs={{0,1},{1,0},{4,5},{5,4},{2,3},{3,2},{6,7},{7,6},{8,9},{9,8},{12,13... | collective-permute-start | bytes 1671176 | tf_op jit(solution)/shard_map/ppermute | solution.py:24
  73.7 0.9 copy-start.2
  84.1 21.2 %copy-start.9 = (s32[4]{0:T(128)S(1)}, s32[4]{0:T(128)}, u32[]{:S(2)}) copy-start(s32[4]{0:T(128)} %constant.78.clone) | copy-start | bytes 52
  95.5 1.4 %copy-start.3 = (f32[1024,512]{1,0:T(8,128)}, f32[1024,512]{1,0:T(8,128)S(1)}, u32[]{:S(2)}) copy-start(f32[1024,512]{1,0:T(8,128)S(1)} %get-tuple-element.25.own_ref) | copy-start | bytes 6291460
  96.9 0.7 copy-start.6
  97.6 18.5 %collective-permute-start.18 = (bf16[1024,512]{1,0:T(8,128)(2,1)S(1)}, bf16[1024,512]{1,0:T(8,128)(2,1)}, u32[]{:S(2)}, u32[]{:S(2)}) collective-permute-start(bf16[1024,512]{1,0:T(8,128)(2,1)S(1)} %get-tuple-element.26), channel_id=1, source_target_pairs={{1,5},{4,2},{3,7},{6,0},{9,13},{12,10},{11,15},{14,8},{17,21},{20,... | collective-permute-start | bytes 3145736 | tf_op jit(solution)/shard_map/ppermute | solution.py:24
  100.3 23.7 %collective-permute-start.19 = (bf16[1024,512]{1,0:T(8,128)(2,1)S(1)}, bf16[1024,512]{1,0:T(8,128)(2,1)}, u32[]{:S(2)}, u32[]{:S(2)}) collective-permute-start(bf16[1024,512]{1,0:T(8,128)(2,1)S(1)} %get-tuple-element.27), channel_id=1, source_target_pairs={{1,7},{4,0},{3,5},{6,2},{9,15},{12,8},{11,13},{14,10},{17,23},{20,... | collective-permute-start | bytes 3145736 | tf_op jit(solution)/shard_map/ppermute | solution.py:24
  102.8 21.1 %collective-permute-start.20 = (bf16[1024,512]{1,0:T(8,128)(2,1)S(1)}, bf16[1024,512]{1,0:T(8,128)(2,1)}, u32[]{:S(2)}, u32[]{:S(2)}) collective-permute-start(bf16[1024,512]{1,0:T(8,128)(2,1)S(1)} %get-tuple-element.26), channel_id=1, source_target_pairs={{0,2},{5,7},{2,0},{7,5},{8,10},{13,15},{10,8},{15,13},{16,18},{21,... | collective-permute-start | bytes 3145736 | tf_op jit(solution)/shard_map/ppermute | solution.py:24
  104.5 3.3 %collective-permute-start.16 = (f32[192,1024]{1,0:T(8,128)S(1)}, f32[192,1024]{1,0:T(8,128)}, u32[]{:S(2)}, u32[]{:S(2)}) collective-permute-start(f32[192,1024]{1,0:T(8,128)S(1)} %get-tuple-element.23), channel_id=1, source_target_pairs={{0,1},{1,0},{4,5},{5,4},{2,3},{3,2},{6,7},{7,6},{8,9},{9,8},{12,13... | collective-permute-start | bytes 2359304 | tf_op jit(solution)/shard_map/ppermute | solution.py:24
  105.2 2.6 %collective-permute-start.17 = (f32[192,512]{1,0:T(8,128)S(1)}, f32[192,512]{1,0:T(8,128)}, u32[]{:S(2)}, u32[]{:S(2)}) collective-permute-start(f32[192,512]{1,0:T(8,128)S(1)} %get-tuple-element.24), channel_id=1, source_target_pairs={{0,1},{1,0},{4,5},{5,4},{2,3},{3,2},{6,7},{7,6},{8,9},{9,8},{12,13... | collective-permute-start | bytes 1179656 | tf_op jit(solution)/shard_map/ppermute | solution.py:24
  110.8 18.7 %all-to-all-start = ((bf16[16,192,128]{2,1,0:T(8,128)(2,1)}), bf16[16,192,128]{2,1,0:T(8,128)(2,1)S(1)}, u32[]{:S(2)}, u32[]{:S(2)}) async-start(bf16[16,192,128]{2,1,0:T(8,128)(2,1)} %pack.1), calls=%async_computation | async-start | bytes 1572864 | tf_op jit(solution)/shard_map/all_to_all | solution.py:249
  128.3 6.8 %collective-permute-start.21 = (bf16[1024,256]{1,0:T(8,128)(2,1)}, bf16[1024,256]{1,0:T(8,128)(2,1)S(1)}, u32[]{:S(2)}, u32[]{:S(2)}) collective-permute-start(bf16[1024,256]{1,0:T(8,128)(2,1)} %get-tuple-element.29), channel_id=1, source_target_pairs={{0,1},{5,4},{2,3},{7,6},{8,9},{13,12},{10,11},{15,14},{16,17},{21,... | collective-permute-start | bytes 1572872 | tf_op jit(solution)/shard_map/ppermute | solution.py:24
  129.6 0.9 copy-start.7

commit v2 on v0

v2 whole, which is shorter than its diff:
```python
import functools
import itertools

import jax
import jax.numpy as jnp
from jax import lax
from jax.experimental import pallas as pl
from jax.experimental.pallas import tpu as pltpu
from jax.sharding import Mesh, PartitionSpec as P

AXES = ("z", "y", "xl", "xh", "core")
BF16, F32, I32 = jnp.bfloat16, jnp.float32, jnp.int32
TAIL = 16
HALF = 512
VMEM_LIMIT = 16 * 2**20
OFFSETS = (0, 3, 1, 2)


def pairs(target):
    flat = lambda z, y, x, c: (((z % 4 * 4 + y % 4) * 2 + x % 2) * 2 + x % 4 // 2) * 2 + c
    places = itertools.product(range(4), range(4), range(4), range(2))
    return [(flat(*at), flat(*target(*at))) for at in places if target(*at) is not None]


def move(array, target):
    return lax.ppermute(array, AXES, pairs(target))


def hop(phase, step):
    return lambda z, y, x, c: (z + step, y, x, c) if c == phase else (z, y + step, x, c)


def to_sibling(z, y, x, c):
    return z, y, x, 1 - c


def to_user(z, y, x, c):
    return (z, y, x ^ 1, c) if c == x % 2 else (z, y, x, 1 - c)


def rows_kernel(own_ref, back_ref, ahead_ref, far_ref, low_ref, high_ref):
    low_ref[:128, :] = own_ref[:128, :]
    low_ref[128:, :] = back_ref[:128, :]
    high_ref[:128, :] = ahead_ref[:128, :]
    high_ref[128:256, :] = far_ref[:128, :]
    refs = (own_ref, back_ref, ahead_ref, far_ref)
    row = lax.broadcasted_iota(I32, (TAIL, 1024), 0)
    tail = jnp.zeros((TAIL, 1024), F32)
    for i, ref in enumerate(refs):
        ids = ref[128:144, :].astype(F32)
        for digit in range(2):
            tail = jnp.where(row == 2 * i + digit, ids[digit : digit + 1, :], tail)
    high_ref[256:, :] = tail.astype(BF16)


def encode(w_ref, enc_ref, wet_ref):
    we = lax.dot_general(
        enc_ref[...], w_ref[...], (((1,), (1,)), ((), ())), preferred_element_type=F32
    )
    high = we.astype(BF16)
    wet_ref[:192, :] = high
    wet_ref[192:, :] = (we - high.astype(F32)).astype(BF16)


def target_bits(tail, block, base):
    digits = tail[2 * block : 2 * block + 2, :]
    local = (digits[0:1] * 256 + digits[1:2]) - base
    low, bit = local & 7, jnp.left_shift(1, (local >> 3) & 31)
    words = [jnp.where((local >> 8) == w, bit, 0) for w in range(4)]
    row = lax.broadcasted_iota(I32, (8, 128), 0)
    bits = [jnp.zeros((8, 128), I32)] * 4
    for slot in range(8):
        lanes = slice(slot * 128, (slot + 1) * 128)
        here = jnp.broadcast_to(low[:, lanes], (8, 128)) == row
        for w in range(4):
            word = jnp.broadcast_to(words[w][:, lanes], (8, 128))
            bits[w] = bits[w] | jnp.where(here, word, 0)
    return bits


def quarters(x, core):
    keeps = core == lax.rem(x, 2)
    half, next_half = x // 2, lax.rem(x + 1, 4) // 2
    away = jnp.where(keeps, 1 - half, next_half)
    column = jnp.where(keeps, 1 - core, core)
    return 2 * away + column, 2 * (1 - away) + core, 2 * away + 1 - column, 2 * (1 - away) + 1 - core


def chunk_kernel(enc_at, first, last, scale, *refs):
    n = len(enc_at)
    place, q_refs, refs = refs[0], refs[1 : 1 + 2 * n], refs[1 + 2 * n :]
    z, y, x, core = (place[i] for i in range(4))
    base = ((z * 4 + y) * 2 + core) * 2 * HALF
    w_ref, enc_ref, refs = refs[0], refs[1], refs[2:]
    if not first:
        total_ref, refs = refs[0], refs[1:]
    outs, (q_all, grads, bits) = refs[:-3], refs[-3:]
    n_enc = 1 + max(out for out, _ in enc_at)
    encs, outs = outs[:n_enc], outs[n_enc:]
    if first:
        wet_ref, outs = outs[0], outs[1:]
        encode(w_ref, enc_ref, wet_ref)
    else:
        wet_ref = enc_ref
    for i in range(n):
        low, high = q_refs[2 * i : 2 * i + 2]
        q_all[512 * i : 512 * i + 256, :] = low[...]
        q_all[512 * i + 256 : 512 * i + 512, :] = high[:256, :]
        tail = high[256:272, :].astype(F32).astype(I32)
        for b in range(4):
            lanes = slice(512 * i + 128 * b, 512 * i + 128 * b + 128)
            for w, word in enumerate(target_bits(tail, b, base)):
                bits[w, :, lanes] = word
    group = lax.broadcasted_iota(I32, (32, 1, 1), 0)
    for i in range(2):
        rows = slice(i * HALF, (i + 1) * HALF)
        for j in range(n):
            lanes = slice(512 * j, 512 * j + 512)
            logits = lax.dot_general(
                w_ref[rows, :], q_all[lanes, :], (((1,), (1,)), ((), ())), preferred_element_type=F32
            )
            for w in range(2):
                hit = (bits[2 * i + w, :, lanes][None] >> group) & 1
                target = hit.reshape(256, 512).astype(F32)
                some = jax.nn.sigmoid(logits[w * 256 : w * 256 + 256]) - target
                grads[i * HALF + w * 256 : i * HALF + w * 256 + 256, lanes] = (some * scale).astype(BF16)
        if not last:
            part = jnp.dot(grads[rows, :], q_all[...], preferred_element_type=F32)
            for c in range(4):
                columns = slice(256 * c, 256 * c + 256)
                old = 0.0 if first else total_ref[c, rows, :]
                outs[0][c, rows, :] = old + part[:, columns]
    encoded = jnp.dot(wet_ref[...], grads[...], preferred_element_type=F32)
    encoded = encoded[:192] + encoded[192:]
    for i, (out, column) in enumerate(enc_at):
        encs[out][:, column : column + 512] = encoded[:, 512 * i : 512 * i + 512]
    if last:
        for o, c in enumerate(quarters(x, core)):
            columns = q_all[:, pl.ds(pl.multiple_of(c * 256, 256), 256)]
            whole = total_ref[c] + jnp.dot(grads[...], columns, preferred_element_type=F32)
            outs[o][...] = whole.astype(BF16)
            if o % 2:
                outs[4 + o // 2][...] = whole


def chunk(place, q_bufs, enc_at, w, enc, total, last, scale):
    first = total is None
    vmem = pl.BlockSpec(memory_space=pltpu.VMEM)
    widths = [0] * (1 + max(out for out, _ in enc_at))
    for out, column in enc_at:
        widths[out] = max(widths[out], column + 512)
    args = [place, *q_bufs, w, enc] + ([] if first else [total])
    labels = 2 * HALF
    shapes = [jax.ShapeDtypeStruct((192, n), F32) for n in widths]
    if first:
        shapes.append(jax.ShapeDtypeStruct((384, labels), BF16))
    if last:
        shapes += [jax.ShapeDtypeStruct((labels, 256), d) for d in (BF16,) * 4 + (F32,) * 2]
    else:
        shapes.append(jax.ShapeDtypeStruct((4, labels, 256), F32))
    n = 512 * len(enc_at)
    return pl.pallas_call(
        functools.partial(chunk_kernel, enc_at, first, last, scale),
        in_specs=[pl.BlockSpec(memory_space=pltpu.SMEM)] + [vmem] * (len(args) - 1),
        out_specs=[vmem] * len(shapes),
        out_shape=shapes,
        scratch_shapes=[
            pltpu.VMEM((n, 1024), BF16), pltpu.VMEM((labels, n), BF16), pltpu.VMEM((4, 8, n), I32)
        ],
        input_output_aliases={} if first or last else {len(args) - 1: len(shapes) - 1},
        compiler_params=pltpu.CompilerParams(vmem_limit_bytes=VMEM_LIMIT),
        cost_estimate=pl.CostEstimate(
            flops=2 * n * labels * (2 * 1024 + 384), bytes_accessed=2**20, transcendentals=0
        ),
        name="chunk",
    )(*args)


def pack_kernel(place, *refs):
    own, sib, out = refs[:3], refs[3:6], refs[6]
    z, y, core = place[0], place[1], place[3]
    first, second = jnp.where(core == 0, z, y), jnp.where(core == 0, y, z)
    at = [(i, j) for i in OFFSETS for j in OFFSETS]
    for a, b in zip(own, sib):
        value = (a[...] + b[...]).astype(BF16)
        for block in range(value.shape[1] // 128):
            i, j = at.pop(0)
            j, i = lax.rem(first + j, 4), lax.rem(second + i, 4)
            out[jnp.where(core == 0, j * 4 + i, i * 4 + j)] = value[:, block * 128 : block * 128 + 128]


def decode_kernel(parts_ref, dec_ref, out_ref):
    total = parts_ref[0].astype(F32)
    for i in range(1, 16):
        total += parts_ref[i].astype(F32)
    dec = dec_ref[...]
    rest, result = total, None
    for _ in range(3):
        digit = rest.astype(BF16)
        rest = rest - digit.astype(F32)
        part = lax.dot_general(digit, dec, (((0,), (0,)), ((), ())), preferred_element_type=F32)
        result = part if result is None else result + part
    out_ref[...] = result.astype(BF16)


def join_kernel(place, own_ref, *refs):
    total = jnp.where(place[3] == lax.rem(place[2], 2), own_ref[...], 0.0)
    for ref in refs[:-1]:
        total += ref[...].astype(F32)
    refs[-1][...] = total.astype(BF16)


def kernel(body, out, *args, name, flops=10**6):
    place = lambda a: pltpu.SMEM if a.dtype == I32 else pltpu.VMEM
    one = not isinstance(out[0][0], tuple)
    shapes = [jax.ShapeDtypeStruct(*o) for o in ([out] if one else out)]
    result = pl.pallas_call(
        body,
        in_specs=[pl.BlockSpec(memory_space=place(a)) for a in args],
        out_specs=[pl.BlockSpec(memory_space=pltpu.VMEM)] * len(shapes),
        out_shape=shapes,
        compiler_params=pltpu.CompilerParams(vmem_limit_bytes=VMEM_LIMIT),
        cost_estimate=pl.CostEstimate(flops=flops, bytes_accessed=2**10, transcendentals=0),
        name=name,
    )(*args)
    return result[0] if one else result


def shards(queries, label_ids, label_counts, weights, encoder, decoder):
    z, y, xl, xh, core = (lax.axis_index(a) for a in AXES)
    scale = float(queries.shape[0] * 128) ** (-0.5)

    slot = lax.broadcasted_iota(I32, (8, 128), 0)
    ids = jnp.where(slot < label_counts[None, :], label_ids.T, 255 * 256).reshape(1, 1024)
    tail = jnp.concatenate([ids >> 8, ids & 255, jnp.zeros((TAIL - 2, 1024), I32)], axis=0)
    own = jnp.concatenate([queries, tail.astype(BF16)], axis=0)

    place = jnp.stack([z, y, 2 * xh + xl, core]).astype(I32)
    w = move(weights, to_user)
    back, ahead, far = (move(own, hop(0, step)) for step in (1, -1, 2))
    low, high = kernel(
        rows_kernel, (((256, 1024), BF16), ((256 + TAIL, 1024), BF16)), own, back, ahead, far, name="rows"
    )
    low_back, high_ahead = move(low, hop(1, 1)), move(high, hop(1, -1))
    high_back, low_ahead = move(high, hop(1, 1)), move(low, hop(1, -1))
    low_far, high_far = move(low_back, hop(1, 1)), move(high_ahead, hop(1, -1))
    rows, backs, aheads, fars = [low, high], [low_back, high_back], [low_ahead, high_ahead], [low_far, high_far]
    sibling = lambda bufs: [move(b, to_sibling) for b in bufs]

    apart, joined = ((0, 0), (1, 0)), ((0, 0), (0, 512))
    enc_a, enc_sa, wet, total = chunk(place, rows + sibling(rows), apart, w, encoder.T, None, False, scale)
    enc_b, total = chunk(place, backs + aheads, joined, w, wet, total, False, scale)
    enc_sb, total = chunk(place, sibling(backs) + sibling(aheads), joined, w, wet, total, False, scale)
    enc_c, enc_sc, out_0, out_1, out_2, out_3, kept, sib = chunk(
        place, fars + sibling(fars), apart, w, wet, total, True, scale
    )

    pick = lambda same, other: lambda z, y, x, c: same(z, y, x, c) if c == x % 2 else other(z, y, x, c)
    none = lambda z, y, x, c: None
    got = [
        move(out_0, pick(lambda z, y, x, c: (z, y, x + 2, 1 - c), lambda z, y, x, c: (z, y, x + 1, c))),
        move(out_1, pick(none, lambda z, y, x, c: (z, y, x - 1, c))),
        move(out_2, pick(lambda z, y, x, c: (z, y, x + 2, c), lambda z, y, x, c: (z, y, x + 1, 1 - c))),
        move(out_3, pick(none, lambda z, y, x, c: (z, y, x - 1, 1 - c))),
        move(sib, pick(to_sibling, none)),
    ]

    packed = kernel(
        pack_kernel, ((16, 192, 128), BF16), place, enc_a, enc_b, enc_c, *sibling([enc_sa, enc_sb, enc_sc]), name="pack"
    )
    parts = lax.all_to_all(packed, ("z", "y"), split_axis=0, concat_axis=0, tiled=True)
    query_grad = kernel(decode_kernel, ((128, 1024), BF16), parts, decoder, name="decode")
    weight_grad = kernel(join_kernel, ((2 * HALF, 256), BF16), place, kept, *got, name="join", flops=10**11)
    return query_grad, weight_grad


def solution(mesh):
    fine = Mesh(mesh.devices.reshape(4, 4, 2, 2, 2), AXES)
    label, dp = AXES[:3], AXES[3:]
    return jax.shard_map(
        shards,
        mesh=fine,
        in_specs=(P(AXES, None), P(AXES, None), P(AXES), P(label, None), P(), P()),
        out_specs=(P(AXES, None), P(label, dp)),
        check_vma=False,
    )
```

time: 490 us -> 110 us (0.22)
  waiting for transfers between devices: 220 us -> 29.3 us
  blocking collectives: 141 us -> 0 us
  matrix products: 58.4 us -> 0 us
  other arithmetic: 54.1 us -> 1.84 us
  starting transfers between devices: 0.12 us -> 37 us
  Pallas kernels: 0 us -> 33.9 us
  between operations: 13.8 us -> 0.77 us
    reduce_scatter x2 -> x0, waiting for transfers between devices: 217 us -> none  [the longest x1 148 us: shards(): summed = lax.psum_scatter(encoded, 'label', scatter_dimension=0, tiled=True)]
    all_gather x2 -> x0, blocking collectives: 141 us -> none  [the longest x1 73.4 us: shards(): lax.all_gather(label_counts, 'label', axis=0, tiled=True)]
    dot_general x5 -> x0, matrix products: 58.4 us -> none  [the longest x1 18.4 us: shards(): lax.dot_general(rows_all, weights, (((1,), (1,)), ((), ())), preferred_el...]
    reduce_or x1 -> x0, other arithmetic: 52 us -> none  [shards(): target = jnp.any(hit, axis=1).astype(jnp.float32)]
    pallas_call x0 -> x8, Pallas kernels: none -> 33.9 us  [the longest x4 28.6 us: chunk(): pl.pallas_call(functools.partial(chunk_kernel, enc_at, first, last, scale...]
    ppermute x0 -> x26, starting transfers between devices: none -> 33.4 us  [move(): return lax.ppermute(array, AXES, pairs(target))]
    ppermute x0 -> x26, waiting for transfers between devices: none -> 29.3 us  [move(): return lax.ppermute(array, AXES, pairs(target))]
    unnamed x6 -> x16, local copies, waits for them, and re-layouts: 0.02 us -> 6.88 us
  transfers between devices with their start and end apart: 3 -> 27, of which waited for: 3 -> 10; matrix products, arithmetic and copies ran while one was open for 15% -> 2% of each run, Pallas kernels for 0% -> 30%
where the time goes in v2:
time: 110 us
  starting transfers between devices  37 us (34%)
  Pallas kernels  33.9 us (31%)
  waiting for transfers between devices  29.3 us (27%)
  local copies, waits for them, and re-layouts  6.97 us (6%)
  other arithmetic  1.84 us (2%)
    ppermute x26, starting transfers between devices, move(): return lax.ppermute(array, AXES, pairs(target))  33.4 us
    ppermute x26, waiting for transfers between devices, move(): return lax.ppermute(array, AXES, pairs(target))  29.3 us
    pallas_call x4, Pallas kernels, chunk(): pl.pallas_call(functools.partial(chunk_kernel, enc_at, first, last, scale...  28.6 us
    unnamed x16, local copies, waits for them, and re-layouts  6.88 us
    pallas_call x4, Pallas kernels, kernel(): pl.pallas_call(body, in_specs=[pl.BlockSpec(memory_space=place(a)) for a...  5.33 us
    all_to_all x1, starting transfers between devices, shards(): lax.all_to_all(packed, ('z', 'y'), split_axis=0, concat_axis=0, tiled=True)  3.61 us
  transfers between devices with their start and end apart: 27, of which 10 were waited for; matrix products, arithmetic and copies ran while one was open for 2% of the time, Pallas kernels for 30%

profile of v2, /device:TPU:1, one launch (start us, length us, event | category | flops | bytes accessed | tf_op | source)
XLA Modules:
  0.0 109.8 jit_solution(8726689593558136225)
XLA Ops:
  0.6 1.5 %collective-permute-start.5 = (bf16[1024,1024]{1,0:T(8,128)(2,1)}, bf16[1024,1024]{1,0:T(8,128)(2,1)S(1)}, u32[]{:S(2)}, u32[]{:S(2)}) collective-permute-start(bf16[1024,1024]{1,0:T(8,128)(2,1)} %param.9), channel_id=1, source_target_pairs={{0,4},{1,0},{4,5},{5,1},{2,6},{3,2},{6,7},{7,3},{8,12},{9,8},{12,1... | collective-permute-start | bytes 6291464 | tf_op jit(solution)/shard_map/ppermute | solution.py:26
  2.1 0.1 pad.3.clone
  2.2 0.7 fusion
  2.9 1.1 maximum_maximum_fusion.own_ref
  4.0 1.4 %collective-permute-start = (bf16[144,1024]{1,0:T(8,128)(2,1)S(1)}, bf16[144,1024]{1,0:T(8,128)(2,1)S(1)}, u32[]{:S(2)}, u32[]{:S(2)}) collective-permute-start(bf16[144,1024]{1,0:T(8,128)(2,1)S(1)} %maximum_maximum_fusion.own_ref), channel_id=1, source_target_pairs={{0,32},{1,9},{4,36},{5,13},{2,34},{3,11},{6,38},{7,15},{8,40},{9,1... | collective-permute-start | bytes 884744 | tf_op jit(solution)/shard_map/ppermute | solution.py:26
  5.4 1.5 %collective-permute-start.1 = (bf16[144,1024]{1,0:T(8,128)(2,1)S(1)}, bf16[144,1024]{1,0:T(8,128)(2,1)S(1)}, u32[]{:S(2)}, u32[]{:S(2)}) collective-permute-start(bf16[144,1024]{1,0:T(8,128)(2,1)S(1)} %maximum_maximum_fusion.own_ref), channel_id=1, source_target_pairs={{0,96},{1,25},{4,100},{5,29},{2,98},{3,27},{6,102},{7,31},{8,104},... | collective-permute-start | bytes 884744 | tf_op jit(solution)/shard_map/ppermute | solution.py:26
  7.0 1.6 %collective-permute-start.2 = (bf16[144,1024]{1,0:T(8,128)(2,1)S(1)}, bf16[144,1024]{1,0:T(8,128)(2,1)S(1)}, u32[]{:S(2)}, u32[]{:S(2)}) collective-permute-start(bf16[144,1024]{1,0:T(8,128)(2,1)S(1)} %maximum_maximum_fusion.own_ref), channel_id=1, source_target_pairs={{0,64},{1,17},{4,68},{5,21},{2,66},{3,19},{6,70},{7,23},{8,72},{9,... | collective-permute-start | bytes 884744 | tf_op jit(solution)/shard_map/ppermute | solution.py:26
  8.5 2.8 %collective-permute-done.back_ref = bf16[144,1024]{1,0:T(8,128)(2,1)S(1)} collective-permute-done((bf16[144,1024]{1,0:T(8,128)(2,1)S(1)}, bf16[144,1024]{1,0:T(8,128)(2,1)S(1)}, u32[]{:S(2)}, u32[]{:S(2)}) %collective-permute-start) | collective-permute-done | bytes 294944 | tf_op jit(solution)/shard_map/ppermute | solution.py:26
  11.3 2.5 %collective-permute-done.1.ahead_ref = bf16[144,1024]{1,0:T(8,128)(2,1)S(1)} collective-permute-done((bf16[144,1024]{1,0:T(8,128)(2,1)S(1)}, bf16[144,1024]{1,0:T(8,128)(2,1)S(1)}, u32[]{:S(2)}, u32[]{:S(2)}) %collective-permute-start.1) | collective-permute-done | bytes 294944 | tf_op jit(solution)/shard_map/ppermute | solution.py:26
  13.8 1.8 %collective-permute-done.2.far_ref = bf16[144,1024]{1,0:T(8,128)(2,1)S(1)} collective-permute-done((bf16[144,1024]{1,0:T(8,128)(2,1)S(1)}, bf16[144,1024]{1,0:T(8,128)(2,1)S(1)}, u32[]{:S(2)}, u32[]{:S(2)}) %collective-permute-start.2) | collective-permute-done | bytes 294944 | tf_op jit(solution)/shard_map/ppermute | solution.py:26
  15.6 0.1 rows.1
  15.7 3.4 %collective-permute-start.3 = (bf16[256,1024]{1,0:T(8,128)(2,1)S(1)}, bf16[256,1024]{1,0:T(8,128)(2,1)S(1)}, u32[]{:S(2)}, u32[]{:S(2)}) collective-permute-start(bf16[256,1024]{1,0:T(8,128)(2,1)S(1)} %get-tuple-element.20.refs_1_), channel_id=1, source_target_pairs={{0,1},{1,0},{4,5},{5,4},{2,3},{3,2},{6,7},{7,6},{8,9},{9,8},{12,13... | collective-permute-start | bytes 1572872 | tf_op jit(solution)/shard_map/ppermute | solution.py:26
  19.2 1.1 %collective-permute-start.6 = (bf16[256,1024]{1,0:T(8,128)(2,1)S(1)}, bf16[256,1024]{1,0:T(8,128)(2,1)}, u32[]{:S(2)}, u32[]{:S(2)}) collective-permute-start(bf16[256,1024]{1,0:T(8,128)(2,1)S(1)} %get-tuple-element.20.refs_1_), channel_id=1, source_target_pairs={{0,8},{1,33},{4,12},{5,37},{2,10},{3,35},{6,14},{7,39},{8,16},{9,4... | collective-permute-start | bytes 1572872 | tf_op jit(solution)/shard_map/ppermute | solution.py:26
  20.3 1.5 %collective-permute-start.8 = (bf16[256,1024]{1,0:T(8,128)(2,1)S(1)}, bf16[256,1024]{1,0:T(8,128)(2,1)}, u32[]{:S(2)}, u32[]{:S(2)}) collective-permute-start(bf16[256,1024]{1,0:T(8,128)(2,1)S(1)} %get-tuple-element.20.refs_1_), channel_id=1, source_target_pairs={{0,24},{1,97},{4,28},{5,101},{2,26},{3,99},{6,30},{7,103},{8,0},{9... | collective-permute-start | bytes 1572872 | tf_op jit(solution)/shard_map/ppermute | solution.py:26
  21.8 0.8 copy-done.1
  22.6 0.6 collective-permute-start.4
  23.3 0.8 copy-done.3
  24.1 1.6 %collective-permute-start.9 = (bf16[272,1024]{1,0:T(8,128)(2,1)S(1)}, bf16[272,1024]{1,0:T(8,128)(2,1)S(1)}, u32[]{:S(2)}, u32[]{:S(2)}) collective-permute-start(bf16[272,1024]{1,0:T(8,128)(2,1)S(1)} %get-tuple-element.21.refs_2_), channel_id=1, source_target_pairs={{0,24},{1,97},{4,28},{5,101},{2,26},{3,99},{6,30},{7,103},{8,0},{9... | collective-permute-start | bytes 1671176 | tf_op jit(solution)/shard_map/ppermute | solution.py:26
  25.7 3.1 %collective-permute-done.6.refs_1_ = bf16[256,1024]{1,0:T(8,128)(2,1)} collective-permute-done((bf16[256,1024]{1,0:T(8,128)(2,1)S(1)}, bf16[256,1024]{1,0:T(8,128)(2,1)}, u32[]{:S(2)}, u32[]{:S(2)}) %collective-permute-start.6) | collective-permute-done | bytes 524320 | tf_op jit(solution)/shard_map/ppermute | solution.py:26
  28.8 0.0 collective-permute-done.8.refs_3_
  28.8 1.3 %collective-permute-start.14 = (bf16[256,1024]{1,0:T(8,128)(2,1)}, bf16[256,1024]{1,0:T(8,128)(2,1)}, u32[]{:S(2)}, u32[]{:S(2)}) collective-permute-start(bf16[256,1024]{1,0:T(8,128)(2,1)} %collective-permute-done.6.refs_1_), channel_id=1, source_target_pairs={{0,1},{1,0},{4,5},{5,4},{2,3},{3,2},{6,7},{7,6},{8,9},{9,8},{12,13... | collective-permute-start | bytes 1572872 | tf_op jit(solution)/shard_map/ppermute | solution.py:26
  30.1 0.0 collective-permute-done.4.refs_4_
  30.1 1.1 %collective-permute-start.10 = (bf16[256,1024]{1,0:T(8,128)(2,1)}, bf16[256,1024]{1,0:T(8,128)(2,1)S(1)}, u32[]{:S(2)}, u32[]{:S(2)}) collective-permute-start(bf16[256,1024]{1,0:T(8,128)(2,1)} %collective-permute-done.6.refs_1_), channel_id=1, source_target_pairs={{0,8},{1,33},{4,12},{5,37},{2,10},{3,35},{6,14},{7,39},{8,16},{9,4... | collective-permute-start | bytes 1572872 | tf_op jit(solution)/shard_map/ppermute | solution.py:26
  31.3 3.4 %collective-permute-done.9.refs_4_ = bf16[272,1024]{1,0:T(8,128)(2,1)S(1)} collective-permute-done((bf16[272,1024]{1,0:T(8,128)(2,1)S(1)}, bf16[272,1024]{1,0:T(8,128)(2,1)S(1)}, u32[]{:S(2)}, u32[]{:S(2)}) %collective-permute-start.9) | collective-permute-done | bytes 557088 | tf_op jit(solution)/shard_map/ppermute | solution.py:26
  34.7 2.7 %collective-permute-start.11 = (bf16[272,1024]{1,0:T(8,128)(2,1)S(1)}, bf16[272,1024]{1,0:T(8,128)(2,1)S(1)}, u32[]{:S(2)}, u32[]{:S(2)}) collective-permute-start(bf16[272,1024]{1,0:T(8,128)(2,1)S(1)} %collective-permute-done.9.refs_4_), channel_id=1, source_target_pairs={{0,24},{1,97},{4,28},{5,101},{2,26},{3,99},{6,30},{7,103},{8,0},{9... | collective-permute-start | bytes 1671176 | tf_op jit(solution)/shard_map/ppermute | solution.py:26
  37.5 0.1 pad_add_fusion.refs_0_.place
  37.5 1.3 %collective-permute-done.7.refs_2_ = bf16[272,1024]{1,0:T(8,128)(2,1)} collective-permute-done((bf16[272,1024]{1,0:T(8,128)(2,1)S(1)}, bf16[272,1024]{1,0:T(8,128)(2,1)}, u32[]{:S(2)}, u32[]{:S(2)}) %collective-permute-start.7) | collective-permute-done | bytes 557088 | tf_op jit(solution)/shard_map/ppermute | solution.py:26
  38.8 1.8 %collective-permute-start.16 = (bf16[256,1024]{1,0:T(8,128)(2,1)}, bf16[256,1024]{1,0:T(8,128)(2,1)S(1)}, u32[]{:S(2)}, u32[]{:S(2)}) collective-permute-start(bf16[256,1024]{1,0:T(8,128)(2,1)} %collective-permute-done.8.refs_3_), channel_id=1, source_target_pairs={{0,1},{1,0},{4,5},{5,4},{2,3},{3,2},{6,7},{7,6},{8,9},{9,8},{12,13... | collective-permute-start | bytes 1572872 | tf_op jit(solution)/shard_map/ppermute | solution.py:26
  40.6 0.0 collective-permute-done.14.refs_1_
  40.6 0.0 collective-permute-start.17
  40.6 0.5 collective-permute-start.15
  41.1 1.0 copy-done.2
  42.2 1.0 copy-done.4
  43.2 1.0 copy-done.5
  44.2 7.3 %chunk.4 = (f32[192,512]{1,0:T(8,128)S(1)}, f32[192,512]{1,0:T(8,128)S(1)}, bf16[384,1024]{1,0:T(8,128)(2,1)S(1)}, f32[4,1024,256]{2,1,0:T(8,128)S(1)}) custom-call(s32[4]{0:T(128)S(1)} %pad_add_fusion.refs_0_.place, bf16[256,1024]{1,0:T(8,128)(2,1)S(1)} %copy-done.2, bf16[272,1024]{1,0:T(8,128)(2,1)S(1)} %get-tuple-element.21.refs_2_, ...), custom_call_target="tpu_custom_call" | custom-call | flops 5100273664 | bytes 1048576 | tf_op jit(solution)/shard_map/chunk/pallas_call | solution.py:162
  51.5 0.0 collective-permute-done.10.refs_1_
  51.5 0.2 collective-permute-start.12
  51.6 0.0 collective-permute-done.11.refs_2_
  51.6 0.4 collective-permute-start.13
  52.1 7.0 %chunk.5 = (f32[192,1024]{1,0:T(8,128)S(1)}, f32[4,1024,256]{2,1,0:T(8,128)S(1)}) custom-call(s32[4]{0:T(128)S(1)} %pad_add_fusion.refs_0_.place, bf16[256,1024]{1,0:T(8,128)(2,1)} %collective-permute-done.6.refs_1_, bf16[272,1024]{1,0:T(8,128)(2,1)} %collective-permute-done.7.refs_2_, ...), custom_call_target="tpu_custom_call", output_to_operand_aliasing={{1}: (7, {})} | custom-call | flops 5100273664 | bytes 1048576 | tf_op jit(solution)/shard_map/chunk/pallas_call | solution.py:162
  59.1 0.0 collective-permute-done.16.refs_3_
  59.1 0.0 collective-permute-done.15.refs_2_
  59.1 6.7 %chunk.6 = (f32[192,1024]{1,0:T(8,128)S(1)}, f32[4,1024,256]{2,1,0:T(8,128)S(1)}) custom-call(s32[4]{0:T(128)S(1)} %pad_add_fusion.refs_0_.place, bf16[256,1024]{1,0:T(8,128)(2,1)} %collective-permute-done.14.refs_1_, bf16[272,1024]{1,0:T(8,128)(2,1)S(1)} %collective-permute-done.15.refs_2_, ...), custom_call_target="tpu_custom_call", output_to_operand_aliasing={{1}: (7, {})} | custom-call | flops 5100273664 | bytes 1048576 | tf_op jit(solution)/shard_map/chunk/pallas_call | solution.py:162
  65.9 0.6 collective-permute-start.19
  66.4 0.0 collective-permute-done.12.refs_3_
  66.4 7.6 %chunk.7 = (f32[192,512]{1,0:T(8,128)S(1)}, f32[192,512]{1,0:T(8,128)S(1)}, bf16[1024,256]{1,0:T(8,128)(2,1)}, bf16[1024,256]{1,0:T(8,128)(2,1)}, bf16[1024,256]...) custom-call(s32[4]{0:T(128)S(1)} %pad_add_fusion.refs_0_.place, ...), custom_call_target="tpu_custom_call" | custom-call | flops 5100273664 | bytes 1048576 | tf_op jit(solution)/shard_map/chunk/pallas_call | solution.py:162
  74.0 1.0 copy-done.6
  75.0 1.3 %collective-permute-start.25 = (f32[1024,256]{1,0:T(8,128)}, f32[1024,256]{1,0:T(8,128)S(1)}, u32[]{:S(2)}, u32[]{:S(2)}) collective-permute-start(f32[1024,256]{1,0:T(8,128)} %get-tuple-element.37), channel_id=1, source_target_pairs={{0,1},{5,4},{2,3},{7,6},{8,9},{13,12},{10,11},{15,14},{16,17},{21,... | collective-permute-start | bytes 3145736 | tf_op jit(solution)/shard_map/ppermute | solution.py:26
  76.3 1.3 %collective-permute-start.20 = (f32[192,512]{1,0:T(8,128)S(1)}, f32[192,512]{1,0:T(8,128)S(1)}, u32[]{:S(2)}, u32[]{:S(2)}) collective-permute-start(f32[192,512]{1,0:T(8,128)S(1)} %get-tuple-element.31), channel_id=1, source_target_pairs={{0,1},{1,0},{4,5},{5,4},{2,3},{3,2},{6,7},{7,6},{8,9},{9,8},{12,13... | collective-permute-start | bytes 1179656 | tf_op jit(solution)/shard_map/ppermute | solution.py:26
  77.5 0.1 collective-permute-start.18
  77.6 2.5 %collective-permute-done.20.refs_5_ = f32[192,512]{1,0:T(8,128)S(1)} collective-permute-done((f32[192,512]{1,0:T(8,128)S(1)}, f32[192,512]{1,0:T(8,128)S(1)}, u32[]{:S(2)}, u32[]{:S(2)}) %collective-permute-start.20) | collective-permute-done | bytes 393248 | tf_op jit(solution)/shard_map/ppermute | solution.py:26
  80.1 2.8 %collective-permute-start.22 = (bf16[1024,256]{1,0:T(8,128)(2,1)}, bf16[1024,256]{1,0:T(8,128)(2,1)S(1)}, u32[]{:S(2)}, u32[]{:S(2)}) collective-permute-start(bf16[1024,256]{1,0:T(8,128)(2,1)} %get-tuple-element.34), channel_id=1, source_target_pairs={{1,7},{4,0},{3,5},{6,2},{9,15},{12,8},{11,13},{14,10},{17,23},{20,... | collective-permute-start | bytes 1572872 | tf_op jit(solution)/shard_map/ppermute | solution.py:26
  82.9 0.0 collective-permute-done.18.refs_3_
  82.9 1.2 %collective-permute-start.23 = (bf16[1024,256]{1,0:T(8,128)(2,1)}, bf16[1024,256]{1,0:T(8,128)(2,1)}, u32[]{:S(2)}, u32[]{:S(2)}) collective-permute-start(bf16[1024,256]{1,0:T(8,128)(2,1)} %get-tuple-element.35), channel_id=1, source_target_pairs={{0,2},{1,4},{4,3},{5,7},{2,0},{3,6},{6,1},{7,5},{8,10},{9,12},{12,... | collective-permute-start | bytes 1572872 | tf_op jit(solution)/shard_map/ppermute | solution.py:26
  84.1 3.7 %collective-permute-start.24 = (bf16[1024,256]{1,0:T(8,128)(2,1)}, bf16[1024,256]{1,0:T(8,128)(2,1)}, u32[]{:S(2)}, u32[]{:S(2)}) collective-permute-start(bf16[1024,256]{1,0:T(8,128)(2,1)} %get-tuple-element.36), channel_id=1, source_target_pairs={{1,6},{4,1},{3,4},{6,3},{9,14},{12,9},{11,12},{14,11},{17,22},{20,... | collective-permute-start | bytes 1572872 | tf_op jit(solution)/shard_map/ppermute | solution.py:26
  87.8 1.6 %pack.1 = bf16[16,192,128]{2,1,0:T(8,128)(2,1)} custom-call(s32[4]{0:T(128)S(1)} %pad_add_fusion.refs_0_.place, f32[192,512]{1,0:T(8,128)S(1)} %get-tuple-element.22.refs_0_, f32[192,1024]{1,0:T(8,128)S(1)} %get-tuple-element.25.refs_1_, f32[192,512]{1,0:T(8,128)S(1)} %get-tuple-element.28.refs_2_, f32[192,512]{1,0:T(8,128)S(1)} %collective-permute-done.18.refs_3_, ...), custom_call_target="tpu_custom_call" | custom-call | flops 1000000 | bytes 1024 | tf_op jit(solution)/shard_map/pack/pallas_call | solution.py:217
  89.5 3.6 %all-to-all-start = ((bf16[16,192,128]{2,1,0:T(8,128)(2,1)}), bf16[16,192,128]{2,1,0:T(8,128)(2,1)S(1)}, u32[]{:S(2)}, u32[]{:S(2)}) async-start(bf16[16,192,128]{2,1,0:T(8,128)(2,1)} %pack.1), calls=%async_computation | async-start | bytes 1572864 | tf_op jit(solution)/shard_map/all_to_all | solution.py:271
  93.1 0.5 collective-permute-done.21.refs_0_
  93.6 2.4 %collective-permute-done.22.refs_1_ = bf16[1024,256]{1,0:T(8,128)(2,1)S(1)} collective-permute-done((bf16[1024,256]{1,0:T(8,128)(2,1)}, bf16[1024,256]{1,0:T(8,128)(2,1)S(1)}, u32[]{:S(2)}, u32[]{:S(2)}) %collective-permute-start.22) | collective-permute-done | bytes 524320 | tf_op jit(solution)/shard_map/ppermute | solution.py:26
  96.0 8.9 %collective-permute-done.23.refs_2_ = bf16[1024,256]{1,0:T(8,128)(2,1)} collective-permute-done((bf16[1024,256]{1,0:T(8,128)(2,1)}, bf16[1024,256]{1,0:T(8,128)(2,1)}, u32[]{:S(2)}, u32[]{:S(2)}) %collective-permute-start.23) | collective-permute-done | bytes 524320 | tf_op jit(solution)/shard_map/ppermute | solution.py:26
  104.9 0.0 collective-permute-done.24.refs_3_
  104.9 1.2 %copy-done.7 = f32[1024,256]{1,0:T(8,128)S(1)} copy-done((f32[1024,256]{1,0:T(8,128)S(1)}, f32[1024,256]{1,0:T(8,128)}, u32[]{:S(2)}) %copy-start.7) | copy-done | bytes 1048600
  106.2 2.4 %join.1 = bf16[1024,256]{1,0:T(8,128)(2,1)} custom-call(s32[4]{0:T(128)S(1)} %pad_add_fusion.refs_0_.place, f32[1024,256]{1,0:T(8,128)S(1)} %copy-done.7, bf16[1024,256]{1,0:T(8,128)(2,1)S(1)} %collective-permute-done.21.refs_0_, bf16[1024,256]{1,0:T(8,128)(2,1)S(1)} %collective-permute-done.22.refs_1_, bf16[1024,256]{1,0:T(8,128)(2,1)} %collective-permute-done.23.refs_2_, ...), custom_call_target="tpu_custom_call" | custom-call | flops 99999997952 | bytes 1024 | tf_op jit(solution)/shard_map/join/pallas_call | solution.py:217
  108.6 1.2 %decode.1 = bf16[128,1024]{1,0:T(8,128)(2,1)} custom-call(bf16[16,192,128]{2,1,0:T(8,128)(2,1)S(1)} %all-to-all-done.parts_ref, bf16[192,1024]{1,0:T(8,128)(2,1)S(1)} %copy-done), custom_call_target="tpu_custom_call" | custom-call | flops 1000000 | bytes 1024 | tf_op jit(solution)/shard_map/decode/pallas_call | solution.py:217
  (20 shorter events, 0.1 us)
Async XLA Ops:
  0.6 40.0 %collective-permute-start.5 = (bf16[1024,1024]{1,0:T(8,128)(2,1)}, bf16[1024,1024]{1,0:T(8,128)(2,1)S(1)}, u32[]{:S(2)}, u32[]{:S(2)}) collective-permute-start(bf16[1024,1024]{1,0:T(8,128)(2,1)} %param.9), channel_id=1, source_target_pairs={{0,4},{1,0},{4,5},{5,1},{2,6},{3,2},{6,7},{7,3},{8,12},{9,8},{12,1... | collective-permute-start | bytes 6291464 | tf_op jit(solution)/shard_map/ppermute | solution.py:26
  4.0 7.3 %collective-permute-start = (bf16[144,1024]{1,0:T(8,128)(2,1)S(1)}, bf16[144,1024]{1,0:T(8,128)(2,1)S(1)}, u32[]{:S(2)}, u32[]{:S(2)}) collective-permute-start(bf16[144,1024]{1,0:T(8,128)(2,1)S(1)} %maximum_maximum_fusion.own_ref), channel_id=1, source_target_pairs={{0,32},{1,9},{4,36},{5,13},{2,34},{3,11},{6,38},{7,15},{8,40},{9,1... | collective-permute-start | bytes 884744 | tf_op jit(solution)/shard_map/ppermute | solution.py:26
  5.4 8.3 %collective-permute-start.1 = (bf16[144,1024]{1,0:T(8,128)(2,1)S(1)}, bf16[144,1024]{1,0:T(8,128)(2,1)S(1)}, u32[]{:S(2)}, u32[]{:S(2)}) collective-permute-start(bf16[144,1024]{1,0:T(8,128)(2,1)S(1)} %maximum_maximum_fusion.own_ref), channel_id=1, source_target_pairs={{0,96},{1,25},{4,100},{5,29},{2,98},{3,27},{6,102},{7,31},{8,104},... | collective-permute-start | bytes 884744 | tf_op jit(solution)/shard_map/ppermute | solution.py:26
  7.0 8.7 %collective-permute-start.2 = (bf16[144,1024]{1,0:T(8,128)(2,1)S(1)}, bf16[144,1024]{1,0:T(8,128)(2,1)S(1)}, u32[]{:S(2)}, u32[]{:S(2)}) collective-permute-start(bf16[144,1024]{1,0:T(8,128)(2,1)S(1)} %maximum_maximum_fusion.own_ref), channel_id=1, source_target_pairs={{0,64},{1,17},{4,68},{5,21},{2,66},{3,19},{6,70},{7,23},{8,72},{9,... | collective-permute-start | bytes 884744 | tf_op jit(solution)/shard_map/ppermute | solution.py:26
  15.7 7.6 %collective-permute-start.3 = (bf16[256,1024]{1,0:T(8,128)(2,1)S(1)}, bf16[256,1024]{1,0:T(8,128)(2,1)S(1)}, u32[]{:S(2)}, u32[]{:S(2)}) collective-permute-start(bf16[256,1024]{1,0:T(8,128)(2,1)S(1)} %get-tuple-element.20.refs_1_), channel_id=1, source_target_pairs={{0,1},{1,0},{4,5},{5,4},{2,3},{3,2},{6,7},{7,6},{8,9},{9,8},{12,13... | collective-permute-start | bytes 1572872 | tf_op jit(solution)/shard_map/ppermute | solution.py:26
  19.2 9.6 %collective-permute-start.6 = (bf16[256,1024]{1,0:T(8,128)(2,1)S(1)}, bf16[256,1024]{1,0:T(8,128)(2,1)}, u32[]{:S(2)}, u32[]{:S(2)}) collective-permute-start(bf16[256,1024]{1,0:T(8,128)(2,1)S(1)} %get-tuple-element.20.refs_1_), channel_id=1, source_target_pairs={{0,8},{1,33},{4,12},{5,37},{2,10},{3,35},{6,14},{7,39},{8,16},{9,4... | collective-permute-start | bytes 1572872 | tf_op jit(solution)/shard_map/ppermute | solution.py:26
  20.3 8.5 %collective-permute-start.8 = (bf16[256,1024]{1,0:T(8,128)(2,1)S(1)}, bf16[256,1024]{1,0:T(8,128)(2,1)}, u32[]{:S(2)}, u32[]{:S(2)}) collective-permute-start(bf16[256,1024]{1,0:T(8,128)(2,1)S(1)} %get-tuple-element.20.refs_1_), channel_id=1, source_target_pairs={{0,24},{1,97},{4,28},{5,101},{2,26},{3,99},{6,30},{7,103},{8,0},{9... | collective-permute-start | bytes 1572872 | tf_op jit(solution)/shard_map/ppermute | solution.py:26
  21.8 0.8 copy-start.1
  22.6 7.5 %collective-permute-start.4 = (bf16[272,1024]{1,0:T(8,128)(2,1)S(1)}, bf16[272,1024]{1,0:T(8,128)(2,1)}, u32[]{:S(2)}, u32[]{:S(2)}) collective-permute-start(bf16[272,1024]{1,0:T(8,128)(2,1)S(1)} %get-tuple-element.21.refs_2_), channel_id=1, source_target_pairs={{0,1},{1,0},{4,5},{5,4},{2,3},{3,2},{6,7},{7,6},{8,9},{9,8},{12,13... | collective-permute-start | bytes 1671176 | tf_op jit(solution)/shard_map/ppermute | solution.py:26
  23.3 0.8 copy-start.3
  24.1 10.6 %collective-permute-start.9 = (bf16[272,1024]{1,0:T(8,128)(2,1)S(1)}, bf16[272,1024]{1,0:T(8,128)(2,1)S(1)}, u32[]{:S(2)}, u32[]{:S(2)}) collective-permute-start(bf16[272,1024]{1,0:T(8,128)(2,1)S(1)} %get-tuple-element.21.refs_2_), channel_id=1, source_target_pairs={{0,24},{1,97},{4,28},{5,101},{2,26},{3,99},{6,30},{7,103},{8,0},{9... | collective-permute-start | bytes 1671176 | tf_op jit(solution)/shard_map/ppermute | solution.py:26
  28.8 10.0 %collective-permute-start.7 = (bf16[272,1024]{1,0:T(8,128)(2,1)S(1)}, bf16[272,1024]{1,0:T(8,128)(2,1)}, u32[]{:S(2)}, u32[]{:S(2)}) collective-permute-start(bf16[272,1024]{1,0:T(8,128)(2,1)S(1)} %get-tuple-element.21.refs_2_), channel_id=1, source_target_pairs={{0,8},{1,33},{4,12},{5,37},{2,10},{3,35},{6,14},{7,39},{8,16},{9,4... | collective-permute-start | bytes 1671176 | tf_op jit(solution)/shard_map/ppermute | solution.py:26
  28.8 11.8 %collective-permute-start.14 = (bf16[256,1024]{1,0:T(8,128)(2,1)}, bf16[256,1024]{1,0:T(8,128)(2,1)}, u32[]{:S(2)}, u32[]{:S(2)}) collective-permute-start(bf16[256,1024]{1,0:T(8,128)(2,1)} %collective-permute-done.6.refs_1_), channel_id=1, source_target_pairs={{0,1},{1,0},{4,5},{5,4},{2,3},{3,2},{6,7},{7,6},{8,9},{9,8},{12,13... | collective-permute-start | bytes 1572872 | tf_op jit(solution)/shard_map/ppermute | solution.py:26
  30.1 21.3 %collective-permute-start.10 = (bf16[256,1024]{1,0:T(8,128)(2,1)}, bf16[256,1024]{1,0:T(8,128)(2,1)S(1)}, u32[]{:S(2)}, u32[]{:S(2)}) collective-permute-start(bf16[256,1024]{1,0:T(8,128)(2,1)} %collective-permute-done.6.refs_1_), channel_id=1, source_target_pairs={{0,8},{1,33},{4,12},{5,37},{2,10},{3,35},{6,14},{7,39},{8,16},{9,4... | collective-permute-start | bytes 1572872 | tf_op jit(solution)/shard_map/ppermute | solution.py:26
  34.7 16.9 %collective-permute-start.11 = (bf16[272,1024]{1,0:T(8,128)(2,1)S(1)}, bf16[272,1024]{1,0:T(8,128)(2,1)S(1)}, u32[]{:S(2)}, u32[]{:S(2)}) collective-permute-start(bf16[272,1024]{1,0:T(8,128)(2,1)S(1)} %collective-permute-done.9.refs_4_), channel_id=1, source_target_pairs={{0,24},{1,97},{4,28},{5,101},{2,26},{3,99},{6,30},{7,103},{8,0},{9... | collective-permute-start | bytes 1671176 | tf_op jit(solution)/shard_map/ppermute | solution.py:26
  38.8 20.3 %collective-permute-start.16 = (bf16[256,1024]{1,0:T(8,128)(2,1)}, bf16[256,1024]{1,0:T(8,128)(2,1)S(1)}, u32[]{:S(2)}, u32[]{:S(2)}) collective-permute-start(bf16[256,1024]{1,0:T(8,128)(2,1)} %collective-permute-done.8.refs_3_), channel_id=1, source_target_pairs={{0,1},{1,0},{4,5},{5,4},{2,3},{3,2},{6,7},{7,6},{8,9},{9,8},{12,13... | collective-permute-start | bytes 1572872 | tf_op jit(solution)/shard_map/ppermute | solution.py:26
  40.6 18.5 %collective-permute-start.17 = (bf16[272,1024]{1,0:T(8,128)(2,1)S(1)}, bf16[272,1024]{1,0:T(8,128)(2,1)S(1)}, u32[]{:S(2)}, u32[]{:S(2)}) collective-permute-start(bf16[272,1024]{1,0:T(8,128)(2,1)S(1)} %collective-permute-done.9.refs_4_), channel_id=1, source_target_pairs={{0,1},{1,0},{4,5},{5,4},{2,3},{3,2},{6,7},{7,6},{8,9},{9,8},{12,13... | collective-permute-start | bytes 1671176 | tf_op jit(solution)/shard_map/ppermute | solution.py:26
  40.6 18.5 %collective-permute-start.15 = (bf16[272,1024]{1,0:T(8,128)(2,1)}, bf16[272,1024]{1,0:T(8,128)(2,1)S(1)}, u32[]{:S(2)}, u32[]{:S(2)}) collective-permute-start(bf16[272,1024]{1,0:T(8,128)(2,1)} %collective-permute-done.7.refs_2_), channel_id=1, source_target_pairs={{0,1},{1,0},{4,5},{5,4},{2,3},{3,2},{6,7},{7,6},{8,9},{9,8},{12,13... | collective-permute-start | bytes 1671176 | tf_op jit(solution)/shard_map/ppermute | solution.py:26
  41.1 1.0 copy-start.2
  42.2 1.0 copy-start.4
  43.2 1.0 copy-start.5
  51.5 15.0 %collective-permute-start.12 = (bf16[256,1024]{1,0:T(8,128)(2,1)S(1)}, bf16[256,1024]{1,0:T(8,128)(2,1)S(1)}, u32[]{:S(2)}, u32[]{:S(2)}) collective-permute-start(bf16[256,1024]{1,0:T(8,128)(2,1)S(1)} %collective-permute-done.10.refs_1_), channel_id=1, source_target_pairs={{0,1},{1,0},{4,5},{5,4},{2,3},{3,2},{6,7},{7,6},{8,9},{9,8},{12,13... | collective-permute-start | bytes 1572872 | tf_op jit(solution)/shard_map/ppermute | solution.py:26
  51.6 14.8 %collective-permute-start.13 = (bf16[272,1024]{1,0:T(8,128)(2,1)S(1)}, bf16[272,1024]{1,0:T(8,128)(2,1)S(1)}, u32[]{:S(2)}, u32[]{:S(2)}) collective-permute-start(bf16[272,1024]{1,0:T(8,128)(2,1)S(1)} %collective-permute-done.11.refs_2_), channel_id=1, source_target_pairs={{0,1},{1,0},{4,5},{5,4},{2,3},{3,2},{6,7},{7,6},{8,9},{9,8},{12,13... | collective-permute-start | bytes 1671176 | tf_op jit(solution)/shard_map/ppermute | solution.py:26
  65.9 18.3 %collective-permute-start.19 = (f32[192,1024]{1,0:T(8,128)S(1)}, f32[192,1024]{1,0:T(8,128)S(1)}, u32[]{:S(2)}, u32[]{:S(2)}) collective-permute-start(f32[192,1024]{1,0:T(8,128)S(1)} %get-tuple-element.30), channel_id=1, source_target_pairs={{0,1},{1,0},{4,5},{5,4},{2,3},{3,2},{6,7},{7,6},{8,9},{9,8},{12,13... | collective-permute-start | bytes 2359304 | tf_op jit(solution)/shard_map/ppermute | solution.py:26
  74.0 1.0 copy-start.6
  75.0 29.9 %collective-permute-start.25 = (f32[1024,256]{1,0:T(8,128)}, f32[1024,256]{1,0:T(8,128)S(1)}, u32[]{:S(2)}, u32[]{:S(2)}) collective-permute-start(f32[1024,256]{1,0:T(8,128)} %get-tuple-element.37), channel_id=1, source_target_pairs={{0,1},{5,4},{2,3},{7,6},{8,9},{13,12},{10,11},{15,14},{16,17},{21,... | collective-permute-start | bytes 3145736 | tf_op jit(solution)/shard_map/ppermute | solution.py:26
  76.3 3.8 %collective-permute-start.20 = (f32[192,512]{1,0:T(8,128)S(1)}, f32[192,512]{1,0:T(8,128)S(1)}, u32[]{:S(2)}, u32[]{:S(2)}) collective-permute-start(f32[192,512]{1,0:T(8,128)S(1)} %get-tuple-element.31), channel_id=1, source_target_pairs={{0,1},{1,0},{4,5},{5,4},{2,3},{3,2},{6,7},{7,6},{8,9},{9,8},{12,13... | collective-permute-start | bytes 1179656 | tf_op jit(solution)/shard_map/ppermute | solution.py:26
  77.5 5.3 %collective-permute-start.18 = (f32[192,512]{1,0:T(8,128)S(1)}, f32[192,512]{1,0:T(8,128)S(1)}, u32[]{:S(2)}, u32[]{:S(2)}) collective-permute-start(f32[192,512]{1,0:T(8,128)S(1)} %get-tuple-element.29), channel_id=1, source_target_pairs={{0,1},{1,0},{4,5},{5,4},{2,3},{3,2},{6,7},{7,6},{8,9},{9,8},{12,13... | collective-permute-start | bytes 1179656 | tf_op jit(solution)/shard_map/ppermute | solution.py:26
  77.6 16.0 %collective-permute-start.21 = (bf16[1024,256]{1,0:T(8,128)(2,1)}, bf16[1024,256]{1,0:T(8,128)(2,1)S(1)}, u32[]{:S(2)}, u32[]{:S(2)}) collective-permute-start(bf16[1024,256]{1,0:T(8,128)(2,1)} %get-tuple-element.33), channel_id=1, source_target_pairs={{0,3},{1,5},{4,2},{5,6},{2,1},{3,7},{6,0},{7,4},{8,11},{9,13},{12,... | collective-permute-start | bytes 1572872 | tf_op jit(solution)/shard_map/ppermute | solution.py:26
  80.1 15.9 %collective-permute-start.22 = (bf16[1024,256]{1,0:T(8,128)(2,1)}, bf16[1024,256]{1,0:T(8,128)(2,1)S(1)}, u32[]{:S(2)}, u32[]{:S(2)}) collective-permute-start(bf16[1024,256]{1,0:T(8,128)(2,1)} %get-tuple-element.34), channel_id=1, source_target_pairs={{1,7},{4,0},{3,5},{6,2},{9,15},{12,8},{11,13},{14,10},{17,23},{20,... | collective-permute-start | bytes 1572872 | tf_op jit(solution)/shard_map/ppermute | solution.py:26
  82.9 22.0 %collective-permute-start.23 = (bf16[1024,256]{1,0:T(8,128)(2,1)}, bf16[1024,256]{1,0:T(8,128)(2,1)}, u32[]{:S(2)}, u32[]{:S(2)}) collective-permute-start(bf16[1024,256]{1,0:T(8,128)(2,1)} %get-tuple-element.35), channel_id=1, source_target_pairs={{0,2},{1,4},{4,3},{5,7},{2,0},{3,6},{6,1},{7,5},{8,10},{9,12},{12,... | collective-permute-start | bytes 1572872 | tf_op jit(solution)/shard_map/ppermute | solution.py:26
  84.1 20.8 %collective-permute-start.24 = (bf16[1024,256]{1,0:T(8,128)(2,1)}, bf16[1024,256]{1,0:T(8,128)(2,1)}, u32[]{:S(2)}, u32[]{:S(2)}) collective-permute-start(bf16[1024,256]{1,0:T(8,128)(2,1)} %get-tuple-element.36), channel_id=1, source_target_pairs={{1,6},{4,1},{3,4},{6,3},{9,14},{12,9},{11,12},{14,11},{17,22},{20,... | collective-permute-start | bytes 1572872 | tf_op jit(solution)/shard_map/ppermute | solution.py:26
  89.5 19.1 %all-to-all-start = ((bf16[16,192,128]{2,1,0:T(8,128)(2,1)}), bf16[16,192,128]{2,1,0:T(8,128)(2,1)S(1)}, u32[]{:S(2)}, u32[]{:S(2)}) async-start(bf16[16,192,128]{2,1,0:T(8,128)(2,1)} %pack.1), calls=%async_computation | async-start | bytes 1572864 | tf_op jit(solution)/shard_map/all_to_all | solution.py:271
  104.9 1.2 %copy-start.7 = (f32[1024,256]{1,0:T(8,128)S(1)}, f32[1024,256]{1,0:T(8,128)}, u32[]{:S(2)}) copy-start(f32[1024,256]{1,0:T(8,128)} %copy-done.6) | copy-start | bytes 3145732
  106.2 2.4 %copy-start = (bf16[192,1024]{1,0:T(8,128)(2,1)S(1)}, bf16[192,1024]{1,0:T(8,128)(2,1)}, u32[]{:S(2)}) copy-start(bf16[192,1024]{1,0:T(8,128)(2,1)} %dec_ref.1) | copy-start | bytes 1179652

commit v3 on v2

--- a/solution.py
+++ b/solution.py
@@ -38,19 +38,22 @@
     return (z, y, x ^ 1, c) if c == x % 2 else (z, y, x, 1 - c)
 
 
-def rows_kernel(own_ref, back_ref, ahead_ref, far_ref, low_ref, high_ref):
-    low_ref[:128, :] = own_ref[:128, :]
-    low_ref[128:, :] = back_ref[:128, :]
-    high_ref[:128, :] = ahead_ref[:128, :]
-    high_ref[128:256, :] = far_ref[:128, :]
+def row_kernel(place, own_ref, back_ref, ahead_ref, far_ref, row_ref):
     refs = (own_ref, back_ref, ahead_ref, far_ref)
+    for i, ref in enumerate(refs):
+        row_ref[i * 128 : i * 128 + 128, :] = ref[:128, :]
     row = lax.broadcasted_iota(I32, (TAIL, 1024), 0)
     tail = jnp.zeros((TAIL, 1024), F32)
     for i, ref in enumerate(refs):
         ids = ref[128:144, :].astype(F32)
         for digit in range(2):
             tail = jnp.where(row == 2 * i + digit, ids[digit : digit + 1, :], tail)
-    high_ref[256:, :] = tail.astype(BF16)
+    row_ref[512:, :] = tail.astype(BF16)
+
+
+def halves_kernel(back_ref, ahead_ref, low_ref, high_ref):
+    low_ref[...] = back_ref[:256, :]
+    high_ref[...] = ahead_ref[256:, :]
 
 
 def encode(w_ref, enc_ref, wet_ref):
@@ -83,17 +86,20 @@
     half, next_half = x // 2, lax.rem(x + 1, 4) // 2
     away = jnp.where(keeps, 1 - half, next_half)
     column = jnp.where(keeps, 1 - core, core)
-    return 2 * away + column, 2 * (1 - away) + core, 2 * away + 1 - column, 2 * (1 - away) + 1 - core
-
-
-def chunk_kernel(enc_at, first, last, scale, *refs):
+    return 2 * away + column, 2 * (1 - away) + column, 2 * away + 1 - column, 2 * (1 - away) + 1 - column
+
+
+def chunk_kernel(parts, enc_at, first, last, scale, *refs):
     n = len(enc_at)
-    place, q_refs, refs = refs[0], refs[1 : 1 + 2 * n], refs[1 + 2 * n :]
+    n_q = sum(parts)
+    place, q_refs, refs = refs[0], refs[1 : 1 + n_q], refs[1 + n_q :]
     z, y, x, core = (place[i] for i in range(4))
     base = ((z * 4 + y) * 2 + core) * 2 * HALF
     w_ref, enc_ref, refs = refs[0], refs[1], refs[2:]
     if not first:
         total_ref, refs = refs[0], refs[1:]
+    if last:
+        refs, (narrow, out_sems) = refs[:-2], refs[-2:]
     outs, (q_all, grads, bits) = refs[:-3], refs[-3:]
     n_enc = 1 + max(out for out, _ in enc_at)
     encs, outs = outs[:n_enc], outs[n_enc:]
@@ -103,10 +109,12 @@
     else:
         wet_ref = enc_ref
     for i in range(n):
-        low, high = q_refs[2 * i : 2 * i + 2]
-        q_all[512 * i : 512 * i + 256, :] = low[...]
-        q_all[512 * i + 256 : 512 * i + 512, :] = high[:256, :]
-        tail = high[256:272, :].astype(F32).astype(I32)
+        bufs, q_refs = q_refs[: parts[i]], q_refs[parts[i] :]
+        size = 512 // parts[i]
+        for j, buf in enumerate(bufs):
+            at = 512 * i + size * j
+            q_all[at : at + size, :] = buf[:size, :]
+        tail = bufs[-1][size : size + TAIL, :].astype(F32).astype(I32)
         for b in range(4):
             lanes = slice(512 * i + 128 * b, 512 * i + 128 * b + 128)
             for w, word in enumerate(target_bits(tail, b, base)):
@@ -135,37 +143,47 @@
     for i, (out, column) in enumerate(enc_at):
         encs[out][:, column : column + 512] = encoded[:, 512 * i : 512 * i + 512]
     if last:
+        copies = []
         for o, c in enumerate(quarters(x, core)):
             columns = q_all[:, pl.ds(pl.multiple_of(c * 256, 256), 256)]
             whole = total_ref[c] + jnp.dot(grads[...], columns, preferred_element_type=F32)
-            outs[o][...] = whole.astype(BF16)
-            if o % 2:
-                outs[4 + o // 2][...] = whole
-
-
-def chunk(place, q_bufs, enc_at, w, enc, total, last, scale):
+            narrow[o] = whole.astype(BF16)
+            copies.append(pltpu.make_async_copy(narrow.at[o], outs[o], out_sems.at[o]))
+            copies[-1].start()
+        for copy in copies:
+            copy.wait()
+
+
+def chunk(place, groups, enc_at, w, enc, total, last, scale):
     first = total is None
     vmem = pl.BlockSpec(memory_space=pltpu.VMEM)
     widths = [0] * (1 + max(out for out, _ in enc_at))
     for out, column in enc_at:
         widths[out] = max(widths[out], column + 512)
-    args = [place, *q_bufs, w, enc] + ([] if first else [total])
+    args = [place, *sum(groups, []), w, enc] + ([] if first else [total])
     labels = 2 * HALF
     shapes = [jax.ShapeDtypeStruct((192, n), F32) for n in widths]
     if first:
         shapes.append(jax.ShapeDtypeStruct((384, labels), BF16))
     if last:
-        shapes += [jax.ShapeDtypeStruct((labels, 256), d) for d in (BF16,) * 4 + (F32,) * 2]
+        shapes += [jax.ShapeDtypeStruct((labels, 256), d) for d in (BF16,) * 4]
     else:
         shapes.append(jax.ShapeDtypeStruct((4, labels, 256), F32))
     n = 512 * len(enc_at)
+    out_specs, scratch = [vmem] * len(shapes), []
+    if last:
+        out_specs[-4:] = [pl.BlockSpec(memory_space=pltpu.HBM)] * 4
+        scratch = [pltpu.VMEM((4, labels, 256), BF16), pltpu.SemaphoreType.DMA((4,))]
     return pl.pallas_call(
-        functools.partial(chunk_kernel, enc_at, first, last, scale),
+        functools.partial(chunk_kernel, [len(g) for g in groups], enc_at, first, last, scale),
         in_specs=[pl.BlockSpec(memory_space=pltpu.SMEM)] + [vmem] * (len(args) - 1),
-        out_specs=[vmem] * len(shapes),
+        out_specs=out_specs,
         out_shape=shapes,
         scratch_shapes=[
-            pltpu.VMEM((n, 1024), BF16), pltpu.VMEM((labels, n), BF16), pltpu.VMEM((4, 8, n), I32)
+            pltpu.VMEM((n, 1024), BF16),
+            pltpu.VMEM((labels, n), BF16),
+            pltpu.VMEM((4, 8, n), I32),
+            *scratch,
         ],
         input_output_aliases={} if first or last else {len(args) - 1: len(shapes) - 1},
         compiler_params=pltpu.CompilerParams(vmem_limit_bytes=VMEM_LIMIT),
@@ -189,29 +207,29 @@
             out[jnp.where(core == 0, j * 4 + i, i * 4 + j)] = value[:, block * 128 : block * 128 + 128]
 
 
-def decode_kernel(parts_ref, dec_ref, out_ref):
+def decode_kernel(parts_ref, dec_ref, after_ref, out_ref):
     total = parts_ref[0].astype(F32)
     for i in range(1, 16):
         total += parts_ref[i].astype(F32)
-    dec = dec_ref[...]
     rest, result = total, None
     for _ in range(3):
         digit = rest.astype(BF16)
         rest = rest - digit.astype(F32)
-        part = lax.dot_general(digit, dec, (((0,), (0,)), ((), ())), preferred_element_type=F32)
+        part = lax.dot_general(digit, dec_ref[...], (((0,), (0,)), ((), ())), preferred_element_type=F32)
         result = part if result is None else result + part
     out_ref[...] = result.astype(BF16)
 
 
-def join_kernel(place, own_ref, *refs):
-    total = jnp.where(place[3] == lax.rem(place[2], 2), own_ref[...], 0.0)
-    for ref in refs[:-1]:
+def join_kernel(*refs):
+    total = refs[0][...].astype(F32)
+    for ref in refs[1:4]:
         total += ref[...].astype(F32)
-    refs[-1][...] = total.astype(BF16)
+    refs[4][...] = total.astype(BF16)
+    refs[5][...] = jnp.zeros_like(refs[5])
 
 
 def kernel(body, out, *args, name, flops=10**6):
-    place = lambda a: pltpu.SMEM if a.dtype == I32 else pltpu.VMEM
+    place = lambda a: pltpu.SMEM if a.shape == (4,) else pltpu.VMEM
     one = not isinstance(out[0][0], tuple)
     shapes = [jax.ShapeDtypeStruct(*o) for o in ([out] if one else out)]
     result = pl.pallas_call(
@@ -226,6 +244,22 @@
     return result[0] if one else result
 
 
+def after(arrays, *others):
+    anywhere = pl.BlockSpec(memory_space=pl.ANY)
+    n = len(arrays)
+    tied = pl.pallas_call(
+        lambda *refs: None,
+        in_specs=[anywhere] * (n + len(others)),
+        out_specs=[anywhere] * n,
+        out_shape=[jax.ShapeDtypeStruct(a.shape, a.dtype) for a in arrays],
+        input_output_aliases={i: i for i in range(n)},
+        compiler_params=pltpu.CompilerParams(vmem_limit_bytes=2**20),
+        cost_estimate=pl.CostEstimate(flops=0, bytes_accessed=0, transcendentals=0),
+        name="after",
+    )(*arrays, *others)
+    return list(tied)
+
+
 def shards(queries, label_ids, label_counts, weights, encoder, decoder):
     z, y, xl, xh, core = (lax.axis_index(a) for a in AXES)
     scale = float(queries.shape[0] * 128) ** (-0.5)
@@ -238,39 +272,41 @@
     place = jnp.stack([z, y, 2 * xh + xl, core]).astype(I32)
     w = move(weights, to_user)
     back, ahead, far = (move(own, hop(0, step)) for step in (1, -1, 2))
-    low, high = kernel(
-        rows_kernel, (((256, 1024), BF16), ((256 + TAIL, 1024), BF16)), own, back, ahead, far, name="rows"
-    )
-    low_back, high_ahead = move(low, hop(1, 1)), move(high, hop(1, -1))
-    high_back, low_ahead = move(high, hop(1, 1)), move(low, hop(1, -1))
-    low_far, high_far = move(low_back, hop(1, 1)), move(high_ahead, hop(1, -1))
-    rows, backs, aheads, fars = [low, high], [low_back, high_back], [low_ahead, high_ahead], [low_far, high_far]
+    row = kernel(row_kernel, ((512 + TAIL, 1024), BF16), place, own, back, ahead, far, name="row")
+    row_back, row_ahead = move(row, hop(1, 1)), move(row, hop(1, -1))
     sibling = lambda bufs: [move(b, to_sibling) for b in bufs]
-
     apart, joined = ((0, 0), (1, 0)), ((0, 0), (0, 512))
-    enc_a, enc_sa, wet, total = chunk(place, rows + sibling(rows), apart, w, encoder.T, None, False, scale)
-    enc_b, total = chunk(place, backs + aheads, joined, w, wet, total, False, scale)
-    enc_sb, total = chunk(place, sibling(backs) + sibling(aheads), joined, w, wet, total, False, scale)
-    enc_c, enc_sc, out_0, out_1, out_2, out_3, kept, sib = chunk(
-        place, fars + sibling(fars), apart, w, wet, total, True, scale
+    enc_a, enc_sa, wet, total = chunk(
+        place, [[row], sibling([row])], apart, w, encoder.T, None, False, scale
+    )
+    half_shapes = (((256, 1024), BF16), ((256 + TAIL, 1024), BF16))
+    row_back, row_ahead = after([row_back, row_ahead], wet)
+    low, high = kernel(halves_kernel, half_shapes, row_back, row_ahead, name="halves")
+    far = [move(low, hop(1, 1)), move(high, hop(1, -1))]
+    enc_b, total = chunk(place, [[row_back], [row_ahead]], joined, w, wet, total, False, scale)
+    enc_sb, total = chunk(
+        place, [sibling([row_back]), sibling([row_ahead])], joined, w, wet, total, False, scale
+    )
+    far = after(far, enc_sb)
+    enc_c, enc_sc, out_0, out_1, out_2, out_3 = chunk(
+        place, [far, sibling(far)], apart, w, wet, total, True, scale
     )
 
     pick = lambda same, other: lambda z, y, x, c: same(z, y, x, c) if c == x % 2 else other(z, y, x, c)
-    none = lambda z, y, x, c: None
     got = [
         move(out_0, pick(lambda z, y, x, c: (z, y, x + 2, 1 - c), lambda z, y, x, c: (z, y, x + 1, c))),
-        move(out_1, pick(none, lambda z, y, x, c: (z, y, x - 1, c))),
+        move(out_1, pick(to_sibling, lambda z, y, x, c: (z, y, x - 1, c))),
         move(out_2, pick(lambda z, y, x, c: (z, y, x + 2, c), lambda z, y, x, c: (z, y, x + 1, 1 - c))),
-        move(out_3, pick(none, lambda z, y, x, c: (z, y, x - 1, 1 - c))),
-        move(sib, pick(to_sibling, none)),
+        move(out_3, pick(lambda z, y, x, c: (z, y, x, c), lambda z, y, x, c: (z, y, x - 1, 1 - c))),
     ]
 
     packed = kernel(
         pack_kernel, ((16, 192, 128), BF16), place, enc_a, enc_b, enc_c, *sibling([enc_sa, enc_sb, enc_sc]), name="pack"
     )
     parts = lax.all_to_all(packed, ("z", "y"), split_axis=0, concat_axis=0, tiled=True)
-    query_grad = kernel(decode_kernel, ((128, 1024), BF16), parts, decoder, name="decode")
-    weight_grad = kernel(join_kernel, ((2 * HALF, 256), BF16), place, kept, *got, name="join", flops=10**11)
+    shapes = (((2 * HALF, 256), BF16), ((8, 128), F32))
+    weight_grad, done = kernel(join_kernel, shapes, *got, name="join", flops=10**11)
+    query_grad = kernel(decode_kernel, ((128, 1024), BF16), parts, decoder, done, name="decode")
     return query_grad, weight_grad
 
 

time: 110 us -> 95.5 us (0.87)
  starting transfers between devices: 37 us -> 30 us
  local copies, waits for them, and re-layouts: 6.97 us -> 0.1 us
  Pallas kernels: 33.9 us -> 30.9 us
  waiting for transfers between devices: 29.3 us -> 31.4 us
    ppermute x26 -> x20, starting transfers between devices: 33.4 us -> 25.4 us  [move(): return lax.ppermute(array, AXES, pairs(target))]
    unnamed x16 -> x4, local copies, waits for them, and re-layouts: 6.88 us -> 0.01 us
    pallas_call x4 -> x6, Pallas kernels: 28.6 us -> 26.3 us  [the longest x4 26.3 us: chunk(): pl.pallas_call(functools.partial(chunk_kernel, [len(g) for g in groups],...]
    ppermute x26 -> x20, waiting for transfers between devices: 29.3 us -> 30.7 us  [move(): return lax.ppermute(array, AXES, pairs(target))]
    pallas_call x4 -> x5, Pallas kernels: 5.33 us -> 4.6 us  [kernel(): pl.pallas_call(body, in_specs=[pl.BlockSpec(memory_space=place(a)) for a...]
  transfers between devices with their start and end apart: 27 -> 21, of which waited for: 10 -> 11; matrix products, arithmetic and copies ran while one was open for 2% -> 2% of each run, Pallas kernels for 30% -> 31%
where the time goes in v3:
time: 95.5 us; the launch traced here: 95 us
  waiting for transfers between devices  31.4 us (33%)
  Pallas kernels  30.9 us (32%)
  starting transfers between devices  30 us (31%)
  other arithmetic  1.84 us (2%)
    ppermute x20, waiting for transfers between devices, move(): return lax.ppermute(array, AXES, pairs(target))  30.7 us
    pallas_call x4, Pallas kernels, chunk(): pl.pallas_call(functools.partial(chunk_kernel, [len(g) for g in groups],...  26.3 us
    ppermute x20, starting transfers between devices, move(): return lax.ppermute(array, AXES, pairs(target))  25.4 us
    all_to_all x1, starting transfers between devices, shards(): lax.all_to_all(packed, ('z', 'y'), split_axis=0, concat_axis=0, tiled=True)  4.68 us
    pallas_call x5, Pallas kernels, kernel(): pl.pallas_call(body, in_specs=[pl.BlockSpec(memory_space=place(a)) for a...  4.6 us
  transfers between devices with their start and end apart: 21, of which 11 were waited for; matrix products, arithmetic and copies ran while one was open for 2% of the time, Pallas kernels for 31%

profile of v3, /device:TPU:1, one launch (start us, length us, event | category | flops | bytes accessed | tf_op | source)
XLA Modules:
  0.0 95.0 jit_solution(11300692838440518434)
XLA Ops:
  0.6 1.5 %collective-permute-start.4 = (bf16[1024,1024]{1,0:T(8,128)(2,1)}, bf16[1024,1024]{1,0:T(8,128)(2,1)S(1)}, u32[]{:S(2)}, u32[]{:S(2)}) collective-permute-start(bf16[1024,1024]{1,0:T(8,128)(2,1)} %param.9), channel_id=1, source_target_pairs={{0,4},{1,0},{4,5},{5,1},{2,6},{3,2},{6,7},{7,3},{8,12},{9,8},{12,1... | collective-permute-start | bytes 6291464 | tf_op jit(solution)/shard_map/ppermute | solution.py:26
  2.1 0.1 pad.3.clone
  2.2 0.7 fusion
  2.9 1.1 %maximum_maximum_fusion.own_ref = bf16[144,1024]{1,0:T(8,128)(2,1)S(1)} fusion(bf16[1,1024]{1,0:T(2,128)(2,1)S(1)} %get-tuple-element.48, bf16[1,1024]{1,0:T(2,128)(2,1)S(1)} %get-tuple-element.49, bf16[128,1024]{1,0:T(8,128)(2,1)} %param.6, bf16[144]{0:T(256)(128)(2,1)S(1)} %pad.3.clone), kind=kLoop, calls=%fused_computation | loop fusion | flops 1179648 | bytes 561440 | tf_op jit(solution)/shard_map/concatenate | solution.py:270
  4.0 3.1 %collective-permute-start.2 = (bf16[144,1024]{1,0:T(8,128)(2,1)S(1)}, bf16[144,1024]{1,0:T(8,128)(2,1)S(1)}, u32[]{:S(2)}, u32[]{:S(2)}) collective-permute-start(bf16[144,1024]{1,0:T(8,128)(2,1)S(1)} %maximum_maximum_fusion.own_ref), channel_id=1, source_target_pairs={{0,64},{1,17},{4,68},{5,21},{2,66},{3,19},{6,70},{7,23},{8,72},{9,... | collective-permute-start | bytes 884744 | tf_op jit(solution)/shard_map/ppermute | solution.py:26
  7.1 0.8 collective-permute-start.1
  7.8 0.7 collective-permute-start
  8.5 0.1 pad_add_fusion.place.refs_0_
  8.6 0.0 copy-start.1
  8.6 2.9 %collective-permute-done.2.far_ref = bf16[144,1024]{1,0:T(8,128)(2,1)S(1)} collective-permute-done((bf16[144,1024]{1,0:T(8,128)(2,1)S(1)}, bf16[144,1024]{1,0:T(8,128)(2,1)S(1)}, u32[]{:S(2)}, u32[]{:S(2)}) %collective-permute-start.2) | collective-permute-done | bytes 294944 | tf_op jit(solution)/shard_map/ppermute | solution.py:26
  11.5 3.6 %collective-permute-done.1.ahead_ref = bf16[144,1024]{1,0:T(8,128)(2,1)S(1)} collective-permute-done((bf16[144,1024]{1,0:T(8,128)(2,1)S(1)}, bf16[144,1024]{1,0:T(8,128)(2,1)S(1)}, u32[]{:S(2)}, u32[]{:S(2)}) %collective-permute-start.1) | collective-permute-done | bytes 294944 | tf_op jit(solution)/shard_map/ppermute | solution.py:26
  15.1 0.0 collective-permute-done.back_ref
  15.1 0.6 row.1.refs_1_
  15.7 3.4 %collective-permute-start.3 = (bf16[528,1024]{1,0:T(8,128)(2,1)S(1)}, bf16[528,1024]{1,0:T(8,128)(2,1)S(1)}, u32[]{:S(2)}, u32[]{:S(2)}) collective-permute-start(bf16[528,1024]{1,0:T(8,128)(2,1)S(1)} %row.1.refs_1_), channel_id=1, source_target_pairs={{0,1},{1,0},{4,5},{5,4},{2,3},{3,2},{6,7},{7,6},{8,9},{9,8},{12,13... | collective-permute-start | bytes 3244040 | tf_op jit(solution)/shard_map/ppermute | solution.py:26
  19.2 2.3 %collective-permute-start.6 = (bf16[528,1024]{1,0:T(8,128)(2,1)S(1)}, bf16[528,1024]{1,0:T(8,128)(2,1)S(1)}, u32[]{:S(2)}, u32[]{:S(2)}) collective-permute-start(bf16[528,1024]{1,0:T(8,128)(2,1)S(1)} %row.1.refs_1_), channel_id=1, source_target_pairs={{0,24},{1,97},{4,28},{5,101},{2,26},{3,99},{6,30},{7,103},{8,0},{9... | collective-permute-start | bytes 3244040 | tf_op jit(solution)/shard_map/ppermute | solution.py:26
  21.5 0.0 collective-permute-start.5
  21.5 0.0 collective-permute-done.3.refs_2_
  21.5 5.2 %collective-permute-done.4.refs_3_.refs_5_ = bf16[1024,1024]{1,0:T(8,128)(2,1)S(1)} collective-permute-done((bf16[1024,1024]{1,0:T(8,128)(2,1)}, bf16[1024,1024]{1,0:T(8,128)(2,1)S(1)}, u32[]{:S(2)}, u32[]{:S(2)}) %collective-permute-start.4) | collective-permute-done | bytes 2097184 | tf_op jit(solution)/shard_map/ppermute | solution.py:26
  26.7 0.0 copy-done.1
  26.7 6.7 %chunk.4 = (f32[192,512]{1,0:T(8,128)S(1)}, f32[192,512]{1,0:T(8,128)S(1)}, bf16[384,1024]{1,0:T(8,128)(2,1)S(1)}, f32[4,1024,256]{2,1,0:T(8,128)S(1)}) custom-call(s32[4]{0:T(128)S(1)} %pad_add_fusion.place.refs_0_, bf16[528,1024]{1,0:T(8,128)(2,1)S(1)} %row.1.refs_1_, bf16[528,1024]{1,0:T(8,128)(2,1)S(1)} %collective-permute-done.3.refs_2_, ...), custom_call_target="tpu_custom_call" | custom-call | flops 5100273664 | bytes 1048576 | tf_op jit(solution)/shard_map/chunk/pallas_call | solution.py:177
  33.4 0.2 collective-permute-done.6.refs_1_
  33.6 3.4 %collective-permute-done.5.refs_0_ = bf16[528,1024]{1,0:T(8,128)(2,1)S(1)} collective-permute-done((bf16[528,1024]{1,0:T(8,128)(2,1)S(1)}, bf16[528,1024]{1,0:T(8,128)(2,1)S(1)}, u32[]{:S(2)}, u32[]{:S(2)}) %collective-permute-start.5) | collective-permute-done | bytes 1081376 | tf_op jit(solution)/shard_map/ppermute | solution.py:26
  37.0 1.6 %collective-permute-start.9 = (bf16[528,1024]{1,0:T(8,128)(2,1)S(1)}, bf16[528,1024]{1,0:T(8,128)(2,1)S(1)}, u32[]{:S(2)}, u32[]{:S(2)}) collective-permute-start(bf16[528,1024]{1,0:T(8,128)(2,1)S(1)} %get-tuple-element.26.refs_1_.back_ref), channel_id=1, source_target_pairs={{0,1},{1,0},{4,5},{5,4},{2,3},{3,2},{6,7},{7,6},{8,9},{9,8},{12,13... | collective-permute-start | bytes 3244040 | tf_op jit(solution)/shard_map/ppermute | solution.py:26
  38.6 0.0 collective-permute-start.10
  38.6 0.1 halves.1
  38.7 0.8 collective-permute-start.7
  39.5 2.0 %collective-permute-start.8 = (bf16[272,1024]{1,0:T(8,128)(2,1)S(1)}, bf16[272,1024]{1,0:T(8,128)(2,1)S(1)}, u32[]{:S(2)}, u32[]{:S(2)}) collective-permute-start(bf16[272,1024]{1,0:T(8,128)(2,1)S(1)} %get-tuple-element.31), channel_id=1, source_target_pairs={{0,24},{1,97},{4,28},{5,101},{2,26},{3,99},{6,30},{7,103},{8,0},{9... | collective-permute-start | bytes 1671176 | tf_op jit(solution)/shard_map/ppermute | solution.py:26
  41.4 6.2 %chunk.5 = (f32[192,1024]{1,0:T(8,128)S(1)}, f32[4,1024,256]{2,1,0:T(8,128)S(1)}) custom-call(s32[4]{0:T(128)S(1)} %pad_add_fusion.place.refs_0_, bf16[528,1024]{1,0:T(8,128)(2,1)S(1)} %get-tuple-element.26.refs_1_.back_ref, bf16[528,1024]{1,0:T(8,128)(2,1)S(1)} %get-tuple-element.27.refs_2_.ahead_ref, ...), custom_call_target="tpu_custom_call", output_to_operand_aliasing={{1}: (5, {})} | custom-call | flops 5100273664 | bytes 1048576 | tf_op jit(solution)/shard_map/chunk/pallas_call | solution.py:177
  47.6 0.0 collective-permute-done.9.refs_1_
  47.6 0.0 collective-permute-done.10.refs_2_
  47.6 6.2 %chunk.6 = (f32[192,1024]{1,0:T(8,128)S(1)}, f32[4,1024,256]{2,1,0:T(8,128)S(1)}) custom-call(s32[4]{0:T(128)S(1)} %pad_add_fusion.place.refs_0_, bf16[528,1024]{1,0:T(8,128)(2,1)S(1)} %collective-permute-done.9.refs_1_, bf16[528,1024]{1,0:T(8,128)(2,1)S(1)} %collective-permute-done.10.refs_2_, ...), custom_call_target="tpu_custom_call", output_to_operand_aliasing={{1}: (5, {})} | custom-call | flops 5100273664 | bytes 1048576 | tf_op jit(solution)/shard_map/chunk/pallas_call | solution.py:177
  53.8 0.0 collective-permute-done.7.refs_0_
  53.8 0.0 collective-permute-done.8.refs_1_
  53.9 1.1 %collective-permute-start.12 = (bf16[272,1024]{1,0:T(8,128)(2,1)S(1)}, bf16[272,1024]{1,0:T(8,128)(2,1)S(1)}, u32[]{:S(2)}, u32[]{:S(2)}) collective-permute-start(bf16[272,1024]{1,0:T(8,128)(2,1)S(1)} %get-tuple-element.35.refs_2_), channel_id=1, source_target_pairs={{0,1},{1,0},{4,5},{5,4},{2,3},{3,2},{6,7},{7,6},{8,9},{9,8},{12,13... | collective-permute-start | bytes 1671176 | tf_op jit(solution)/shard_map/ppermute | solution.py:26
  55.0 0.1 collective-permute-start.11
  55.1 0.4 collective-permute-start.14
  55.5 0.1 collective-permute-start.13
  55.6 1.7 %collective-permute-done.11.refs_3_ = bf16[256,1024]{1,0:T(8,128)(2,1)S(1)} collective-permute-done((bf16[256,1024]{1,0:T(8,128)(2,1)S(1)}, bf16[256,1024]{1,0:T(8,128)(2,1)S(1)}, u32[]{:S(2)}, u32[]{:S(2)}) %collective-permute-start.11) | collective-permute-done | bytes 524320 | tf_op jit(solution)/shard_map/ppermute | solution.py:26
  57.3 0.0 collective-permute-done.12.refs_4_
  57.3 7.2 %chunk.7 = (f32[192,512]{1,0:T(8,128)S(1)}, f32[192,512]{1,0:T(8,128)S(1)}, bf16[1024,256]{1,0:T(8,128)(2,1)}, bf16[1024,256]{1,0:T(8,128)(2,1)}, bf16[1024,256]{1,0:T(8,128)(2,1)}, /*index=5*/bf16[1024,256]{1,0:T(8,128)(2,1)}) custom-call(s32[4]{0:T(128)S(1)} %pad_add_fusion.place.refs_0_, bf16[256,1024]{1,0:T(8,128)(2,1)S(1)} %get-tuple-element.34.refs_1_, ...), custom_call_target="tpu_custom_call" | custom-call | flops 5100273664 | bytes 1048576 | tf_op jit(solution)/shard_map/chunk/pallas_call | solution.py:177
  64.6 0.1 collective-permute-start.16
  64.7 2.4 %collective-permute-start.17 = (bf16[1024,256]{1,0:T(8,128)(2,1)}, bf16[1024,256]{1,0:T(8,128)(2,1)S(1)}, u32[]{:S(2)}, u32[]{:S(2)}) collective-permute-start(bf16[1024,256]{1,0:T(8,128)(2,1)} %get-tuple-element.41), channel_id=1, source_target_pairs={{0,1},{1,7},{4,0},{5,4},{2,3},{3,5},{6,2},{7,6},{8,9},{9,15},{12,8... | collective-permute-start | bytes 1572872 | tf_op jit(solution)/shard_map/ppermute | solution.py:26
  67.1 2.1 %collective-permute-start.18 = (bf16[1024,256]{1,0:T(8,128)(2,1)}, bf16[1024,256]{1,0:T(8,128)(2,1)S(1)}, u32[]{:S(2)}, u32[]{:S(2)}) collective-permute-start(bf16[1024,256]{1,0:T(8,128)(2,1)} %get-tuple-element.42), channel_id=1, source_target_pairs={{0,2},{1,4},{4,3},{5,7},{2,0},{3,6},{6,1},{7,5},{8,10},{9,12},{12,... | collective-permute-start | bytes 1572872 | tf_op jit(solution)/shard_map/ppermute | solution.py:26
  69.2 0.0 collective-permute-done.13.refs_3_
  69.2 2.8 %collective-permute-start.19 = (bf16[1024,256]{1,0:T(8,128)(2,1)}, bf16[1024,256]{1,0:T(8,128)(2,1)S(1)}, u32[]{:S(2)}, u32[]{:S(2)}) collective-permute-start(bf16[1024,256]{1,0:T(8,128)(2,1)} %get-tuple-element.43), channel_id=1, source_target_pairs={{0,0},{1,6},{4,1},{5,5},{2,2},{3,4},{6,3},{7,7},{8,8},{9,14},{12,9... | collective-permute-start | bytes 1572872 | tf_op jit(solution)/shard_map/ppermute | solution.py:26
  71.9 0.0 collective-permute-done.14.refs_4_
  72.0 0.1 collective-permute-start.15
  72.1 1.7 %collective-permute-done.15.refs_5_ = f32[192,512]{1,0:T(8,128)S(1)} collective-permute-done((f32[192,512]{1,0:T(8,128)S(1)}, f32[192,512]{1,0:T(8,128)S(1)}, u32[]{:S(2)}, u32[]{:S(2)}) %collective-permute-start.15) | collective-permute-done | bytes 393248 | tf_op jit(solution)/shard_map/ppermute | solution.py:26
  73.8 1.6 %pack.1 = bf16[16,192,128]{2,1,0:T(8,128)(2,1)} custom-call(s32[4]{0:T(128)S(1)} %pad_add_fusion.place.refs_0_, f32[192,512]{1,0:T(8,128)S(1)} %get-tuple-element.24.refs_0_, f32[192,1024]{1,0:T(8,128)S(1)} %get-tuple-element.29.refs_1_, f32[192,512]{1,0:T(8,128)S(1)} %get-tuple-element.37.refs_2_, f32[192,512]{1,0:T(8,128)S(1)} %collective-permute-done.13.refs_3_, ...), custom_call_target="tpu_custom_call" | custom-call | flops 1000000 | bytes 1024 | tf_op jit(solution)/shard_map/pack/pallas_call | solution.py:235
  75.4 4.7 %all-to-all-start = ((bf16[16,192,128]{2,1,0:T(8,128)(2,1)}), bf16[16,192,128]{2,1,0:T(8,128)(2,1)S(1)}, u32[]{:S(2)}, u32[]{:S(2)}) async-start(bf16[16,192,128]{2,1,0:T(8,128)(2,1)} %pack.1), calls=%async_computation | async-start | bytes 1572864 | tf_op jit(solution)/shard_map/all_to_all | solution.py:306
  80.1 0.0 copy-start
  80.1 0.5 collective-permute-done.16.refs_0_
  80.6 0.4 collective-permute-done.17.refs_1_
  81.1 11.1 %collective-permute-done.18.refs_2_ = bf16[1024,256]{1,0:T(8,128)(2,1)S(1)} collective-permute-done((bf16[1024,256]{1,0:T(8,128)(2,1)}, bf16[1024,256]{1,0:T(8,128)(2,1)S(1)}, u32[]{:S(2)}, u32[]{:S(2)}) %collective-permute-start.18) | collective-permute-done | bytes 524320 | tf_op jit(solution)/shard_map/ppermute | solution.py:26
  92.1 0.0 collective-permute-done.19.refs_3_
  92.1 1.1 %join.1 = (bf16[1024,256]{1,0:T(8,128)(2,1)}, f32[8,128]{1,0:T(8,128)S(1)}) custom-call(bf16[1024,256]{1,0:T(8,128)(2,1)S(1)} %collective-permute-done.16.refs_0_, bf16[1024,256]{1,0:T(8,128)(2,1)S(1)} %collective-permute-done.17.refs_1_, bf16[1024,256]{1,0:T(8,128)(2,1)S(1)} %collective-permute-done.18.refs_2_, ...), custom_call_target="tpu_custom_call" | custom-call | flops 99999997952 | bytes 1024 | tf_op jit(solution)/shard_map/join/pallas_call | solution.py:235
  93.2 0.7 all-to-all-done.parts_ref
  93.8 0.0 copy-done
  93.8 1.2 %decode.1 = bf16[128,1024]{1,0:T(8,128)(2,1)} custom-call(bf16[16,192,128]{2,1,0:T(8,128)(2,1)S(1)} %all-to-all-done.parts_ref, bf16[192,1024]{1,0:T(8,128)(2,1)S(1)} %copy-done, f32[8,128]{1,0:T(8,128)S(1)} %get-tuple-element.44.after_ref), custom_call_target="tpu_custom_call" | custom-call | flops 1000000 | bytes 1024 | tf_op jit(solution)/shard_map/decode/pallas_call | solution.py:235
  (4 shorter events, 0.0 us)
Async XLA Ops:
  0.6 26.0 %collective-permute-start.4 = (bf16[1024,1024]{1,0:T(8,128)(2,1)}, bf16[1024,1024]{1,0:T(8,128)(2,1)S(1)}, u32[]{:S(2)}, u32[]{:S(2)}) collective-permute-start(bf16[1024,1024]{1,0:T(8,128)(2,1)} %param.9), channel_id=1, source_target_pairs={{0,4},{1,0},{4,5},{5,1},{2,6},{3,2},{6,7},{7,3},{8,12},{9,8},{12,1... | collective-permute-start | bytes 6291464 | tf_op jit(solution)/shard_map/ppermute | solution.py:26
  4.0 7.5 %collective-permute-start.2 = (bf16[144,1024]{1,0:T(8,128)(2,1)S(1)}, bf16[144,1024]{1,0:T(8,128)(2,1)S(1)}, u32[]{:S(2)}, u32[]{:S(2)}) collective-permute-start(bf16[144,1024]{1,0:T(8,128)(2,1)S(1)} %maximum_maximum_fusion.own_ref), channel_id=1, source_target_pairs={{0,64},{1,17},{4,68},{5,21},{2,66},{3,19},{6,70},{7,23},{8,72},{9,... | collective-permute-start | bytes 884744 | tf_op jit(solution)/shard_map/ppermute | solution.py:26
  7.1 8.0 %collective-permute-start.1 = (bf16[144,1024]{1,0:T(8,128)(2,1)S(1)}, bf16[144,1024]{1,0:T(8,128)(2,1)S(1)}, u32[]{:S(2)}, u32[]{:S(2)}) collective-permute-start(bf16[144,1024]{1,0:T(8,128)(2,1)S(1)} %maximum_maximum_fusion.own_ref), channel_id=1, source_target_pairs={{0,96},{1,25},{4,100},{5,29},{2,98},{3,27},{6,102},{7,31},{8,104},... | collective-permute-start | bytes 884744 | tf_op jit(solution)/shard_map/ppermute | solution.py:26
  7.8 7.2 %collective-permute-start = (bf16[144,1024]{1,0:T(8,128)(2,1)S(1)}, bf16[144,1024]{1,0:T(8,128)(2,1)S(1)}, u32[]{:S(2)}, u32[]{:S(2)}) collective-permute-start(bf16[144,1024]{1,0:T(8,128)(2,1)S(1)} %maximum_maximum_fusion.own_ref), channel_id=1, source_target_pairs={{0,32},{1,9},{4,36},{5,13},{2,34},{3,11},{6,38},{7,15},{8,40},{9,1... | collective-permute-start | bytes 884744 | tf_op jit(solution)/shard_map/ppermute | solution.py:26
  8.6 18.1 %copy-start.1 = (bf16[1024,192]{0,1:T(8,128)(2,1)S(1)}, bf16[1024,192]{0,1:T(8,128)(2,1)}, u32[]{:S(2)}) copy-start(bf16[1024,192]{0,1:T(8,128)(2,1)} %param.10) | copy-start | bytes 1179652
  15.7 5.8 %collective-permute-start.3 = (bf16[528,1024]{1,0:T(8,128)(2,1)S(1)}, bf16[528,1024]{1,0:T(8,128)(2,1)S(1)}, u32[]{:S(2)}, u32[]{:S(2)}) collective-permute-start(bf16[528,1024]{1,0:T(8,128)(2,1)S(1)} %row.1.refs_1_), channel_id=1, source_target_pairs={{0,1},{1,0},{4,5},{5,4},{2,3},{3,2},{6,7},{7,6},{8,9},{9,8},{12,13... | collective-permute-start | bytes 3244040 | tf_op jit(solution)/shard_map/ppermute | solution.py:26
  19.2 14.4 %collective-permute-start.6 = (bf16[528,1024]{1,0:T(8,128)(2,1)S(1)}, bf16[528,1024]{1,0:T(8,128)(2,1)S(1)}, u32[]{:S(2)}, u32[]{:S(2)}) collective-permute-start(bf16[528,1024]{1,0:T(8,128)(2,1)S(1)} %row.1.refs_1_), channel_id=1, source_target_pairs={{0,24},{1,97},{4,28},{5,101},{2,26},{3,99},{6,30},{7,103},{8,0},{9... | collective-permute-start | bytes 3244040 | tf_op jit(solution)/shard_map/ppermute | solution.py:26
  21.5 15.5 %collective-permute-start.5 = (bf16[528,1024]{1,0:T(8,128)(2,1)S(1)}, bf16[528,1024]{1,0:T(8,128)(2,1)S(1)}, u32[]{:S(2)}, u32[]{:S(2)}) collective-permute-start(bf16[528,1024]{1,0:T(8,128)(2,1)S(1)} %row.1.refs_1_), channel_id=1, source_target_pairs={{0,8},{1,33},{4,12},{5,37},{2,10},{3,35},{6,14},{7,39},{8,16},{9,4... | collective-permute-start | bytes 3244040 | tf_op jit(solution)/shard_map/ppermute | solution.py:26
  37.0 10.6 %collective-permute-start.9 = (bf16[528,1024]{1,0:T(8,128)(2,1)S(1)}, bf16[528,1024]{1,0:T(8,128)(2,1)S(1)}, u32[]{:S(2)}, u32[]{:S(2)}) collective-permute-start(bf16[528,1024]{1,0:T(8,128)(2,1)S(1)} %get-tuple-element.26.refs_1_.back_ref), channel_id=1, source_target_pairs={{0,1},{1,0},{4,5},{5,4},{2,3},{3,2},{6,7},{7,6},{8,9},{9,8},{12,13... | collective-permute-start | bytes 3244040 | tf_op jit(solution)/shard_map/ppermute | solution.py:26
  38.6 9.0 %collective-permute-start.10 = (bf16[528,1024]{1,0:T(8,128)(2,1)S(1)}, bf16[528,1024]{1,0:T(8,128)(2,1)S(1)}, u32[]{:S(2)}, u32[]{:S(2)}) collective-permute-start(bf16[528,1024]{1,0:T(8,128)(2,1)S(1)} %get-tuple-element.27.refs_2_.ahead_ref), channel_id=1, source_target_pairs={{0,1},{1,0},{4,5},{5,4},{2,3},{3,2},{6,7},{7,6},{8,9},{9,8},{12,13... | collective-permute-start | bytes 3244040 | tf_op jit(solution)/shard_map/ppermute | solution.py:26
  38.7 15.1 %collective-permute-start.7 = (bf16[256,1024]{1,0:T(8,128)(2,1)S(1)}, bf16[256,1024]{1,0:T(8,128)(2,1)S(1)}, u32[]{:S(2)}, u32[]{:S(2)}) collective-permute-start(bf16[256,1024]{1,0:T(8,128)(2,1)S(1)} %get-tuple-element.30), channel_id=1, source_target_pairs={{0,8},{1,33},{4,12},{5,37},{2,10},{3,35},{6,14},{7,39},{8,16},{9,4... | collective-permute-start | bytes 1572872 | tf_op jit(solution)/shard_map/ppermute | solution.py:26
  39.5 14.4 %collective-permute-start.8 = (bf16[272,1024]{1,0:T(8,128)(2,1)S(1)}, bf16[272,1024]{1,0:T(8,128)(2,1)S(1)}, u32[]{:S(2)}, u32[]{:S(2)}) collective-permute-start(bf16[272,1024]{1,0:T(8,128)(2,1)S(1)} %get-tuple-element.31), channel_id=1, source_target_pairs={{0,24},{1,97},{4,28},{5,101},{2,26},{3,99},{6,30},{7,103},{8,0},{9... | collective-permute-start | bytes 1671176 | tf_op jit(solution)/shard_map/ppermute | solution.py:26
  53.9 3.5 %collective-permute-start.12 = (bf16[272,1024]{1,0:T(8,128)(2,1)S(1)}, bf16[272,1024]{1,0:T(8,128)(2,1)S(1)}, u32[]{:S(2)}, u32[]{:S(2)}) collective-permute-start(bf16[272,1024]{1,0:T(8,128)(2,1)S(1)} %get-tuple-element.35.refs_2_), channel_id=1, source_target_pairs={{0,1},{1,0},{4,5},{5,4},{2,3},{3,2},{6,7},{7,6},{8,9},{9,8},{12,13... | collective-permute-start | bytes 1671176 | tf_op jit(solution)/shard_map/ppermute | solution.py:26
  55.0 2.3 %collective-permute-start.11 = (bf16[256,1024]{1,0:T(8,128)(2,1)S(1)}, bf16[256,1024]{1,0:T(8,128)(2,1)S(1)}, u32[]{:S(2)}, u32[]{:S(2)}) collective-permute-start(bf16[256,1024]{1,0:T(8,128)(2,1)S(1)} %get-tuple-element.34.refs_1_), channel_id=1, source_target_pairs={{0,1},{1,0},{4,5},{5,4},{2,3},{3,2},{6,7},{7,6},{8,9},{9,8},{12,13... | collective-permute-start | bytes 1572872 | tf_op jit(solution)/shard_map/ppermute | solution.py:26
  55.1 16.8 %collective-permute-start.14 = (f32[192,1024]{1,0:T(8,128)S(1)}, f32[192,1024]{1,0:T(8,128)S(1)}, u32[]{:S(2)}, u32[]{:S(2)}) collective-permute-start(f32[192,1024]{1,0:T(8,128)S(1)} %get-tuple-element.33.refs_2_), channel_id=1, source_target_pairs={{0,1},{1,0},{4,5},{5,4},{2,3},{3,2},{6,7},{7,6},{8,9},{9,8},{12,13... | collective-permute-start | bytes 2359304 | tf_op jit(solution)/shard_map/ppermute | solution.py:26
  55.5 13.6 %collective-permute-start.13 = (f32[192,512]{1,0:T(8,128)S(1)}, f32[192,512]{1,0:T(8,128)S(1)}, u32[]{:S(2)}, u32[]{:S(2)}) collective-permute-start(f32[192,512]{1,0:T(8,128)S(1)} %get-tuple-element.38), channel_id=1, source_target_pairs={{0,1},{1,0},{4,5},{5,4},{2,3},{3,2},{6,7},{7,6},{8,9},{9,8},{12,13... | collective-permute-start | bytes 1179656 | tf_op jit(solution)/shard_map/ppermute | solution.py:26
  64.6 16.0 %collective-permute-start.16 = (bf16[1024,256]{1,0:T(8,128)(2,1)}, bf16[1024,256]{1,0:T(8,128)(2,1)S(1)}, u32[]{:S(2)}, u32[]{:S(2)}) collective-permute-start(bf16[1024,256]{1,0:T(8,128)(2,1)} %get-tuple-element.40), channel_id=1, source_target_pairs={{0,3},{1,5},{4,2},{5,6},{2,1},{3,7},{6,0},{7,4},{8,11},{9,13},{12,... | collective-permute-start | bytes 1572872 | tf_op jit(solution)/shard_map/ppermute | solution.py:26
  64.7 16.4 %collective-permute-start.17 = (bf16[1024,256]{1,0:T(8,128)(2,1)}, bf16[1024,256]{1,0:T(8,128)(2,1)S(1)}, u32[]{:S(2)}, u32[]{:S(2)}) collective-permute-start(bf16[1024,256]{1,0:T(8,128)(2,1)} %get-tuple-element.41), channel_id=1, source_target_pairs={{0,1},{1,7},{4,0},{5,4},{2,3},{3,5},{6,2},{7,6},{8,9},{9,15},{12,8... | collective-permute-start | bytes 1572872 | tf_op jit(solution)/shard_map/ppermute | solution.py:26
  67.1 25.0 %collective-permute-start.18 = (bf16[1024,256]{1,0:T(8,128)(2,1)}, bf16[1024,256]{1,0:T(8,128)(2,1)S(1)}, u32[]{:S(2)}, u32[]{:S(2)}) collective-permute-start(bf16[1024,256]{1,0:T(8,128)(2,1)} %get-tuple-element.42), channel_id=1, source_target_pairs={{0,2},{1,4},{4,3},{5,7},{2,0},{3,6},{6,1},{7,5},{8,10},{9,12},{12,... | collective-permute-start | bytes 1572872 | tf_op jit(solution)/shard_map/ppermute | solution.py:26
  69.2 23.0 %collective-permute-start.19 = (bf16[1024,256]{1,0:T(8,128)(2,1)}, bf16[1024,256]{1,0:T(8,128)(2,1)S(1)}, u32[]{:S(2)}, u32[]{:S(2)}) collective-permute-start(bf16[1024,256]{1,0:T(8,128)(2,1)} %get-tuple-element.43), channel_id=1, source_target_pairs={{0,0},{1,6},{4,1},{5,5},{2,2},{3,4},{6,3},{7,7},{8,8},{9,14},{12,9... | collective-permute-start | bytes 1572872 | tf_op jit(solution)/shard_map/ppermute | solution.py:26
  72.0 1.8 %collective-permute-start.15 = (f32[192,512]{1,0:T(8,128)S(1)}, f32[192,512]{1,0:T(8,128)S(1)}, u32[]{:S(2)}, u32[]{:S(2)}) collective-permute-start(f32[192,512]{1,0:T(8,128)S(1)} %get-tuple-element.39), channel_id=1, source_target_pairs={{0,1},{1,0},{4,5},{5,4},{2,3},{3,2},{6,7},{7,6},{8,9},{9,8},{12,13... | collective-permute-start | bytes 1179656 | tf_op jit(solution)/shard_map/ppermute | solution.py:26
  75.4 18.4 %all-to-all-start = ((bf16[16,192,128]{2,1,0:T(8,128)(2,1)}), bf16[16,192,128]{2,1,0:T(8,128)(2,1)S(1)}, u32[]{:S(2)}, u32[]{:S(2)}) async-start(bf16[16,192,128]{2,1,0:T(8,128)(2,1)} %pack.1), calls=%async_computation | async-start | bytes 1572864 | tf_op jit(solution)/shard_map/all_to_all | solution.py:306
  80.1 13.7 %copy-start = (bf16[192,1024]{1,0:T(8,128)(2,1)S(1)}, bf16[192,1024]{1,0:T(8,128)(2,1)}, u32[]{:S(2)}) copy-start(bf16[192,1024]{1,0:T(8,128)(2,1)} %dec_ref.1) | copy-start | bytes 1179652

commit v4 on v3

--- a/solution.py
+++ b/solution.py
@@ -38,22 +38,18 @@
     return (z, y, x ^ 1, c) if c == x % 2 else (z, y, x, 1 - c)
 
 
-def row_kernel(place, own_ref, back_ref, ahead_ref, far_ref, row_ref):
+def rows_kernel(place, own_ref, back_ref, ahead_ref, far_ref, low_ref, high_ref):
     refs = (own_ref, back_ref, ahead_ref, far_ref)
     for i, ref in enumerate(refs):
-        row_ref[i * 128 : i * 128 + 128, :] = ref[:128, :]
+        half_ref = high_ref if i // 2 else low_ref
+        half_ref[i % 2 * 128 : i % 2 * 128 + 128, :] = ref[:128, :]
     row = lax.broadcasted_iota(I32, (TAIL, 1024), 0)
     tail = jnp.zeros((TAIL, 1024), F32)
     for i, ref in enumerate(refs):
         ids = ref[128:144, :].astype(F32)
         for digit in range(2):
             tail = jnp.where(row == 2 * i + digit, ids[digit : digit + 1, :], tail)
-    row_ref[512:, :] = tail.astype(BF16)
-
-
-def halves_kernel(back_ref, ahead_ref, low_ref, high_ref):
-    low_ref[...] = back_ref[:256, :]
-    high_ref[...] = ahead_ref[256:, :]
+    high_ref[256:, :] = tail.astype(BF16)
 
 
 def encode(w_ref, enc_ref, wet_ref):
@@ -89,32 +85,31 @@
     return 2 * away + column, 2 * (1 - away) + column, 2 * away + 1 - column, 2 * (1 - away) + 1 - column
 
 
-def chunk_kernel(parts, enc_at, first, last, scale, *refs):
+def chunk_kernel(enc_at, fresh, first, last, scale, *refs):
     n = len(enc_at)
-    n_q = sum(parts)
-    place, q_refs, refs = refs[0], refs[1 : 1 + n_q], refs[1 + n_q :]
+    place, q_refs, refs = refs[0], refs[1 : 1 + 2 * n], refs[1 + 2 * n :]
     z, y, x, core = (place[i] for i in range(4))
     base = ((z * 4 + y) * 2 + core) * 2 * HALF
     w_ref, enc_ref, refs = refs[0], refs[1], refs[2:]
     if not first:
         total_ref, refs = refs[0], refs[1:]
+    sums = sorted({out for out, _ in enc_at})
+    if not fresh:
+        refs = refs[len(sums) :]
     if last:
         refs, (narrow, out_sems) = refs[:-2], refs[-2:]
     outs, (q_all, grads, bits) = refs[:-3], refs[-3:]
-    n_enc = 1 + max(out for out, _ in enc_at)
-    encs, outs = outs[:n_enc], outs[n_enc:]
+    encs, outs = dict(zip(sums, outs)), outs[len(sums) :]
     if first:
         wet_ref, outs = outs[0], outs[1:]
         encode(w_ref, enc_ref, wet_ref)
     else:
         wet_ref = enc_ref
     for i in range(n):
-        bufs, q_refs = q_refs[: parts[i]], q_refs[parts[i] :]
-        size = 512 // parts[i]
-        for j, buf in enumerate(bufs):
-            at = 512 * i + size * j
-            q_all[at : at + size, :] = buf[:size, :]
-        tail = bufs[-1][size : size + TAIL, :].astype(F32).astype(I32)
+        low, high = q_refs[2 * i : 2 * i + 2]
+        q_all[512 * i : 512 * i + 256, :] = low[...]
+        q_all[512 * i + 256 : 512 * i + 512, :] = high[:256, :]
+        tail = high[256:, :].astype(F32).astype(I32)
         for b in range(4):
             lanes = slice(512 * i + 128 * b, 512 * i + 128 * b + 128)
             for w, word in enumerate(target_bits(tail, b, base)):
@@ -138,10 +133,6 @@
                 columns = slice(256 * c, 256 * c + 256)
                 old = 0.0 if first else total_ref[c, rows, :]
                 outs[0][c, rows, :] = old + part[:, columns]
-    encoded = jnp.dot(wet_ref[...], grads[...], preferred_element_type=F32)
-    encoded = encoded[:192] + encoded[192:]
-    for i, (out, column) in enumerate(enc_at):
-        encs[out][:, column : column + 512] = encoded[:, 512 * i : 512 * i + 512]
     if last:
         copies = []
         for o, c in enumerate(quarters(x, core)):
@@ -150,32 +141,39 @@
             narrow[o] = whole.astype(BF16)
             copies.append(pltpu.make_async_copy(narrow.at[o], outs[o], out_sems.at[o]))
             copies[-1].start()
+    encoded = jnp.dot(wet_ref[...], grads[...], preferred_element_type=F32)
+    encoded = encoded[:192] + encoded[192:]
+    for i, (out, column) in enumerate(enc_at):
+        encs[out][:, column : column + 512] = encoded[:, 512 * i : 512 * i + 512]
+    if last:
         for copy in copies:
             copy.wait()
 
 
-def chunk(place, groups, enc_at, w, enc, total, last, scale):
-    first = total is None
+def chunk(place, groups, enc_at, w, enc, total, sums, last, scale):
+    first, fresh = total is None, sums is None
     vmem = pl.BlockSpec(memory_space=pltpu.VMEM)
-    widths = [0] * (1 + max(out for out, _ in enc_at))
-    for out, column in enc_at:
-        widths[out] = max(widths[out], column + 512)
+    labels, n = 2 * HALF, 512 * len(enc_at)
+    named = sorted({out for out, _ in enc_at})
     args = [place, *sum(groups, []), w, enc] + ([] if first else [total])
-    labels = 2 * HALF
-    shapes = [jax.ShapeDtypeStruct((192, n), F32) for n in widths]
+    shapes = [jax.ShapeDtypeStruct((192, 2048), F32) for _ in named]
+    aliases = {} if fresh else {len(args) + i: i for i in range(len(named))}
     if first:
         shapes.append(jax.ShapeDtypeStruct((384, labels), BF16))
     if last:
-        shapes += [jax.ShapeDtypeStruct((labels, 256), d) for d in (BF16,) * 4]
+        shapes += [jax.ShapeDtypeStruct((labels, 256), BF16)] * 4
     else:
+        if not first:
+            aliases[len(args) - 1] = len(shapes)
         shapes.append(jax.ShapeDtypeStruct((4, labels, 256), F32))
-    n = 512 * len(enc_at)
+    if not fresh:
+        args += [sums[i] for i in named]
     out_specs, scratch = [vmem] * len(shapes), []
     if last:
         out_specs[-4:] = [pl.BlockSpec(memory_space=pltpu.HBM)] * 4
         scratch = [pltpu.VMEM((4, labels, 256), BF16), pltpu.SemaphoreType.DMA((4,))]
-    return pl.pallas_call(
-        functools.partial(chunk_kernel, [len(g) for g in groups], enc_at, first, last, scale),
+    out = pl.pallas_call(
+        functools.partial(chunk_kernel, enc_at, fresh, first, last, scale),
         in_specs=[pl.BlockSpec(memory_space=pltpu.SMEM)] + [vmem] * (len(args) - 1),
         out_specs=out_specs,
         out_shape=shapes,
@@ -185,26 +183,26 @@
             pltpu.VMEM((4, 8, n), I32),
             *scratch,
         ],
-        input_output_aliases={} if first or last else {len(args) - 1: len(shapes) - 1},
+        input_output_aliases=aliases,
         compiler_params=pltpu.CompilerParams(vmem_limit_bytes=VMEM_LIMIT),
         cost_estimate=pl.CostEstimate(
             flops=2 * n * labels * (2 * 1024 + 384), bytes_accessed=2**20, transcendentals=0
         ),
         name="chunk",
     )(*args)
+    new = dict(enumerate([None, None] if fresh else sums)) | dict(zip(named, out))
+    return ([new[0], new[1]], *out[len(named) :])
 
 
 def pack_kernel(place, *refs):
-    own, sib, out = refs[:3], refs[3:6], refs[6]
+    own, sib, out = refs
     z, y, core = place[0], place[1], place[3]
     first, second = jnp.where(core == 0, z, y), jnp.where(core == 0, y, z)
-    at = [(i, j) for i in OFFSETS for j in OFFSETS]
-    for a, b in zip(own, sib):
-        value = (a[...] + b[...]).astype(BF16)
-        for block in range(value.shape[1] // 128):
-            i, j = at.pop(0)
-            j, i = lax.rem(first + j, 4), lax.rem(second + i, 4)
-            out[jnp.where(core == 0, j * 4 + i, i * 4 + j)] = value[:, block * 128 : block * 128 + 128]
+    for part in range(4):
+        for block in range(4):
+            lanes = slice(512 * part + 128 * block, 512 * part + 128 * block + 128)
+            j, i = lax.rem(first + OFFSETS[block], 4), lax.rem(second + OFFSETS[part], 4)
+            out[jnp.where(core == 0, j * 4 + i, i * 4 + j)] = (own[:, lanes] + sib[:, lanes]).astype(BF16)
 
 
 def decode_kernel(parts_ref, dec_ref, after_ref, out_ref):
@@ -267,42 +265,42 @@
     slot = lax.broadcasted_iota(I32, (8, 128), 0)
     ids = jnp.where(slot < label_counts[None, :], label_ids.T, 255 * 256).reshape(1, 1024)
     tail = jnp.concatenate([ids >> 8, ids & 255, jnp.zeros((TAIL - 2, 1024), I32)], axis=0)
-    own = jnp.concatenate([queries, tail.astype(BF16)], axis=0)
+    block = jnp.concatenate([queries, tail.astype(BF16)], axis=0)
 
     place = jnp.stack([z, y, 2 * xh + xl, core]).astype(I32)
     w = move(weights, to_user)
-    back, ahead, far = (move(own, hop(0, step)) for step in (1, -1, 2))
-    row = kernel(row_kernel, ((512 + TAIL, 1024), BF16), place, own, back, ahead, far, name="row")
-    row_back, row_ahead = move(row, hop(1, 1)), move(row, hop(1, -1))
-    sibling = lambda bufs: [move(b, to_sibling) for b in bufs]
-    apart, joined = ((0, 0), (1, 0)), ((0, 0), (0, 512))
-    enc_a, enc_sa, wet, total = chunk(
-        place, [[row], sibling([row])], apart, w, encoder.T, None, False, scale
+    back, ahead, far = (move(block, hop(0, step)) for step in (1, -1, 2))
+    half_shapes = (((256, 1024), BF16), ((256 + TAIL, 1024), BF16))
+    low, high = kernel(rows_kernel, half_shapes, place, block, back, ahead, far, name="rows")
+    low_back, high_ahead = move(low, hop(1, 1)), move(high, hop(1, -1))
+    high_back, low_ahead = move(high, hop(1, 1)), move(low, hop(1, -1))
+    sibling = lambda array: move(array, to_sibling)
+    row, own, sib = [low, high], 0, 1
+    sums, wet, total = chunk(
+        place, [row, [sibling(low), sibling(high)]], ((own, 0), (sib, 0)), w, encoder.T, None, None, False, scale
     )
-    half_shapes = (((256, 1024), BF16), ((256 + TAIL, 1024), BF16))
-    row_back, row_ahead = after([row_back, row_ahead], wet)
-    low, high = kernel(halves_kernel, half_shapes, row_back, row_ahead, name="halves")
-    far = [move(low, hop(1, 1)), move(high, hop(1, -1))]
-    enc_b, total = chunk(place, [[row_back], [row_ahead]], joined, w, wet, total, False, scale)
-    enc_sb, total = chunk(
-        place, [sibling([row_back]), sibling([row_ahead])], joined, w, wet, total, False, scale
-    )
-    far = after(far, enc_sb)
-    enc_c, enc_sc, out_0, out_1, out_2, out_3 = chunk(
-        place, [far, sibling(far)], apart, w, wet, total, True, scale
-    )
+    low_back, high_ahead = after([low_back, high_ahead], wet)
+    far = [move(low_back, hop(1, 1)), move(high_ahead, hop(1, -1))]
+    early = [sibling(low_back), sibling(high_ahead)]
+    high_back, low_ahead = after([high_back, low_ahead], *early)
+    late = [sibling(high_back), sibling(low_ahead)]
+    back, ahead = [low_back, high_back], [low_ahead, high_ahead]
+    sums, total = chunk(place, [back, ahead], ((own, 512), (own, 1024)), w, wet, total, sums, False, scale)
+    far = after(far, sums[own])
+    back, ahead = [early[0], late[0]], [late[1], early[1]]
+    sums, total = chunk(place, [back, ahead], ((sib, 512), (sib, 1024)), w, wet, total, sums, False, scale)
+    far_sib = [sibling(f) for f in far]
+    sums, *outs = chunk(place, [far, far_sib], ((own, 1536), (sib, 1536)), w, wet, total, sums, True, scale)
 
     pick = lambda same, other: lambda z, y, x, c: same(z, y, x, c) if c == x % 2 else other(z, y, x, c)
     got = [
-        move(out_0, pick(lambda z, y, x, c: (z, y, x + 2, 1 - c), lambda z, y, x, c: (z, y, x + 1, c))),
-        move(out_1, pick(to_sibling, lambda z, y, x, c: (z, y, x - 1, c))),
-        move(out_2, pick(lambda z, y, x, c: (z, y, x + 2, c), lambda z, y, x, c: (z, y, x + 1, 1 - c))),
-        move(out_3, pick(lambda z, y, x, c: (z, y, x, c), lambda z, y, x, c: (z, y, x - 1, 1 - c))),
+        move(outs[0], pick(lambda z, y, x, c: (z, y, x + 2, 1 - c), lambda z, y, x, c: (z, y, x + 1, c))),
+        move(outs[1], pick(to_sibling, lambda z, y, x, c: (z, y, x - 1, c))),
+        move(outs[2], pick(lambda z, y, x, c: (z, y, x + 2, c), lambda z, y, x, c: (z, y, x + 1, 1 - c))),
+        move(outs[3], pick(lambda z, y, x, c: (z, y, x, c), lambda z, y, x, c: (z, y, x - 1, 1 - c))),
     ]
 
-    packed = kernel(
-        pack_kernel, ((16, 192, 128), BF16), place, enc_a, enc_b, enc_c, *sibling([enc_sa, enc_sb, enc_sc]), name="pack"
-    )
+    packed = kernel(pack_kernel, ((16, 192, 128), BF16), place, sums[own], sibling(sums[sib]), name="pack")
     parts = lax.all_to_all(packed, ("z", "y"), split_axis=0, concat_axis=0, tiled=True)
     shapes = (((2 * HALF, 256), BF16), ((8, 128), F32))
     weight_grad, done = kernel(join_kernel, shapes, *got, name="join", flops=10**11)

time: 95.5 us -> 93.6 us (0.980)
  waiting for transfers between devices: 31.4 us -> 24.4 us
  starting transfers between devices: 30 us -> 34.9 us
  local copies, waits for them, and re-layouts: 0.1 us -> 1.09 us
    ppermute x20 -> x23, waiting for transfers between devices: 30.7 us -> 24 us  [move(): return lax.ppermute(array, AXES, pairs(target))]
    ppermute x20 -> x23, starting transfers between devices: 25.4 us -> 29.8 us  [move(): return lax.ppermute(array, AXES, pairs(target))]
    unnamed x4, local copies, waits for them, and re-layouts: 0.01 us -> 1 us
    pallas_call x5 -> x4, Pallas kernels: 4.6 us -> 4.51 us  [kernel(): pl.pallas_call(body, in_specs=[pl.BlockSpec(memory_space=place(a)) for a...]
  transfers between devices with their start and end apart: 21 -> 24, of which waited for: 11 -> 10; matrix products, arithmetic and copies ran while one was open for 2% -> 2% of each run, Pallas kernels for 31% -> 24%
where the time goes in v4:
time: 93.6 us; the launch traced here: 93.2 us
  starting transfers between devices  34.9 us (37%)
  Pallas kernels  30.2 us (32%)
  waiting for transfers between devices  24.4 us (26%)
  other arithmetic  1.84 us (2%)
  local copies, waits for them, and re-layouts  1.09 us (1%)
    ppermute x23, starting transfers between devices, move(): return lax.ppermute(array, AXES, pairs(target))  29.8 us
    pallas_call x4, Pallas kernels, chunk(): pl.pallas_call(functools.partial(chunk_kernel, enc_at, fresh, first, last...  25.7 us
    ppermute x23, waiting for transfers between devices, move(): return lax.ppermute(array, AXES, pairs(target))  24 us
    all_to_all x1, starting transfers between devices, shards(): lax.all_to_all(packed, ('z', 'y'), split_axis=0, concat_axis=0, tiled=True)  5.14 us
    pallas_call x4, Pallas kernels, kernel(): pl.pallas_call(body, in_specs=[pl.BlockSpec(memory_space=place(a)) for a...  4.51 us
  transfers between devices with their start and end apart: 24, of which 10 were waited for; matrix products, arithmetic and copies ran while one was open for 2% of the time, Pallas kernels for 24%

profile of v4, /device:TPU:1, one launch (start us, length us, event | category | flops | bytes accessed | tf_op | source)
XLA Modules:
  0.0 93.2 jit_solution(16309937293943248185)
XLA Ops:
  0.6 1.5 %collective-permute-start.7 = (bf16[1024,1024]{1,0:T(8,128)(2,1)}, bf16[1024,1024]{1,0:T(8,128)(2,1)S(1)}, u32[]{:S(2)}, u32[]{:S(2)}) collective-permute-start(bf16[1024,1024]{1,0:T(8,128)(2,1)} %param.9), channel_id=1, source_target_pairs={{0,4},{1,0},{4,5},{5,1},{2,6},{3,2},{6,7},{7,3},{8,12},{9,8},{12,1... | collective-permute-start | bytes 6291464 | tf_op jit(solution)/shard_map/ppermute | solution.py:26
  2.1 0.1 pad.3.clone
  2.2 0.7 fusion
  2.9 1.1 %maximum_maximum_fusion.own_ref = bf16[144,1024]{1,0:T(8,128)(2,1)S(1)} fusion(bf16[1,1024]{1,0:T(2,128)(2,1)S(1)} %get-tuple-element.52, bf16[1,1024]{1,0:T(2,128)(2,1)S(1)} %get-tuple-element.53, bf16[128,1024]{1,0:T(8,128)(2,1)} %param.6, bf16[144]{0:T(256)(128)(2,1)S(1)} %pad.3.clone), kind=kLoop, calls=%fused_computation | loop fusion | flops 1179648 | bytes 561440 | tf_op jit(solution)/shard_map/concatenate | solution.py:268
  4.0 1.4 %collective-permute-start = (bf16[144,1024]{1,0:T(8,128)(2,1)S(1)}, bf16[144,1024]{1,0:T(8,128)(2,1)S(1)}, u32[]{:S(2)}, u32[]{:S(2)}) collective-permute-start(bf16[144,1024]{1,0:T(8,128)(2,1)S(1)} %maximum_maximum_fusion.own_ref), channel_id=1, source_target_pairs={{0,32},{1,9},{4,36},{5,13},{2,34},{3,11},{6,38},{7,15},{8,40},{9,1... | collective-permute-start | bytes 884744 | tf_op jit(solution)/shard_map/ppermute | solution.py:26
  5.4 1.5 %collective-permute-start.1 = (bf16[144,1024]{1,0:T(8,128)(2,1)S(1)}, bf16[144,1024]{1,0:T(8,128)(2,1)S(1)}, u32[]{:S(2)}, u32[]{:S(2)}) collective-permute-start(bf16[144,1024]{1,0:T(8,128)(2,1)S(1)} %maximum_maximum_fusion.own_ref), channel_id=1, source_target_pairs={{0,96},{1,25},{4,100},{5,29},{2,98},{3,27},{6,102},{7,31},{8,104},... | collective-permute-start | bytes 884744 | tf_op jit(solution)/shard_map/ppermute | solution.py:26
  7.0 1.6 %collective-permute-start.2 = (bf16[144,1024]{1,0:T(8,128)(2,1)S(1)}, bf16[144,1024]{1,0:T(8,128)(2,1)S(1)}, u32[]{:S(2)}, u32[]{:S(2)}) collective-permute-start(bf16[144,1024]{1,0:T(8,128)(2,1)S(1)} %maximum_maximum_fusion.own_ref), channel_id=1, source_target_pairs={{0,64},{1,17},{4,68},{5,21},{2,66},{3,19},{6,70},{7,23},{8,72},{9,... | collective-permute-start | bytes 884744 | tf_op jit(solution)/shard_map/ppermute | solution.py:26
  8.5 0.1 pad_add_fusion.place.refs_0_
  8.6 2.7 %collective-permute-done.back_ref = bf16[144,1024]{1,0:T(8,128)(2,1)S(1)} collective-permute-done((bf16[144,1024]{1,0:T(8,128)(2,1)S(1)}, bf16[144,1024]{1,0:T(8,128)(2,1)S(1)}, u32[]{:S(2)}, u32[]{:S(2)}) %collective-permute-start) | collective-permute-done | bytes 294944 | tf_op jit(solution)/shard_map/ppermute | solution.py:26
  11.3 2.5 %collective-permute-done.1.ahead_ref = bf16[144,1024]{1,0:T(8,128)(2,1)S(1)} collective-permute-done((bf16[144,1024]{1,0:T(8,128)(2,1)S(1)}, bf16[144,1024]{1,0:T(8,128)(2,1)S(1)}, u32[]{:S(2)}, u32[]{:S(2)}) %collective-permute-start.1) | collective-permute-done | bytes 294944 | tf_op jit(solution)/shard_map/ppermute | solution.py:26
  13.8 1.8 %collective-permute-done.2.far_ref = bf16[144,1024]{1,0:T(8,128)(2,1)S(1)} collective-permute-done((bf16[144,1024]{1,0:T(8,128)(2,1)S(1)}, bf16[144,1024]{1,0:T(8,128)(2,1)S(1)}, u32[]{:S(2)}, u32[]{:S(2)}) %collective-permute-start.2) | collective-permute-done | bytes 294944 | tf_op jit(solution)/shard_map/ppermute | solution.py:26
  15.6 0.6 rows.1
  16.3 3.4 %collective-permute-start.6 = (bf16[272,1024]{1,0:T(8,128)(2,1)S(1)}, bf16[272,1024]{1,0:T(8,128)(2,1)S(1)}, u32[]{:S(2)}, u32[]{:S(2)}) collective-permute-start(bf16[272,1024]{1,0:T(8,128)(2,1)S(1)} %get-tuple-element.27.refs_2_), channel_id=1, source_target_pairs={{0,1},{1,0},{4,5},{5,4},{2,3},{3,2},{6,7},{7,6},{8,9},{9,8},{12,13... | collective-permute-start | bytes 1671176 | tf_op jit(solution)/shard_map/ppermute | solution.py:26
  19.7 0.1 collective-permute-start.5
  19.8 1.6 %collective-permute-start.4 = (bf16[272,1024]{1,0:T(8,128)(2,1)S(1)}, bf16[272,1024]{1,0:T(8,128)(2,1)S(1)}, u32[]{:S(2)}, u32[]{:S(2)}) collective-permute-start(bf16[272,1024]{1,0:T(8,128)(2,1)S(1)} %get-tuple-element.27.refs_2_), channel_id=1, source_target_pairs={{0,24},{1,97},{4,28},{5,101},{2,26},{3,99},{6,30},{7,103},{8,0},{9... | collective-permute-start | bytes 1671176 | tf_op jit(solution)/shard_map/ppermute | solution.py:26
  21.4 0.0 collective-permute-start.3
  21.4 0.7 collective-permute-done.5.refs_3_
  22.0 1.1 %collective-permute-start.10 = (bf16[272,1024]{1,0:T(8,128)(2,1)S(1)}, bf16[272,1024]{1,0:T(8,128)(2,1)S(1)}, u32[]{:S(2)}, u32[]{:S(2)}) collective-permute-start(bf16[272,1024]{1,0:T(8,128)(2,1)S(1)} %get-tuple-element.27.refs_2_), channel_id=1, source_target_pairs={{0,8},{1,33},{4,12},{5,37},{2,10},{3,35},{6,14},{7,39},{8,16},{9,4... | collective-permute-start | bytes 1671176 | tf_op jit(solution)/shard_map/ppermute | solution.py:26
  23.2 0.0 collective-permute-done.6.refs_4_
  23.2 1.5 %collective-permute-start.11 = (bf16[256,1024]{1,0:T(8,128)(2,1)S(1)}, bf16[256,1024]{1,0:T(8,128)(2,1)S(1)}, u32[]{:S(2)}, u32[]{:S(2)}) collective-permute-start(bf16[256,1024]{1,0:T(8,128)(2,1)S(1)} %get-tuple-element.26.refs_1_), channel_id=1, source_target_pairs={{0,24},{1,97},{4,28},{5,101},{2,26},{3,99},{6,30},{7,103},{8,0},{9... | collective-permute-start | bytes 1572872 | tf_op jit(solution)/shard_map/ppermute | solution.py:26
  24.7 2.0 %collective-permute-done.7.refs_5_ = bf16[1024,1024]{1,0:T(8,128)(2,1)S(1)} collective-permute-done((bf16[1024,1024]{1,0:T(8,128)(2,1)}, bf16[1024,1024]{1,0:T(8,128)(2,1)S(1)}, u32[]{:S(2)}, u32[]{:S(2)}) %collective-permute-start.7) | collective-permute-done | bytes 2097184 | tf_op jit(solution)/shard_map/ppermute | solution.py:26
  26.7 0.0 copy-start.1
  26.7 1.0 %copy-done.1 = bf16[1024,192]{0,1:T(8,128)(2,1)S(1)} copy-done((bf16[1024,192]{0,1:T(8,128)(2,1)S(1)}, bf16[1024,192]{0,1:T(8,128)(2,1)}, u32[]{:S(2)}) %copy-start.1) | copy-done | bytes 393240
  27.7 6.7 %chunk.4 = (f32[192,2048]{1,0:T(8,128)S(1)}, f32[192,2048]{1,0:T(8,128)S(1)}, bf16[384,1024]{1,0:T(8,128)(2,1)S(1)}, f32[4,1024,256]{2,1,0:T(8,128)S(1)}) custom-call(s32[4]{0:T(128)S(1)} %pad_add_fusion.place.refs_0_, bf16[256,1024]{1,0:T(8,128)(2,1)S(1)} %get-tuple-element.26.refs_1_, bf16[272,1024]{1,0:T(8,128)(2,1)S(1)} %get-tuple-element.27.refs_2_, ...), custom_call_target="tpu_custom_call" | custom-call | flops 5100273664 | bytes 1048576 | tf_op jit(solution)/shard_map/chunk/pallas_call | solution.py:175
  34.4 0.0 collective-permute-done.3.refs_0_
  34.4 0.0 collective-permute-done.4.refs_1_
  34.4 1.0 %collective-permute-start.13 = (bf16[272,1024]{1,0:T(8,128)(2,1)S(1)}, bf16[272,1024]{1,0:T(8,128)(2,1)S(1)}, u32[]{:S(2)}, u32[]{:S(2)}) collective-permute-start(bf16[272,1024]{1,0:T(8,128)(2,1)S(1)} %get-tuple-element.30.refs_4_), channel_id=1, source_target_pairs={{0,1},{1,0},{4,5},{5,4},{2,3},{3,2},{6,7},{7,6},{8,9},{9,8},{12,13... | collective-permute-start | bytes 1671176 | tf_op jit(solution)/shard_map/ppermute | solution.py:26
  35.4 0.1 collective-permute-start.12
  35.5 3.7 %collective-permute-start.9 = (bf16[272,1024]{1,0:T(8,128)(2,1)S(1)}, bf16[272,1024]{1,0:T(8,128)(2,1)S(1)}, u32[]{:S(2)}, u32[]{:S(2)}) collective-permute-start(bf16[272,1024]{1,0:T(8,128)(2,1)S(1)} %get-tuple-element.30.refs_4_), channel_id=1, source_target_pairs={{0,24},{1,97},{4,28},{5,101},{2,26},{3,99},{6,30},{7,103},{8,0},{9... | collective-permute-start | bytes 1671176 | tf_op jit(solution)/shard_map/ppermute | solution.py:26
  39.2 0.0 collective-permute-done.11.refs_1_
  39.2 0.0 collective-permute-start.8
  39.2 0.0 collective-permute-done.10.refs_0_
  39.2 0.0 collective-permute-done.12.refs_2_.refs_1_
  39.2 0.0 collective-permute-done.13.refs_3_.refs_4_
  39.3 0.4 collective-permute-start.16
  39.7 0.3 collective-permute-start.17
  40.0 6.2 %chunk.5 = (f32[192,2048]{1,0:T(8,128)S(1)}, f32[4,1024,256]{2,1,0:T(8,128)S(1)}) custom-call(s32[4]{0:T(128)S(1)} %pad_add_fusion.place.refs_0_, bf16[256,1024]{1,0:T(8,128)(2,1)S(1)} %get-tuple-element.29.refs_1_, bf16[272,1024]{1,0:T(8,128)(2,1)S(1)} %get-tuple-element.31.refs_2_, ...), custom_call_target="tpu_custom_call", output_to_operand_aliasing={{0}: (8, {}), {1}: (7, {})} | custom-call | flops 5100273664 | bytes 1048576 | tf_op jit(solution)/shard_map/chunk/pallas_call | solution.py:175
  46.1 2.6 %collective-permute-done.8.refs_0_ = bf16[256,1024]{1,0:T(8,128)(2,1)S(1)} collective-permute-done((bf16[256,1024]{1,0:T(8,128)(2,1)S(1)}, bf16[256,1024]{1,0:T(8,128)(2,1)S(1)}, u32[]{:S(2)}, u32[]{:S(2)}) %collective-permute-start.8) | collective-permute-done | bytes 524320 | tf_op jit(solution)/shard_map/ppermute | solution.py:26
  48.8 0.0 collective-permute-done.9.refs_1_
  48.8 0.5 collective-permute-start.15
  49.3 0.1 collective-permute-start.14
  49.4 0.0 collective-permute-done.17.refs_3_
  49.4 0.0 collective-permute-done.16.refs_2_
  49.4 6.2 %chunk.6 = (f32[192,2048]{1,0:T(8,128)S(1)}, f32[4,1024,256]{2,1,0:T(8,128)S(1)}) custom-call(s32[4]{0:T(128)S(1)} %pad_add_fusion.place.refs_0_, bf16[256,1024]{1,0:T(8,128)(2,1)S(1)} %collective-permute-done.12.refs_2_.refs_1_, bf16[272,1024]{1,0:T(8,128)(2,1)S(1)} %collective-permute-done.16.refs_2_, ...), custom_call_target="tpu_custom_call", output_to_operand_aliasing={{0}: (8, {}), {1}: (7, {})} | custom-call | flops 5100273664 | bytes 1048576 | tf_op jit(solution)/shard_map/chunk/pallas_call | solution.py:175
  55.6 0.0 collective-permute-done.14.refs_3_
  55.6 0.0 collective-permute-done.15.refs_4_
  55.6 6.6 %chunk.7 = (f32[192,2048]{1,0:T(8,128)S(1)}, f32[192,2048]{1,0:T(8,128)S(1)}, bf16[1024,256]{1,0:T(8,128)(2,1)}, bf16[1024,256]{1,0:T(8,128)(2,1)}, bf16[1024,25...) custom-call(s32[4]{0:T(128)S(1)} %pad_add_fusion.place.refs_0_, ...), custom_call_target="tpu_custom_call", output_to_operand_aliasing={{0}: (8, {}), {1}: (9, {})} | custom-call | flops 5100273664 | bytes 1048576 | tf_op jit(solution)/shard_map/chunk/pallas_call | solution.py:175
  62.2 0.5 collective-permute-start.18
  62.7 2.1 %collective-permute-start.19 = (bf16[1024,256]{1,0:T(8,128)(2,1)}, bf16[1024,256]{1,0:T(8,128)(2,1)S(1)}, u32[]{:S(2)}, u32[]{:S(2)}) collective-permute-start(bf16[1024,256]{1,0:T(8,128)(2,1)} %get-tuple-element.44), channel_id=1, source_target_pairs={{0,3},{1,5},{4,2},{5,6},{2,1},{3,7},{6,0},{7,4},{8,11},{9,13},{12,... | collective-permute-start | bytes 1572872 | tf_op jit(solution)/shard_map/ppermute | solution.py:26
  64.8 2.4 %collective-permute-start.20 = (bf16[1024,256]{1,0:T(8,128)(2,1)}, bf16[1024,256]{1,0:T(8,128)(2,1)S(1)}, u32[]{:S(2)}, u32[]{:S(2)}) collective-permute-start(bf16[1024,256]{1,0:T(8,128)(2,1)} %get-tuple-element.45), channel_id=1, source_target_pairs={{0,1},{1,7},{4,0},{5,4},{2,3},{3,5},{6,2},{7,6},{8,9},{9,15},{12,8... | collective-permute-start | bytes 1572872 | tf_op jit(solution)/shard_map/ppermute | solution.py:26
  67.2 0.0 collective-permute-start.21
  67.2 4.8 %collective-permute-start.22 = (bf16[1024,256]{1,0:T(8,128)(2,1)}, bf16[1024,256]{1,0:T(8,128)(2,1)S(1)}, u32[]{:S(2)}, u32[]{:S(2)}) collective-permute-start(bf16[1024,256]{1,0:T(8,128)(2,1)} %get-tuple-element.47), channel_id=1, source_target_pairs={{0,0},{1,6},{4,1},{5,5},{2,2},{3,4},{6,3},{7,7},{8,8},{9,14},{12,9... | collective-permute-start | bytes 1572872 | tf_op jit(solution)/shard_map/ppermute | solution.py:26
  72.1 0.0 collective-permute-done.18.refs_1_
  72.1 1.6 %pack.1 = bf16[16,192,128]{2,1,0:T(8,128)(2,1)} custom-call(s32[4]{0:T(128)S(1)} %pad_add_fusion.place.refs_0_, f32[192,2048]{1,0:T(8,128)S(1)} %get-tuple-element.42.refs_0_, f32[192,2048]{1,0:T(8,128)S(1)} %collective-permute-done.18.refs_1_), custom_call_target="tpu_custom_call" | custom-call | flops 1000000 | bytes 1024 | tf_op jit(solution)/shard_map/pack/pallas_call | solution.py:233
  73.7 5.1 %all-to-all-start = ((bf16[16,192,128]{2,1,0:T(8,128)(2,1)}), bf16[16,192,128]{2,1,0:T(8,128)(2,1)S(1)}, u32[]{:S(2)}, u32[]{:S(2)}) async-start(bf16[16,192,128]{2,1,0:T(8,128)(2,1)} %pack.1), calls=%async_computation | async-start | bytes 1572864 | tf_op jit(solution)/shard_map/all_to_all | solution.py:304
  78.8 0.0 copy-start
  78.9 0.0 collective-permute-done.19.refs_0_
  78.9 0.2 collective-permute-done.20.refs_1_
  79.1 11.1 %collective-permute-done.21.refs_2_ = bf16[1024,256]{1,0:T(8,128)(2,1)S(1)} collective-permute-done((bf16[1024,256]{1,0:T(8,128)(2,1)}, bf16[1024,256]{1,0:T(8,128)(2,1)S(1)}, u32[]{:S(2)}, u32[]{:S(2)}) %collective-permute-start.21) | collective-permute-done | bytes 524320 | tf_op jit(solution)/shard_map/ppermute | solution.py:26
  90.2 0.4 collective-permute-done.22.refs_3_
  90.6 1.0 %join.1 = (bf16[1024,256]{1,0:T(8,128)(2,1)}, f32[8,128]{1,0:T(8,128)S(1)}) custom-call(bf16[1024,256]{1,0:T(8,128)(2,1)S(1)} %collective-permute-done.19.refs_0_, bf16[1024,256]{1,0:T(8,128)(2,1)S(1)} %collective-permute-done.20.refs_1_, bf16[1024,256]{1,0:T(8,128)(2,1)S(1)} %collective-permute-done.21.refs_2_, ...), custom_call_target="tpu_custom_call" | custom-call | flops 99999997952 | bytes 1024 | tf_op jit(solution)/shard_map/join/pallas_call | solution.py:233
  91.6 0.4 all-to-all-done.parts_ref
  92.0 0.0 copy-done
  92.0 1.2 %decode.1 = bf16[128,1024]{1,0:T(8,128)(2,1)} custom-call(bf16[16,192,128]{2,1,0:T(8,128)(2,1)S(1)} %all-to-all-done.parts_ref, bf16[192,1024]{1,0:T(8,128)(2,1)S(1)} %copy-done, f32[8,128]{1,0:T(8,128)S(1)} %get-tuple-element.48.after_ref), custom_call_target="tpu_custom_call" | custom-call | flops 1000000 | bytes 1024 | tf_op jit(solution)/shard_map/decode/pallas_call | solution.py:233
  (5 shorter events, 0.0 us)
Async XLA Ops:
  0.6 26.0 %collective-permute-start.7 = (bf16[1024,1024]{1,0:T(8,128)(2,1)}, bf16[1024,1024]{1,0:T(8,128)(2,1)S(1)}, u32[]{:S(2)}, u32[]{:S(2)}) collective-permute-start(bf16[1024,1024]{1,0:T(8,128)(2,1)} %param.9), channel_id=1, source_target_pairs={{0,4},{1,0},{4,5},{5,1},{2,6},{3,2},{6,7},{7,3},{8,12},{9,8},{12,1... | collective-permute-start | bytes 6291464 | tf_op jit(solution)/shard_map/ppermute | solution.py:26
  4.0 7.3 %collective-permute-start = (bf16[144,1024]{1,0:T(8,128)(2,1)S(1)}, bf16[144,1024]{1,0:T(8,128)(2,1)S(1)}, u32[]{:S(2)}, u32[]{:S(2)}) collective-permute-start(bf16[144,1024]{1,0:T(8,128)(2,1)S(1)} %maximum_maximum_fusion.own_ref), channel_id=1, source_target_pairs={{0,32},{1,9},{4,36},{5,13},{2,34},{3,11},{6,38},{7,15},{8,40},{9,1... | collective-permute-start | bytes 884744 | tf_op jit(solution)/shard_map/ppermute | solution.py:26
  5.4 8.3 %collective-permute-start.1 = (bf16[144,1024]{1,0:T(8,128)(2,1)S(1)}, bf16[144,1024]{1,0:T(8,128)(2,1)S(1)}, u32[]{:S(2)}, u32[]{:S(2)}) collective-permute-start(bf16[144,1024]{1,0:T(8,128)(2,1)S(1)} %maximum_maximum_fusion.own_ref), channel_id=1, source_target_pairs={{0,96},{1,25},{4,100},{5,29},{2,98},{3,27},{6,102},{7,31},{8,104},... | collective-permute-start | bytes 884744 | tf_op jit(solution)/shard_map/ppermute | solution.py:26
  7.0 8.7 %collective-permute-start.2 = (bf16[144,1024]{1,0:T(8,128)(2,1)S(1)}, bf16[144,1024]{1,0:T(8,128)(2,1)S(1)}, u32[]{:S(2)}, u32[]{:S(2)}) collective-permute-start(bf16[144,1024]{1,0:T(8,128)(2,1)S(1)} %maximum_maximum_fusion.own_ref), channel_id=1, source_target_pairs={{0,64},{1,17},{4,68},{5,21},{2,66},{3,19},{6,70},{7,23},{8,72},{9,... | collective-permute-start | bytes 884744 | tf_op jit(solution)/shard_map/ppermute | solution.py:26
  16.3 6.9 %collective-permute-start.6 = (bf16[272,1024]{1,0:T(8,128)(2,1)S(1)}, bf16[272,1024]{1,0:T(8,128)(2,1)S(1)}, u32[]{:S(2)}, u32[]{:S(2)}) collective-permute-start(bf16[272,1024]{1,0:T(8,128)(2,1)S(1)} %get-tuple-element.27.refs_2_), channel_id=1, source_target_pairs={{0,1},{1,0},{4,5},{5,4},{2,3},{3,2},{6,7},{7,6},{8,9},{9,8},{12,13... | collective-permute-start | bytes 1671176 | tf_op jit(solution)/shard_map/ppermute | solution.py:26
  19.7 2.3 %collective-permute-start.5 = (bf16[256,1024]{1,0:T(8,128)(2,1)S(1)}, bf16[256,1024]{1,0:T(8,128)(2,1)S(1)}, u32[]{:S(2)}, u32[]{:S(2)}) collective-permute-start(bf16[256,1024]{1,0:T(8,128)(2,1)S(1)} %get-tuple-element.26.refs_1_), channel_id=1, source_target_pairs={{0,1},{1,0},{4,5},{5,4},{2,3},{3,2},{6,7},{7,6},{8,9},{9,8},{12,13... | collective-permute-start | bytes 1572872 | tf_op jit(solution)/shard_map/ppermute | solution.py:26
  19.8 14.6 %collective-permute-start.4 = (bf16[272,1024]{1,0:T(8,128)(2,1)S(1)}, bf16[272,1024]{1,0:T(8,128)(2,1)S(1)}, u32[]{:S(2)}, u32[]{:S(2)}) collective-permute-start(bf16[272,1024]{1,0:T(8,128)(2,1)S(1)} %get-tuple-element.27.refs_2_), channel_id=1, source_target_pairs={{0,24},{1,97},{4,28},{5,101},{2,26},{3,99},{6,30},{7,103},{8,0},{9... | collective-permute-start | bytes 1671176 | tf_op jit(solution)/shard_map/ppermute | solution.py:26
  21.4 13.0 %collective-permute-start.3 = (bf16[256,1024]{1,0:T(8,128)(2,1)S(1)}, bf16[256,1024]{1,0:T(8,128)(2,1)S(1)}, u32[]{:S(2)}, u32[]{:S(2)}) collective-permute-start(bf16[256,1024]{1,0:T(8,128)(2,1)S(1)} %get-tuple-element.26.refs_1_), channel_id=1, source_target_pairs={{0,8},{1,33},{4,12},{5,37},{2,10},{3,35},{6,14},{7,39},{8,16},{9,4... | collective-permute-start | bytes 1572872 | tf_op jit(solution)/shard_map/ppermute | solution.py:26
  22.0 17.2 %collective-permute-start.10 = (bf16[272,1024]{1,0:T(8,128)(2,1)S(1)}, bf16[272,1024]{1,0:T(8,128)(2,1)S(1)}, u32[]{:S(2)}, u32[]{:S(2)}) collective-permute-start(bf16[272,1024]{1,0:T(8,128)(2,1)S(1)} %get-tuple-element.27.refs_2_), channel_id=1, source_target_pairs={{0,8},{1,33},{4,12},{5,37},{2,10},{3,35},{6,14},{7,39},{8,16},{9,4... | collective-permute-start | bytes 1671176 | tf_op jit(solution)/shard_map/ppermute | solution.py:26
  23.2 16.0 %collective-permute-start.11 = (bf16[256,1024]{1,0:T(8,128)(2,1)S(1)}, bf16[256,1024]{1,0:T(8,128)(2,1)S(1)}, u32[]{:S(2)}, u32[]{:S(2)}) collective-permute-start(bf16[256,1024]{1,0:T(8,128)(2,1)S(1)} %get-tuple-element.26.refs_1_), channel_id=1, source_target_pairs={{0,24},{1,97},{4,28},{5,101},{2,26},{3,99},{6,30},{7,103},{8,0},{9... | collective-permute-start | bytes 1572872 | tf_op jit(solution)/shard_map/ppermute | solution.py:26
  26.7 1.0 %copy-start.1 = (bf16[1024,192]{0,1:T(8,128)(2,1)S(1)}, bf16[1024,192]{0,1:T(8,128)(2,1)}, u32[]{:S(2)}) copy-start(bf16[1024,192]{0,1:T(8,128)(2,1)} %param.10) | copy-start | bytes 1179652
  34.4 4.8 %collective-permute-start.13 = (bf16[272,1024]{1,0:T(8,128)(2,1)S(1)}, bf16[272,1024]{1,0:T(8,128)(2,1)S(1)}, u32[]{:S(2)}, u32[]{:S(2)}) collective-permute-start(bf16[272,1024]{1,0:T(8,128)(2,1)S(1)} %get-tuple-element.30.refs_4_), channel_id=1, source_target_pairs={{0,1},{1,0},{4,5},{5,4},{2,3},{3,2},{6,7},{7,6},{8,9},{9,8},{12,13... | collective-permute-start | bytes 1671176 | tf_op jit(solution)/shard_map/ppermute | solution.py:26
  35.4 3.9 %collective-permute-start.12 = (bf16[256,1024]{1,0:T(8,128)(2,1)S(1)}, bf16[256,1024]{1,0:T(8,128)(2,1)S(1)}, u32[]{:S(2)}, u32[]{:S(2)}) collective-permute-start(bf16[256,1024]{1,0:T(8,128)(2,1)S(1)} %get-tuple-element.29.refs_1_), channel_id=1, source_target_pairs={{0,1},{1,0},{4,5},{5,4},{2,3},{3,2},{6,7},{7,6},{8,9},{9,8},{12,13... | collective-permute-start | bytes 1572872 | tf_op jit(solution)/shard_map/ppermute | solution.py:26
  35.5 13.3 %collective-permute-start.9 = (bf16[272,1024]{1,0:T(8,128)(2,1)S(1)}, bf16[272,1024]{1,0:T(8,128)(2,1)S(1)}, u32[]{:S(2)}, u32[]{:S(2)}) collective-permute-start(bf16[272,1024]{1,0:T(8,128)(2,1)S(1)} %get-tuple-element.30.refs_4_), channel_id=1, source_target_pairs={{0,24},{1,97},{4,28},{5,101},{2,26},{3,99},{6,30},{7,103},{8,0},{9... | collective-permute-start | bytes 1671176 | tf_op jit(solution)/shard_map/ppermute | solution.py:26
  39.2 9.5 %collective-permute-start.8 = (bf16[256,1024]{1,0:T(8,128)(2,1)S(1)}, bf16[256,1024]{1,0:T(8,128)(2,1)S(1)}, u32[]{:S(2)}, u32[]{:S(2)}) collective-permute-start(bf16[256,1024]{1,0:T(8,128)(2,1)S(1)} %get-tuple-element.29.refs_1_), channel_id=1, source_target_pairs={{0,8},{1,33},{4,12},{5,37},{2,10},{3,35},{6,14},{7,39},{8,16},{9,4... | collective-permute-start | bytes 1572872 | tf_op jit(solution)/shard_map/ppermute | solution.py:26
  39.3 10.1 %collective-permute-start.16 = (bf16[272,1024]{1,0:T(8,128)(2,1)S(1)}, bf16[272,1024]{1,0:T(8,128)(2,1)S(1)}, u32[]{:S(2)}, u32[]{:S(2)}) collective-permute-start(bf16[272,1024]{1,0:T(8,128)(2,1)S(1)} %get-tuple-element.31.refs_2_), channel_id=1, source_target_pairs={{0,1},{1,0},{4,5},{5,4},{2,3},{3,2},{6,7},{7,6},{8,9},{9,8},{12,13... | collective-permute-start | bytes 1671176 | tf_op jit(solution)/shard_map/ppermute | solution.py:26
  39.7 9.7 %collective-permute-start.17 = (bf16[256,1024]{1,0:T(8,128)(2,1)S(1)}, bf16[256,1024]{1,0:T(8,128)(2,1)S(1)}, u32[]{:S(2)}, u32[]{:S(2)}) collective-permute-start(bf16[256,1024]{1,0:T(8,128)(2,1)S(1)} %get-tuple-element.32.refs_3_), channel_id=1, source_target_pairs={{0,1},{1,0},{4,5},{5,4},{2,3},{3,2},{6,7},{7,6},{8,9},{9,8},{12,13... | collective-permute-start | bytes 1572872 | tf_op jit(solution)/shard_map/ppermute | solution.py:26
  48.8 6.8 %collective-permute-start.15 = (bf16[272,1024]{1,0:T(8,128)(2,1)S(1)}, bf16[272,1024]{1,0:T(8,128)(2,1)S(1)}, u32[]{:S(2)}, u32[]{:S(2)}) collective-permute-start(bf16[272,1024]{1,0:T(8,128)(2,1)S(1)} %get-tuple-element.37.refs_2_), channel_id=1, source_target_pairs={{0,1},{1,0},{4,5},{5,4},{2,3},{3,2},{6,7},{7,6},{8,9},{9,8},{12,13... | collective-permute-start | bytes 1671176 | tf_op jit(solution)/shard_map/ppermute | solution.py:26
  49.3 6.3 %collective-permute-start.14 = (bf16[256,1024]{1,0:T(8,128)(2,1)S(1)}, bf16[256,1024]{1,0:T(8,128)(2,1)S(1)}, u32[]{:S(2)}, u32[]{:S(2)}) collective-permute-start(bf16[256,1024]{1,0:T(8,128)(2,1)S(1)} %get-tuple-element.36.refs_1_), channel_id=1, source_target_pairs={{0,1},{1,0},{4,5},{5,4},{2,3},{3,2},{6,7},{7,6},{8,9},{9,8},{12,13... | collective-permute-start | bytes 1572872 | tf_op jit(solution)/shard_map/ppermute | solution.py:26
  62.2 9.8 %collective-permute-start.18 = (f32[192,2048]{1,0:T(8,128)S(1)}, f32[192,2048]{1,0:T(8,128)S(1)}, u32[]{:S(2)}, u32[]{:S(2)}) collective-permute-start(f32[192,2048]{1,0:T(8,128)S(1)} %get-tuple-element.43), channel_id=1, source_target_pairs={{0,1},{1,0},{4,5},{5,4},{2,3},{3,2},{6,7},{7,6},{8,9},{9,8},{12,13... | collective-permute-start | bytes 4718600 | tf_op jit(solution)/shard_map/ppermute | solution.py:26
  62.7 16.1 %collective-permute-start.19 = (bf16[1024,256]{1,0:T(8,128)(2,1)}, bf16[1024,256]{1,0:T(8,128)(2,1)S(1)}, u32[]{:S(2)}, u32[]{:S(2)}) collective-permute-start(bf16[1024,256]{1,0:T(8,128)(2,1)} %get-tuple-element.44), channel_id=1, source_target_pairs={{0,3},{1,5},{4,2},{5,6},{2,1},{3,7},{6,0},{7,4},{8,11},{9,13},{12,... | collective-permute-start | bytes 1572872 | tf_op jit(solution)/shard_map/ppermute | solution.py:26
  64.8 14.3 %collective-permute-start.20 = (bf16[1024,256]{1,0:T(8,128)(2,1)}, bf16[1024,256]{1,0:T(8,128)(2,1)S(1)}, u32[]{:S(2)}, u32[]{:S(2)}) collective-permute-start(bf16[1024,256]{1,0:T(8,128)(2,1)} %get-tuple-element.45), channel_id=1, source_target_pairs={{0,1},{1,7},{4,0},{5,4},{2,3},{3,5},{6,2},{7,6},{8,9},{9,15},{12,8... | collective-permute-start | bytes 1572872 | tf_op jit(solution)/shard_map/ppermute | solution.py:26
  67.2 23.0 %collective-permute-start.21 = (bf16[1024,256]{1,0:T(8,128)(2,1)}, bf16[1024,256]{1,0:T(8,128)(2,1)S(1)}, u32[]{:S(2)}, u32[]{:S(2)}) collective-permute-start(bf16[1024,256]{1,0:T(8,128)(2,1)} %get-tuple-element.46), channel_id=1, source_target_pairs={{0,2},{1,4},{4,3},{5,7},{2,0},{3,6},{6,1},{7,5},{8,10},{9,12},{12,... | collective-permute-start | bytes 1572872 | tf_op jit(solution)/shard_map/ppermute | solution.py:26
  67.2 23.4 %collective-permute-start.22 = (bf16[1024,256]{1,0:T(8,128)(2,1)}, bf16[1024,256]{1,0:T(8,128)(2,1)S(1)}, u32[]{:S(2)}, u32[]{:S(2)}) collective-permute-start(bf16[1024,256]{1,0:T(8,128)(2,1)} %get-tuple-element.47), channel_id=1, source_target_pairs={{0,0},{1,6},{4,1},{5,5},{2,2},{3,4},{6,3},{7,7},{8,8},{9,14},{12,9... | collective-permute-start | bytes 1572872 | tf_op jit(solution)/shard_map/ppermute | solution.py:26
  73.7 18.3 %all-to-all-start = ((bf16[16,192,128]{2,1,0:T(8,128)(2,1)}), bf16[16,192,128]{2,1,0:T(8,128)(2,1)S(1)}, u32[]{:S(2)}, u32[]{:S(2)}) async-start(bf16[16,192,128]{2,1,0:T(8,128)(2,1)} %pack.1), calls=%async_computation | async-start | bytes 1572864 | tf_op jit(solution)/shard_map/all_to_all | solution.py:304
  78.8 13.2 %copy-start = (bf16[192,1024]{1,0:T(8,128)(2,1)S(1)}, bf16[192,1024]{1,0:T(8,128)(2,1)}, u32[]{:S(2)}) copy-start(bf16[192,1024]{1,0:T(8,128)(2,1)} %dec_ref.1) | copy-start | bytes 1179652

commit v5 on v4

--- a/solution.py
+++ b/solution.py
@@ -85,26 +85,28 @@
     return 2 * away + column, 2 * (1 - away) + column, 2 * away + 1 - column, 2 * (1 - away) + 1 - column
 
 
-def chunk_kernel(enc_at, fresh, first, last, scale, *refs):
+def chunk_kernel(enc_at, stage, scale, *refs):
     n = len(enc_at)
     place, q_refs, refs = refs[0], refs[1 : 1 + 2 * n], refs[1 + 2 * n :]
     z, y, x, core = (place[i] for i in range(4))
     base = ((z * 4 + y) * 2 + core) * 2 * HALF
-    w_ref, enc_ref, refs = refs[0], refs[1], refs[2:]
-    if not first:
-        total_ref, refs = refs[0], refs[1:]
-    sums = sorted({out for out, _ in enc_at})
-    if not fresh:
-        refs = refs[len(sums) :]
-    if last:
-        refs, (narrow, out_sems) = refs[:-2], refs[-2:]
-    outs, (q_all, grads, bits) = refs[:-3], refs[-3:]
-    encs, outs = dict(zip(sums, outs)), outs[len(sums) :]
-    if first:
-        wet_ref, outs = outs[0], outs[1:]
-        encode(w_ref, enc_ref, wet_ref)
+    w_ref, refs = refs[0], refs[1:]
+    q_all, bits, refs = refs[-2], refs[-1], refs[:-2]
+    if stage == 0:
+        outs, grads = refs[:1], refs[1]
     else:
-        wet_ref = enc_ref
+        grads, refs = refs[-1], refs[:-1]
+        total_ref, enc_ref, refs = refs[0], refs[1], refs[2:]
+        if stage == 3:
+            refs, (narrow, out_sems) = refs[:-2], refs[-2:]
+        if stage == 1:
+            early, encs, wet_ref, outs = refs[0], refs[1:3], refs[3], refs[4:]
+            encode(w_ref, enc_ref, wet_ref)
+        else:
+            wet_ref = enc_ref
+            named = sorted({out for out, _ in enc_at})
+            refs = refs[len(named) :]
+            encs, outs = dict(zip(named, refs)), refs[len(named) :]
     for i in range(n):
         low, high = q_refs[2 * i : 2 * i + 2]
         q_all[512 * i : 512 * i + 256, :] = low[...]
@@ -127,13 +129,15 @@
                 target = hit.reshape(256, 512).astype(F32)
                 some = jax.nn.sigmoid(logits[w * 256 : w * 256 + 256]) - target
                 grads[i * HALF + w * 256 : i * HALF + w * 256 + 256, lanes] = (some * scale).astype(BF16)
-        if not last:
+        if stage != 3:
             part = jnp.dot(grads[rows, :], q_all[...], preferred_element_type=F32)
             for c in range(4):
                 columns = slice(256 * c, 256 * c + 256)
-                old = 0.0 if first else total_ref[c, rows, :]
+                old = total_ref[c, rows, :] if stage else 0.0
                 outs[0][c, rows, :] = old + part[:, columns]
-    if last:
+    if stage == 0:
+        return
+    if stage == 3:
         copies = []
         for o, c in enumerate(quarters(x, core)):
             columns = q_all[:, pl.ds(pl.multiple_of(c * 256, 256), 256)]
@@ -141,48 +145,52 @@
             narrow[o] = whole.astype(BF16)
             copies.append(pltpu.make_async_copy(narrow.at[o], outs[o], out_sems.at[o]))
             copies[-1].start()
-    encoded = jnp.dot(wet_ref[...], grads[...], preferred_element_type=F32)
-    encoded = encoded[:192] + encoded[192:]
-    for i, (out, column) in enumerate(enc_at):
-        encs[out][:, column : column + 512] = encoded[:, 512 * i : 512 * i + 512]
-    if last:
+    both = [(grads, enc_at)] + ([(early, ((0, 0), (1, 0)))] if stage == 1 else [])
+    for values, to in both:
+        encoded = jnp.dot(wet_ref[...], values[...], preferred_element_type=F32)
+        encoded = encoded[:192] + encoded[192:]
+        for i, (out, column) in enumerate(to):
+            encs[out][:, column : column + 512] = encoded[:, 512 * i : 512 * i + 512]
+    if stage == 3:
         for copy in copies:
             copy.wait()
 
 
-def chunk(place, groups, enc_at, w, enc, total, sums, last, scale):
-    first, fresh = total is None, sums is None
+def chunk(stage, place, groups, enc_at, w, scale, total=None, enc=None, early=None, sums=()):
     vmem = pl.BlockSpec(memory_space=pltpu.VMEM)
     labels, n = 2 * HALF, 512 * len(enc_at)
-    named = sorted({out for out, _ in enc_at})
-    args = [place, *sum(groups, []), w, enc] + ([] if first else [total])
-    shapes = [jax.ShapeDtypeStruct((192, 2048), F32) for _ in named]
-    aliases = {} if fresh else {len(args) + i: i for i in range(len(named))}
-    if first:
+    named = sorted({out for out, _ in enc_at}) if stage > 1 else [0, 1]
+    args = [place, *sum(groups, []), w] + ([total, enc] if stage else [])
+    at_total = len(args) - 2
+    shapes, aliases = [], {}
+    if stage:
+        shapes = [jax.ShapeDtypeStruct((192, 2048), F32) for _ in named]
+    if stage == 1:
+        args.append(early)
         shapes.append(jax.ShapeDtypeStruct((384, labels), BF16))
-    if last:
+    if stage > 1:
+        aliases = {len(args) + i: i for i in range(len(named))}
+        args += [sums[i] for i in named]
+    if stage == 3:
         shapes += [jax.ShapeDtypeStruct((labels, 256), BF16)] * 4
     else:
-        if not first:
-            aliases[len(args) - 1] = len(shapes)
+        if stage:
+            aliases[at_total] = len(shapes)
         shapes.append(jax.ShapeDtypeStruct((4, labels, 256), F32))
-    if not fresh:
-        args += [sums[i] for i in named]
+    grads = [pltpu.VMEM((labels, n), BF16)]
+    if stage == 0:
+        shapes.append(jax.ShapeDtypeStruct((labels, n), BF16))
+        grads = []
     out_specs, scratch = [vmem] * len(shapes), []
-    if last:
+    if stage == 3:
         out_specs[-4:] = [pl.BlockSpec(memory_space=pltpu.HBM)] * 4
         scratch = [pltpu.VMEM((4, labels, 256), BF16), pltpu.SemaphoreType.DMA((4,))]
     out = pl.pallas_call(
-        functools.partial(chunk_kernel, enc_at, fresh, first, last, scale),
+        functools.partial(chunk_kernel, enc_at, stage, scale),
         in_specs=[pl.BlockSpec(memory_space=pltpu.SMEM)] + [vmem] * (len(args) - 1),
         out_specs=out_specs,
         out_shape=shapes,
-        scratch_shapes=[
-            pltpu.VMEM((n, 1024), BF16),
-            pltpu.VMEM((labels, n), BF16),
-            pltpu.VMEM((4, 8, n), I32),
-            *scratch,
-        ],
+        scratch_shapes=[*scratch, *grads, pltpu.VMEM((n, 1024), BF16), pltpu.VMEM((4, 8, n), I32)],
         input_output_aliases=aliases,
         compiler_params=pltpu.CompilerParams(vmem_limit_bytes=VMEM_LIMIT),
         cost_estimate=pl.CostEstimate(
@@ -190,7 +198,9 @@
         ),
         name="chunk",
     )(*args)
-    new = dict(enumerate([None, None] if fresh else sums)) | dict(zip(named, out))
+    if stage == 0:
+        return out
+    new = dict(enumerate(sums)) | dict(zip(named, out))
     return ([new[0], new[1]], *out[len(named) :])
 
 
@@ -276,21 +286,22 @@
     high_back, low_ahead = move(high, hop(1, 1)), move(low, hop(1, -1))
     sibling = lambda array: move(array, to_sibling)
     row, own, sib = [low, high], 0, 1
-    sums, wet, total = chunk(
-        place, [row, [sibling(low), sibling(high)]], ((own, 0), (sib, 0)), w, encoder.T, None, None, False, scale
-    )
-    low_back, high_ahead = after([low_back, high_ahead], wet)
+    rows = [row, [sibling(low), sibling(high)]]
+    total, early_grads = chunk(0, place, rows, ((own, 0), (sib, 0)), w, scale)
+    low_back, high_ahead = after([low_back, high_ahead], early_grads)
     far = [move(low_back, hop(1, 1)), move(high_ahead, hop(1, -1))]
     early = [sibling(low_back), sibling(high_ahead)]
     high_back, low_ahead = after([high_back, low_ahead], *early)
     late = [sibling(high_back), sibling(low_ahead)]
     back, ahead = [low_back, high_back], [low_ahead, high_ahead]
-    sums, total = chunk(place, [back, ahead], ((own, 512), (own, 1024)), w, wet, total, sums, False, scale)
+    sums, wet, total = chunk(
+        1, place, [back, ahead], ((own, 512), (own, 1024)), w, scale, total, encoder.T, early_grads
+    )
     far = after(far, sums[own])
     back, ahead = [early[0], late[0]], [late[1], early[1]]
-    sums, total = chunk(place, [back, ahead], ((sib, 512), (sib, 1024)), w, wet, total, sums, False, scale)
+    sums, total = chunk(2, place, [back, ahead], ((sib, 512), (sib, 1024)), w, scale, total, wet, None, sums)
     far_sib = [sibling(f) for f in far]
-    sums, *outs = chunk(place, [far, far_sib], ((own, 1536), (sib, 1536)), w, wet, total, sums, True, scale)
+    sums, *outs = chunk(3, place, [far, far_sib], ((own, 1536), (sib, 1536)), w, scale, total, wet, None, sums)
 
     pick = lambda same, other: lambda z, y, x, c: same(z, y, x, c) if c == x % 2 else other(z, y, x, c)
     got = [

time: 93.6 us -> 91.9 us (0.982)
  waiting for transfers between devices: 24.4 us -> 21.5 us
  starting transfers between devices: 34.9 us -> 36.9 us
  local copies, waits for them, and re-layouts: 1.09 us -> 0.1 us
    ppermute x23, waiting for transfers between devices: 24 us -> 20.8 us  [move(): return lax.ppermute(array, AXES, pairs(target))]
    ppermute x23, starting transfers between devices: 29.8 us -> 30.8 us  [move(): return lax.ppermute(array, AXES, pairs(target))]
    unnamed x4, local copies, waits for them, and re-layouts: 1 us -> 0.01 us
  transfers between devices with their start and end apart: 24 -> 24, of which waited for: 10 -> 8; matrix products, arithmetic and copies ran while one was open for 2% -> 2% of each run, Pallas kernels for 24% -> 25%
where the time goes in v5:
time: 91.9 us; the launch traced here: 91.6 us
  starting transfers between devices  36.9 us (40%)
  Pallas kernels  30.4 us (33%)
  waiting for transfers between devices  21.5 us (23%)
  other arithmetic  1.84 us (2%)
    ppermute x23, starting transfers between devices, move(): return lax.ppermute(array, AXES, pairs(target))  30.8 us
    pallas_call x4, Pallas kernels, chunk(): pl.pallas_call(functools.partial(chunk_kernel, enc_at, stage, scale), in_...  25.9 us
    ppermute x23, waiting for transfers between devices, move(): return lax.ppermute(array, AXES, pairs(target))  20.8 us
    all_to_all x1, starting transfers between devices, shards(): lax.all_to_all(packed, ('z', 'y'), split_axis=0, concat_axis=0, tiled=True)  6.05 us
    pallas_call x4, Pallas kernels, kernel(): pl.pallas_call(body, in_specs=[pl.BlockSpec(memory_space=place(a)) for a...  4.51 us
  transfers between devices with their start and end apart: 24, of which 8 were waited for; matrix products, arithmetic and copies ran while one was open for 2% of the time, Pallas kernels for 25%

profile of v5, /device:TPU:1, one launch (start us, length us, event | category | flops | bytes accessed | tf_op | source)
XLA Modules:
  0.0 91.6 jit_solution(14579837885785500715)
XLA Ops:
  0.6 1.5 %collective-permute-start.7 = (bf16[1024,1024]{1,0:T(8,128)(2,1)}, bf16[1024,1024]{1,0:T(8,128)(2,1)S(1)}, u32[]{:S(2)}, u32[]{:S(2)}) collective-permute-start(bf16[1024,1024]{1,0:T(8,128)(2,1)} %param.9), channel_id=1, source_target_pairs={{0,4},{1,0},{4,5},{5,1},{2,6},{3,2},{6,7},{7,3},{8,12},{9,8},{12,1... | collective-permute-start | bytes 6291464 | tf_op jit(solution)/shard_map/ppermute | solution.py:26
  2.1 0.1 pad.3.clone
  2.2 0.7 fusion
  2.9 1.1 %maximum_maximum_fusion.own_ref = bf16[144,1024]{1,0:T(8,128)(2,1)S(1)} fusion(bf16[1,1024]{1,0:T(2,128)(2,1)S(1)} %get-tuple-element.52, bf16[1,1024]{1,0:T(2,128)(2,1)S(1)} %get-tuple-element.53, bf16[128,1024]{1,0:T(8,128)(2,1)} %param.6, bf16[144]{0:T(256)(128)(2,1)S(1)} %pad.3.clone), kind=kLoop, calls=%fused_computation | loop fusion | flops 1179648 | bytes 561440 | tf_op jit(solution)/shard_map/concatenate | solution.py:278
  4.0 1.4 %collective-permute-start = (bf16[144,1024]{1,0:T(8,128)(2,1)S(1)}, bf16[144,1024]{1,0:T(8,128)(2,1)S(1)}, u32[]{:S(2)}, u32[]{:S(2)}) collective-permute-start(bf16[144,1024]{1,0:T(8,128)(2,1)S(1)} %maximum_maximum_fusion.own_ref), channel_id=1, source_target_pairs={{0,32},{1,9},{4,36},{5,13},{2,34},{3,11},{6,38},{7,15},{8,40},{9,1... | collective-permute-start | bytes 884744 | tf_op jit(solution)/shard_map/ppermute | solution.py:26
  5.4 1.5 %collective-permute-start.1 = (bf16[144,1024]{1,0:T(8,128)(2,1)S(1)}, bf16[144,1024]{1,0:T(8,128)(2,1)S(1)}, u32[]{:S(2)}, u32[]{:S(2)}) collective-permute-start(bf16[144,1024]{1,0:T(8,128)(2,1)S(1)} %maximum_maximum_fusion.own_ref), channel_id=1, source_target_pairs={{0,96},{1,25},{4,100},{5,29},{2,98},{3,27},{6,102},{7,31},{8,104},... | collective-permute-start | bytes 884744 | tf_op jit(solution)/shard_map/ppermute | solution.py:26
  7.0 1.6 %collective-permute-start.2 = (bf16[144,1024]{1,0:T(8,128)(2,1)S(1)}, bf16[144,1024]{1,0:T(8,128)(2,1)S(1)}, u32[]{:S(2)}, u32[]{:S(2)}) collective-permute-start(bf16[144,1024]{1,0:T(8,128)(2,1)S(1)} %maximum_maximum_fusion.own_ref), channel_id=1, source_target_pairs={{0,64},{1,17},{4,68},{5,21},{2,66},{3,19},{6,70},{7,23},{8,72},{9,... | collective-permute-start | bytes 884744 | tf_op jit(solution)/shard_map/ppermute | solution.py:26
  8.5 0.1 pad_add_fusion.place.refs_0_
  8.6 2.7 %collective-permute-done.back_ref = bf16[144,1024]{1,0:T(8,128)(2,1)S(1)} collective-permute-done((bf16[144,1024]{1,0:T(8,128)(2,1)S(1)}, bf16[144,1024]{1,0:T(8,128)(2,1)S(1)}, u32[]{:S(2)}, u32[]{:S(2)}) %collective-permute-start) | collective-permute-done | bytes 294944 | tf_op jit(solution)/shard_map/ppermute | solution.py:26
  11.3 2.5 %collective-permute-done.1.ahead_ref = bf16[144,1024]{1,0:T(8,128)(2,1)S(1)} collective-permute-done((bf16[144,1024]{1,0:T(8,128)(2,1)S(1)}, bf16[144,1024]{1,0:T(8,128)(2,1)S(1)}, u32[]{:S(2)}, u32[]{:S(2)}) %collective-permute-start.1) | collective-permute-done | bytes 294944 | tf_op jit(solution)/shard_map/ppermute | solution.py:26
  13.8 1.8 %collective-permute-done.2.far_ref = bf16[144,1024]{1,0:T(8,128)(2,1)S(1)} collective-permute-done((bf16[144,1024]{1,0:T(8,128)(2,1)S(1)}, bf16[144,1024]{1,0:T(8,128)(2,1)S(1)}, u32[]{:S(2)}, u32[]{:S(2)}) %collective-permute-start.2) | collective-permute-done | bytes 294944 | tf_op jit(solution)/shard_map/ppermute | solution.py:26
  15.6 0.6 rows.1
  16.3 3.4 %collective-permute-start.6 = (bf16[272,1024]{1,0:T(8,128)(2,1)S(1)}, bf16[272,1024]{1,0:T(8,128)(2,1)S(1)}, u32[]{:S(2)}, u32[]{:S(2)}) collective-permute-start(bf16[272,1024]{1,0:T(8,128)(2,1)S(1)} %get-tuple-element.27.refs_2_), channel_id=1, source_target_pairs={{0,1},{1,0},{4,5},{5,4},{2,3},{3,2},{6,7},{7,6},{8,9},{9,8},{12,13... | collective-permute-start | bytes 1671176 | tf_op jit(solution)/shard_map/ppermute | solution.py:26
  19.7 0.1 collective-permute-start.5
  19.8 1.6 %collective-permute-start.4 = (bf16[272,1024]{1,0:T(8,128)(2,1)S(1)}, bf16[272,1024]{1,0:T(8,128)(2,1)S(1)}, u32[]{:S(2)}, u32[]{:S(2)}) collective-permute-start(bf16[272,1024]{1,0:T(8,128)(2,1)S(1)} %get-tuple-element.27.refs_2_), channel_id=1, source_target_pairs={{0,24},{1,97},{4,28},{5,101},{2,26},{3,99},{6,30},{7,103},{8,0},{9... | collective-permute-start | bytes 1671176 | tf_op jit(solution)/shard_map/ppermute | solution.py:26
  21.4 0.0 collective-permute-start.3
  21.4 0.7 collective-permute-done.5.refs_3_
  22.0 1.1 %collective-permute-start.10 = (bf16[272,1024]{1,0:T(8,128)(2,1)S(1)}, bf16[272,1024]{1,0:T(8,128)(2,1)S(1)}, u32[]{:S(2)}, u32[]{:S(2)}) collective-permute-start(bf16[272,1024]{1,0:T(8,128)(2,1)S(1)} %get-tuple-element.27.refs_2_), channel_id=1, source_target_pairs={{0,8},{1,33},{4,12},{5,37},{2,10},{3,35},{6,14},{7,39},{8,16},{9,4... | collective-permute-start | bytes 1671176 | tf_op jit(solution)/shard_map/ppermute | solution.py:26
  23.2 0.0 collective-permute-done.6.refs_4_
  23.2 1.5 %collective-permute-start.11 = (bf16[256,1024]{1,0:T(8,128)(2,1)S(1)}, bf16[256,1024]{1,0:T(8,128)(2,1)S(1)}, u32[]{:S(2)}, u32[]{:S(2)}) collective-permute-start(bf16[256,1024]{1,0:T(8,128)(2,1)S(1)} %get-tuple-element.26.refs_1_), channel_id=1, source_target_pairs={{0,24},{1,97},{4,28},{5,101},{2,26},{3,99},{6,30},{7,103},{8,0},{9... | collective-permute-start | bytes 1572872 | tf_op jit(solution)/shard_map/ppermute | solution.py:26
  24.7 2.0 %collective-permute-done.7.refs_5_ = bf16[1024,1024]{1,0:T(8,128)(2,1)S(1)} collective-permute-done((bf16[1024,1024]{1,0:T(8,128)(2,1)}, bf16[1024,1024]{1,0:T(8,128)(2,1)S(1)}, u32[]{:S(2)}, u32[]{:S(2)}) %collective-permute-start.7) | collective-permute-done | bytes 2097184 | tf_op jit(solution)/shard_map/ppermute | solution.py:26
  26.7 5.4 %chunk.4 = (f32[4,1024,256]{2,1,0:T(8,128)S(1)}, bf16[1024,1024]{1,0:T(8,128)(2,1)S(1)}) custom-call(s32[4]{0:T(128)S(1)} %pad_add_fusion.place.refs_0_, bf16[256,1024]{1,0:T(8,128)(2,1)S(1)} %get-tuple-element.26.refs_1_, bf16[272,1024]{1,0:T(8,128)(2,1)S(1)} %get-tuple-element.27.refs_2_, bf16[256,1024]{1,0:T(8,128)(2,1)S(1)} %collective-permute-done.5.refs_3_, ...), custom_call_target="tpu_custom_call" | custom-call | flops 5100273664 | bytes 1048576 | tf_op jit(solution)/shard_map/chunk/pallas_call | solution.py:188
  32.1 0.0 collective-permute-done.3.refs_0_
  32.1 0.0 collective-permute-done.4.refs_1_
  32.1 0.0 copy-start.1
  32.1 1.5 %collective-permute-start.13 = (bf16[272,1024]{1,0:T(8,128)(2,1)S(1)}, bf16[272,1024]{1,0:T(8,128)(2,1)S(1)}, u32[]{:S(2)}, u32[]{:S(2)}) collective-permute-start(bf16[272,1024]{1,0:T(8,128)(2,1)S(1)} %get-tuple-element.30.refs_4_), channel_id=1, source_target_pairs={{0,1},{1,0},{4,5},{5,4},{2,3},{3,2},{6,7},{7,6},{8,9},{9,8},{12,13... | collective-permute-start | bytes 1671176 | tf_op jit(solution)/shard_map/ppermute | solution.py:26
  33.6 0.1 collective-permute-start.12
  33.7 3.2 %collective-permute-start.9 = (bf16[272,1024]{1,0:T(8,128)(2,1)S(1)}, bf16[272,1024]{1,0:T(8,128)(2,1)S(1)}, u32[]{:S(2)}, u32[]{:S(2)}) collective-permute-start(bf16[272,1024]{1,0:T(8,128)(2,1)S(1)} %get-tuple-element.30.refs_4_), channel_id=1, source_target_pairs={{0,24},{1,97},{4,28},{5,101},{2,26},{3,99},{6,30},{7,103},{8,0},{9... | collective-permute-start | bytes 1671176 | tf_op jit(solution)/shard_map/ppermute | solution.py:26
  37.0 0.0 collective-permute-done.11.refs_1_
  37.0 0.0 collective-permute-start.8
  37.0 0.0 collective-permute-done.10.refs_0_
  37.0 0.0 collective-permute-done.12.refs_2_.refs_1_
  37.0 0.0 collective-permute-done.13.refs_3_.refs_4_
  37.0 2.7 %collective-permute-start.16 = (bf16[272,1024]{1,0:T(8,128)(2,1)S(1)}, bf16[272,1024]{1,0:T(8,128)(2,1)S(1)}, u32[]{:S(2)}, u32[]{:S(2)}) collective-permute-start(bf16[272,1024]{1,0:T(8,128)(2,1)S(1)} %get-tuple-element.31.refs_2_), channel_id=1, source_target_pairs={{0,1},{1,0},{4,5},{5,4},{2,3},{3,2},{6,7},{7,6},{8,9},{9,8},{12,13... | collective-permute-start | bytes 1671176 | tf_op jit(solution)/shard_map/ppermute | solution.py:26
  39.7 0.3 collective-permute-start.17
  40.0 0.0 copy-done.1
  40.0 7.7 %chunk.5 = (f32[192,2048]{1,0:T(8,128)S(1)}, f32[192,2048]{1,0:T(8,128)S(1)}, bf16[384,1024]{1,0:T(8,128)(2,1)S(1)}, f32[4,1024,256]{2,1,0:T(8,128)S(1)}) custom-call(s32[4]{0:T(128)S(1)} %pad_add_fusion.place.refs_0_, bf16[256,1024]{1,0:T(8,128)(2,1)S(1)} %get-tuple-element.29.refs_1_, ...), custom_call_target="tpu_custom_call", output_to_operand_aliasing={{3}: (6, {})} | custom-call | flops 5100273664 | bytes 1048576 | tf_op jit(solution)/shard_map/chunk/pallas_call | solution.py:188
  47.7 0.0 collective-permute-done.8.refs_0_
  47.7 0.0 collective-permute-done.9.refs_1_
  47.7 0.3 collective-permute-start.15
  48.0 0.3 collective-permute-start.14
  48.3 0.0 collective-permute-done.17.refs_3_
  48.3 0.0 collective-permute-done.16.refs_2_
  48.3 6.2 %chunk.6 = (f32[192,2048]{1,0:T(8,128)S(1)}, f32[4,1024,256]{2,1,0:T(8,128)S(1)}) custom-call(s32[4]{0:T(128)S(1)} %pad_add_fusion.place.refs_0_, bf16[256,1024]{1,0:T(8,128)(2,1)S(1)} %collective-permute-done.12.refs_2_.refs_1_, bf16[272,1024]{1,0:T(8,128)(2,1)S(1)} %collective-permute-done.16.refs_2_, ...), custom_call_target="tpu_custom_call", output_to_operand_aliasing={{0}: (8, {}), {1}: (6, {})} | custom-call | flops 5100273664 | bytes 1048576 | tf_op jit(solution)/shard_map/chunk/pallas_call | solution.py:188
  54.5 0.0 collective-permute-done.14.refs_3_
  54.5 0.0 collective-permute-done.15.refs_4_
  54.5 6.6 %chunk.7 = (f32[192,2048]{1,0:T(8,128)S(1)}, f32[192,2048]{1,0:T(8,128)S(1)}, bf16[1024,256]{1,0:T(8,128)(2,1)}, bf16[1024,256]{1,0:T(8,128)(2,1)}, bf16[1024,25...) custom-call(s32[4]{0:T(128)S(1)} %pad_add_fusion.place.refs_0_, ...), custom_call_target="tpu_custom_call", output_to_operand_aliasing={{0}: (8, {}), {1}: (9, {})} | custom-call | flops 5100273664 | bytes 1048576 | tf_op jit(solution)/shard_map/chunk/pallas_call | solution.py:188
  61.1 0.3 collective-permute-start.18
  61.5 1.1 %collective-permute-start.19 = (bf16[1024,256]{1,0:T(8,128)(2,1)}, bf16[1024,256]{1,0:T(8,128)(2,1)S(1)}, u32[]{:S(2)}, u32[]{:S(2)}) collective-permute-start(bf16[1024,256]{1,0:T(8,128)(2,1)} %get-tuple-element.44), channel_id=1, source_target_pairs={{0,3},{1,5},{4,2},{5,6},{2,1},{3,7},{6,0},{7,4},{8,11},{9,13},{12,... | collective-permute-start | bytes 1572872 | tf_op jit(solution)/shard_map/ppermute | solution.py:26
  62.5 2.4 %collective-permute-start.20 = (bf16[1024,256]{1,0:T(8,128)(2,1)}, bf16[1024,256]{1,0:T(8,128)(2,1)S(1)}, u32[]{:S(2)}, u32[]{:S(2)}) collective-permute-start(bf16[1024,256]{1,0:T(8,128)(2,1)} %get-tuple-element.45), channel_id=1, source_target_pairs={{0,1},{1,7},{4,0},{5,4},{2,3},{3,5},{6,2},{7,6},{8,9},{9,15},{12,8... | collective-permute-start | bytes 1572872 | tf_op jit(solution)/shard_map/ppermute | solution.py:26
  64.9 1.0 %collective-permute-start.21 = (bf16[1024,256]{1,0:T(8,128)(2,1)}, bf16[1024,256]{1,0:T(8,128)(2,1)S(1)}, u32[]{:S(2)}, u32[]{:S(2)}) collective-permute-start(bf16[1024,256]{1,0:T(8,128)(2,1)} %get-tuple-element.46), channel_id=1, source_target_pairs={{0,2},{1,4},{4,3},{5,7},{2,0},{3,6},{6,1},{7,5},{8,10},{9,12},{12,... | collective-permute-start | bytes 1572872 | tf_op jit(solution)/shard_map/ppermute | solution.py:26
  65.9 3.8 %collective-permute-start.22 = (bf16[1024,256]{1,0:T(8,128)(2,1)}, bf16[1024,256]{1,0:T(8,128)(2,1)S(1)}, u32[]{:S(2)}, u32[]{:S(2)}) collective-permute-start(bf16[1024,256]{1,0:T(8,128)(2,1)} %get-tuple-element.47), channel_id=1, source_target_pairs={{0,0},{1,6},{4,1},{5,5},{2,2},{3,4},{6,3},{7,7},{8,8},{9,14},{12,9... | collective-permute-start | bytes 1572872 | tf_op jit(solution)/shard_map/ppermute | solution.py:26
  69.8 0.0 collective-permute-done.18.refs_1_
  69.8 1.6 %pack.1 = bf16[16,192,128]{2,1,0:T(8,128)(2,1)} custom-call(s32[4]{0:T(128)S(1)} %pad_add_fusion.place.refs_0_, f32[192,2048]{1,0:T(8,128)S(1)} %get-tuple-element.42.refs_0_, f32[192,2048]{1,0:T(8,128)S(1)} %collective-permute-done.18.refs_1_), custom_call_target="tpu_custom_call" | custom-call | flops 1000000 | bytes 1024 | tf_op jit(solution)/shard_map/pack/pallas_call | solution.py:243
  71.4 6.1 %all-to-all-start = ((bf16[16,192,128]{2,1,0:T(8,128)(2,1)}), bf16[16,192,128]{2,1,0:T(8,128)(2,1)S(1)}, u32[]{:S(2)}, u32[]{:S(2)}) async-start(bf16[16,192,128]{2,1,0:T(8,128)(2,1)} %pack.1), calls=%async_computation | async-start | bytes 1572864 | tf_op jit(solution)/shard_map/all_to_all | solution.py:315
  77.5 0.0 copy-start
  77.5 0.0 collective-permute-done.19.refs_0_
  77.5 0.4 collective-permute-done.20.refs_1_
  77.9 10.7 %collective-permute-done.21.refs_2_ = bf16[1024,256]{1,0:T(8,128)(2,1)S(1)} collective-permute-done((bf16[1024,256]{1,0:T(8,128)(2,1)}, bf16[1024,256]{1,0:T(8,128)(2,1)S(1)}, u32[]{:S(2)}, u32[]{:S(2)}) %collective-permute-start.21) | collective-permute-done | bytes 524320 | tf_op jit(solution)/shard_map/ppermute | solution.py:26
  88.6 0.0 collective-permute-done.22.refs_3_
  88.6 1.1 %join.1 = (bf16[1024,256]{1,0:T(8,128)(2,1)}, f32[8,128]{1,0:T(8,128)S(1)}) custom-call(bf16[1024,256]{1,0:T(8,128)(2,1)S(1)} %collective-permute-done.19.refs_0_, bf16[1024,256]{1,0:T(8,128)(2,1)S(1)} %collective-permute-done.20.refs_1_, bf16[1024,256]{1,0:T(8,128)(2,1)S(1)} %collective-permute-done.21.refs_2_, ...), custom_call_target="tpu_custom_call" | custom-call | flops 99999997952 | bytes 1024 | tf_op jit(solution)/shard_map/join/pallas_call | solution.py:243
  89.7 0.7 all-to-all-done.parts_ref
  90.4 0.0 copy-done
  90.4 1.2 %decode.1 = bf16[128,1024]{1,0:T(8,128)(2,1)} custom-call(bf16[16,192,128]{2,1,0:T(8,128)(2,1)S(1)} %all-to-all-done.parts_ref, bf16[192,1024]{1,0:T(8,128)(2,1)S(1)} %copy-done, f32[8,128]{1,0:T(8,128)S(1)} %get-tuple-element.48.after_ref), custom_call_target="tpu_custom_call" | custom-call | flops 1000000 | bytes 1024 | tf_op jit(solution)/shard_map/decode/pallas_call | solution.py:243
  (5 shorter events, 0.0 us)
Async XLA Ops:
  0.6 26.0 %collective-permute-start.7 = (bf16[1024,1024]{1,0:T(8,128)(2,1)}, bf16[1024,1024]{1,0:T(8,128)(2,1)S(1)}, u32[]{:S(2)}, u32[]{:S(2)}) collective-permute-start(bf16[1024,1024]{1,0:T(8,128)(2,1)} %param.9), channel_id=1, source_target_pairs={{0,4},{1,0},{4,5},{5,1},{2,6},{3,2},{6,7},{7,3},{8,12},{9,8},{12,1... | collective-permute-start | bytes 6291464 | tf_op jit(solution)/shard_map/ppermute | solution.py:26
  4.0 7.3 %collective-permute-start = (bf16[144,1024]{1,0:T(8,128)(2,1)S(1)}, bf16[144,1024]{1,0:T(8,128)(2,1)S(1)}, u32[]{:S(2)}, u32[]{:S(2)}) collective-permute-start(bf16[144,1024]{1,0:T(8,128)(2,1)S(1)} %maximum_maximum_fusion.own_ref), channel_id=1, source_target_pairs={{0,32},{1,9},{4,36},{5,13},{2,34},{3,11},{6,38},{7,15},{8,40},{9,1... | collective-permute-start | bytes 884744 | tf_op jit(solution)/shard_map/ppermute | solution.py:26
  5.4 8.3 %collective-permute-start.1 = (bf16[144,1024]{1,0:T(8,128)(2,1)S(1)}, bf16[144,1024]{1,0:T(8,128)(2,1)S(1)}, u32[]{:S(2)}, u32[]{:S(2)}) collective-permute-start(bf16[144,1024]{1,0:T(8,128)(2,1)S(1)} %maximum_maximum_fusion.own_ref), channel_id=1, source_target_pairs={{0,96},{1,25},{4,100},{5,29},{2,98},{3,27},{6,102},{7,31},{8,104},... | collective-permute-start | bytes 884744 | tf_op jit(solution)/shard_map/ppermute | solution.py:26
  7.0 8.7 %collective-permute-start.2 = (bf16[144,1024]{1,0:T(8,128)(2,1)S(1)}, bf16[144,1024]{1,0:T(8,128)(2,1)S(1)}, u32[]{:S(2)}, u32[]{:S(2)}) collective-permute-start(bf16[144,1024]{1,0:T(8,128)(2,1)S(1)} %maximum_maximum_fusion.own_ref), channel_id=1, source_target_pairs={{0,64},{1,17},{4,68},{5,21},{2,66},{3,19},{6,70},{7,23},{8,72},{9,... | collective-permute-start | bytes 884744 | tf_op jit(solution)/shard_map/ppermute | solution.py:26
  16.3 6.9 %collective-permute-start.6 = (bf16[272,1024]{1,0:T(8,128)(2,1)S(1)}, bf16[272,1024]{1,0:T(8,128)(2,1)S(1)}, u32[]{:S(2)}, u32[]{:S(2)}) collective-permute-start(bf16[272,1024]{1,0:T(8,128)(2,1)S(1)} %get-tuple-element.27.refs_2_), channel_id=1, source_target_pairs={{0,1},{1,0},{4,5},{5,4},{2,3},{3,2},{6,7},{7,6},{8,9},{9,8},{12,13... | collective-permute-start | bytes 1671176 | tf_op jit(solution)/shard_map/ppermute | solution.py:26
  19.7 2.3 %collective-permute-start.5 = (bf16[256,1024]{1,0:T(8,128)(2,1)S(1)}, bf16[256,1024]{1,0:T(8,128)(2,1)S(1)}, u32[]{:S(2)}, u32[]{:S(2)}) collective-permute-start(bf16[256,1024]{1,0:T(8,128)(2,1)S(1)} %get-tuple-element.26.refs_1_), channel_id=1, source_target_pairs={{0,1},{1,0},{4,5},{5,4},{2,3},{3,2},{6,7},{7,6},{8,9},{9,8},{12,13... | collective-permute-start | bytes 1572872 | tf_op jit(solution)/shard_map/ppermute | solution.py:26
  19.8 12.3 %collective-permute-start.4 = (bf16[272,1024]{1,0:T(8,128)(2,1)S(1)}, bf16[272,1024]{1,0:T(8,128)(2,1)S(1)}, u32[]{:S(2)}, u32[]{:S(2)}) collective-permute-start(bf16[272,1024]{1,0:T(8,128)(2,1)S(1)} %get-tuple-element.27.refs_2_), channel_id=1, source_target_pairs={{0,24},{1,97},{4,28},{5,101},{2,26},{3,99},{6,30},{7,103},{8,0},{9... | collective-permute-start | bytes 1671176 | tf_op jit(solution)/shard_map/ppermute | solution.py:26
  21.4 10.7 %collective-permute-start.3 = (bf16[256,1024]{1,0:T(8,128)(2,1)S(1)}, bf16[256,1024]{1,0:T(8,128)(2,1)S(1)}, u32[]{:S(2)}, u32[]{:S(2)}) collective-permute-start(bf16[256,1024]{1,0:T(8,128)(2,1)S(1)} %get-tuple-element.26.refs_1_), channel_id=1, source_target_pairs={{0,8},{1,33},{4,12},{5,37},{2,10},{3,35},{6,14},{7,39},{8,16},{9,4... | collective-permute-start | bytes 1572872 | tf_op jit(solution)/shard_map/ppermute | solution.py:26
  22.0 14.9 %collective-permute-start.10 = (bf16[272,1024]{1,0:T(8,128)(2,1)S(1)}, bf16[272,1024]{1,0:T(8,128)(2,1)S(1)}, u32[]{:S(2)}, u32[]{:S(2)}) collective-permute-start(bf16[272,1024]{1,0:T(8,128)(2,1)S(1)} %get-tuple-element.27.refs_2_), channel_id=1, source_target_pairs={{0,8},{1,33},{4,12},{5,37},{2,10},{3,35},{6,14},{7,39},{8,16},{9,4... | collective-permute-start | bytes 1671176 | tf_op jit(solution)/shard_map/ppermute | solution.py:26
  23.2 13.8 %collective-permute-start.11 = (bf16[256,1024]{1,0:T(8,128)(2,1)S(1)}, bf16[256,1024]{1,0:T(8,128)(2,1)S(1)}, u32[]{:S(2)}, u32[]{:S(2)}) collective-permute-start(bf16[256,1024]{1,0:T(8,128)(2,1)S(1)} %get-tuple-element.26.refs_1_), channel_id=1, source_target_pairs={{0,24},{1,97},{4,28},{5,101},{2,26},{3,99},{6,30},{7,103},{8,0},{9... | collective-permute-start | bytes 1572872 | tf_op jit(solution)/shard_map/ppermute | solution.py:26
  32.1 7.8 %copy-start.1 = (bf16[1024,192]{0,1:T(8,128)(2,1)S(1)}, bf16[1024,192]{0,1:T(8,128)(2,1)}, u32[]{:S(2)}) copy-start(bf16[1024,192]{0,1:T(8,128)(2,1)} %param.10) | copy-start | bytes 1179652
  32.1 4.9 %collective-permute-start.13 = (bf16[272,1024]{1,0:T(8,128)(2,1)S(1)}, bf16[272,1024]{1,0:T(8,128)(2,1)S(1)}, u32[]{:S(2)}, u32[]{:S(2)}) collective-permute-start(bf16[272,1024]{1,0:T(8,128)(2,1)S(1)} %get-tuple-element.30.refs_4_), channel_id=1, source_target_pairs={{0,1},{1,0},{4,5},{5,4},{2,3},{3,2},{6,7},{7,6},{8,9},{9,8},{12,13... | collective-permute-start | bytes 1671176 | tf_op jit(solution)/shard_map/ppermute | solution.py:26
  33.6 3.3 %collective-permute-start.12 = (bf16[256,1024]{1,0:T(8,128)(2,1)S(1)}, bf16[256,1024]{1,0:T(8,128)(2,1)S(1)}, u32[]{:S(2)}, u32[]{:S(2)}) collective-permute-start(bf16[256,1024]{1,0:T(8,128)(2,1)S(1)} %get-tuple-element.29.refs_1_), channel_id=1, source_target_pairs={{0,1},{1,0},{4,5},{5,4},{2,3},{3,2},{6,7},{7,6},{8,9},{9,8},{12,13... | collective-permute-start | bytes 1572872 | tf_op jit(solution)/shard_map/ppermute | solution.py:26
  33.7 14.0 %collective-permute-start.9 = (bf16[272,1024]{1,0:T(8,128)(2,1)S(1)}, bf16[272,1024]{1,0:T(8,128)(2,1)S(1)}, u32[]{:S(2)}, u32[]{:S(2)}) collective-permute-start(bf16[272,1024]{1,0:T(8,128)(2,1)S(1)} %get-tuple-element.30.refs_4_), channel_id=1, source_target_pairs={{0,24},{1,97},{4,28},{5,101},{2,26},{3,99},{6,30},{7,103},{8,0},{9... | collective-permute-start | bytes 1671176 | tf_op jit(solution)/shard_map/ppermute | solution.py:26
  37.0 10.7 %collective-permute-start.8 = (bf16[256,1024]{1,0:T(8,128)(2,1)S(1)}, bf16[256,1024]{1,0:T(8,128)(2,1)S(1)}, u32[]{:S(2)}, u32[]{:S(2)}) collective-permute-start(bf16[256,1024]{1,0:T(8,128)(2,1)S(1)} %get-tuple-element.29.refs_1_), channel_id=1, source_target_pairs={{0,8},{1,33},{4,12},{5,37},{2,10},{3,35},{6,14},{7,39},{8,16},{9,4... | collective-permute-start | bytes 1572872 | tf_op jit(solution)/shard_map/ppermute | solution.py:26
  37.0 11.3 %collective-permute-start.16 = (bf16[272,1024]{1,0:T(8,128)(2,1)S(1)}, bf16[272,1024]{1,0:T(8,128)(2,1)S(1)}, u32[]{:S(2)}, u32[]{:S(2)}) collective-permute-start(bf16[272,1024]{1,0:T(8,128)(2,1)S(1)} %get-tuple-element.31.refs_2_), channel_id=1, source_target_pairs={{0,1},{1,0},{4,5},{5,4},{2,3},{3,2},{6,7},{7,6},{8,9},{9,8},{12,13... | collective-permute-start | bytes 1671176 | tf_op jit(solution)/shard_map/ppermute | solution.py:26
  39.7 8.6 %collective-permute-start.17 = (bf16[256,1024]{1,0:T(8,128)(2,1)S(1)}, bf16[256,1024]{1,0:T(8,128)(2,1)S(1)}, u32[]{:S(2)}, u32[]{:S(2)}) collective-permute-start(bf16[256,1024]{1,0:T(8,128)(2,1)S(1)} %get-tuple-element.32.refs_3_), channel_id=1, source_target_pairs={{0,1},{1,0},{4,5},{5,4},{2,3},{3,2},{6,7},{7,6},{8,9},{9,8},{12,13... | collective-permute-start | bytes 1572872 | tf_op jit(solution)/shard_map/ppermute | solution.py:26
  47.7 6.8 %collective-permute-start.15 = (bf16[272,1024]{1,0:T(8,128)(2,1)S(1)}, bf16[272,1024]{1,0:T(8,128)(2,1)S(1)}, u32[]{:S(2)}, u32[]{:S(2)}) collective-permute-start(bf16[272,1024]{1,0:T(8,128)(2,1)S(1)} %get-tuple-element.36.refs_2_), channel_id=1, source_target_pairs={{0,1},{1,0},{4,5},{5,4},{2,3},{3,2},{6,7},{7,6},{8,9},{9,8},{12,13... | collective-permute-start | bytes 1671176 | tf_op jit(solution)/shard_map/ppermute | solution.py:26
  48.0 6.4 %collective-permute-start.14 = (bf16[256,1024]{1,0:T(8,128)(2,1)S(1)}, bf16[256,1024]{1,0:T(8,128)(2,1)S(1)}, u32[]{:S(2)}, u32[]{:S(2)}) collective-permute-start(bf16[256,1024]{1,0:T(8,128)(2,1)S(1)} %get-tuple-element.35.refs_1_), channel_id=1, source_target_pairs={{0,1},{1,0},{4,5},{5,4},{2,3},{3,2},{6,7},{7,6},{8,9},{9,8},{12,13... | collective-permute-start | bytes 1572872 | tf_op jit(solution)/shard_map/ppermute | solution.py:26
  61.1 8.6 %collective-permute-start.18 = (f32[192,2048]{1,0:T(8,128)S(1)}, f32[192,2048]{1,0:T(8,128)S(1)}, u32[]{:S(2)}, u32[]{:S(2)}) collective-permute-start(f32[192,2048]{1,0:T(8,128)S(1)} %get-tuple-element.43), channel_id=1, source_target_pairs={{0,1},{1,0},{4,5},{5,4},{2,3},{3,2},{6,7},{7,6},{8,9},{9,8},{12,13... | collective-permute-start | bytes 4718600 | tf_op jit(solution)/shard_map/ppermute | solution.py:26
  61.5 16.0 %collective-permute-start.19 = (bf16[1024,256]{1,0:T(8,128)(2,1)}, bf16[1024,256]{1,0:T(8,128)(2,1)S(1)}, u32[]{:S(2)}, u32[]{:S(2)}) collective-permute-start(bf16[1024,256]{1,0:T(8,128)(2,1)} %get-tuple-element.44), channel_id=1, source_target_pairs={{0,3},{1,5},{4,2},{5,6},{2,1},{3,7},{6,0},{7,4},{8,11},{9,13},{12,... | collective-permute-start | bytes 1572872 | tf_op jit(solution)/shard_map/ppermute | solution.py:26
  62.5 15.4 %collective-permute-start.20 = (bf16[1024,256]{1,0:T(8,128)(2,1)}, bf16[1024,256]{1,0:T(8,128)(2,1)S(1)}, u32[]{:S(2)}, u32[]{:S(2)}) collective-permute-start(bf16[1024,256]{1,0:T(8,128)(2,1)} %get-tuple-element.45), channel_id=1, source_target_pairs={{0,1},{1,7},{4,0},{5,4},{2,3},{3,5},{6,2},{7,6},{8,9},{9,15},{12,8... | collective-permute-start | bytes 1572872 | tf_op jit(solution)/shard_map/ppermute | solution.py:26
  64.9 23.7 %collective-permute-start.21 = (bf16[1024,256]{1,0:T(8,128)(2,1)}, bf16[1024,256]{1,0:T(8,128)(2,1)S(1)}, u32[]{:S(2)}, u32[]{:S(2)}) collective-permute-start(bf16[1024,256]{1,0:T(8,128)(2,1)} %get-tuple-element.46), channel_id=1, source_target_pairs={{0,2},{1,4},{4,3},{5,7},{2,0},{3,6},{6,1},{7,5},{8,10},{9,12},{12,... | collective-permute-start | bytes 1572872 | tf_op jit(solution)/shard_map/ppermute | solution.py:26
  65.9 22.7 %collective-permute-start.22 = (bf16[1024,256]{1,0:T(8,128)(2,1)}, bf16[1024,256]{1,0:T(8,128)(2,1)S(1)}, u32[]{:S(2)}, u32[]{:S(2)}) collective-permute-start(bf16[1024,256]{1,0:T(8,128)(2,1)} %get-tuple-element.47), channel_id=1, source_target_pairs={{0,0},{1,6},{4,1},{5,5},{2,2},{3,4},{6,3},{7,7},{8,8},{9,14},{12,9... | collective-permute-start | bytes 1572872 | tf_op jit(solution)/shard_map/ppermute | solution.py:26
  71.4 18.9 %all-to-all-start = ((bf16[16,192,128]{2,1,0:T(8,128)(2,1)}), bf16[16,192,128]{2,1,0:T(8,128)(2,1)S(1)}, u32[]{:S(2)}, u32[]{:S(2)}) async-start(bf16[16,192,128]{2,1,0:T(8,128)(2,1)} %pack.1), calls=%async_computation | async-start | bytes 1572864 | tf_op jit(solution)/shard_map/all_to_all | solution.py:315
  77.5 12.9 %copy-start = (bf16[192,1024]{1,0:T(8,128)(2,1)S(1)}, bf16[192,1024]{1,0:T(8,128)(2,1)}, u32[]{:S(2)}) copy-start(bf16[192,1024]{1,0:T(8,128)(2,1)} %dec_ref.1) | copy-start | bytes 1179652

commit v6 on v5

--- a/solution.py
+++ b/solution.py
@@ -12,7 +12,7 @@
 BF16, F32, I32 = jnp.bfloat16, jnp.float32, jnp.int32
 TAIL = 16
 HALF = 512
-VMEM_LIMIT = 16 * 2**20
+VMEM_LIMIT = 12 * 2**20
 OFFSETS = (0, 3, 1, 2)
 
 
@@ -96,17 +96,12 @@
         outs, grads = refs[:1], refs[1]
     else:
         grads, refs = refs[-1], refs[:-1]
-        total_ref, enc_ref, refs = refs[0], refs[1], refs[2:]
+        total_ref, wet_ref, refs = refs[0], refs[1], refs[2:]
         if stage == 3:
             refs, (narrow, out_sems) = refs[:-2], refs[-2:]
-        if stage == 1:
-            early, encs, wet_ref, outs = refs[0], refs[1:3], refs[3], refs[4:]
-            encode(w_ref, enc_ref, wet_ref)
-        else:
-            wet_ref = enc_ref
-            named = sorted({out for out, _ in enc_at})
-            refs = refs[len(named) :]
-            encs, outs = dict(zip(named, refs)), refs[len(named) :]
+        named = sorted({out for out, _ in enc_at})
+        refs = refs[len(named) :]
+        encs, outs = dict(zip(named, refs)), refs[len(named) :]
     for i in range(n):
         low, high = q_refs[2 * i : 2 * i + 2]
         q_all[512 * i : 512 * i + 256, :] = low[...]
@@ -145,34 +140,28 @@
             narrow[o] = whole.astype(BF16)
             copies.append(pltpu.make_async_copy(narrow.at[o], outs[o], out_sems.at[o]))
             copies[-1].start()
-    both = [(grads, enc_at)] + ([(early, ((0, 0), (1, 0)))] if stage == 1 else [])
-    for values, to in both:
-        encoded = jnp.dot(wet_ref[...], values[...], preferred_element_type=F32)
-        encoded = encoded[:192] + encoded[192:]
-        for i, (out, column) in enumerate(to):
-            encs[out][:, column : column + 512] = encoded[:, 512 * i : 512 * i + 512]
+    encoded = jnp.dot(wet_ref[...], grads[...], preferred_element_type=F32)
+    encoded = encoded[:192] + encoded[192:]
+    for i, (out, column) in enumerate(enc_at):
+        encs[out][:, column : column + 512] = encoded[:, 512 * i : 512 * i + 512]
     if stage == 3:
         for copy in copies:
             copy.wait()
 
 
-def chunk(stage, place, groups, enc_at, w, scale, total=None, enc=None, early=None, sums=()):
+def chunk(stage, place, groups, enc_at, w, scale, total=None, wet=None, sums=()):
     vmem = pl.BlockSpec(memory_space=pltpu.VMEM)
     labels, n = 2 * HALF, 512 * len(enc_at)
-    named = sorted({out for out, _ in enc_at}) if stage > 1 else [0, 1]
-    args = [place, *sum(groups, []), w] + ([total, enc] if stage else [])
+    named = sorted({out for out, _ in enc_at})
+    args = [place, *sum(groups, []), w] + ([total, wet] if stage else [])
     at_total = len(args) - 2
     shapes, aliases = [], {}
     if stage:
         shapes = [jax.ShapeDtypeStruct((192, 2048), F32) for _ in named]
-    if stage == 1:
-        args.append(early)
-        shapes.append(jax.ShapeDtypeStruct((384, labels), BF16))
-    if stage > 1:
         aliases = {len(args) + i: i for i in range(len(named))}
         args += [sums[i] for i in named]
     if stage == 3:
-        shapes += [jax.ShapeDtypeStruct((labels, 256), BF16)] * 4
+        shapes += [pltpu.HBM((labels, 256), BF16)] * 4
     else:
         if stage:
             aliases[at_total] = len(shapes)
@@ -204,6 +193,14 @@
     return ([new[0], new[1]], *out[len(named) :])
 
 
+def early_kernel(w_ref, enc_ref, grads_ref, own_ref, sib_ref, wet_ref):
+    encode(w_ref, enc_ref, wet_ref)
+    encoded = jnp.dot(wet_ref[...], grads_ref[...], preferred_element_type=F32)
+    encoded = encoded[:192] + encoded[192:]
+    own_ref[:, :512] = encoded[:, :512]
+    sib_ref[:, :512] = encoded[:, 512:]
+
+
 def pack_kernel(place, *refs):
     own, sib, out = refs
     z, y, core = place[0], place[1], place[3]
@@ -279,7 +276,7 @@
 
     place = jnp.stack([z, y, 2 * xh + xl, core]).astype(I32)
     w = move(weights, to_user)
-    back, ahead, far = (move(block, hop(0, step)) for step in (1, -1, 2))
+    far, ahead, back = (move(block, hop(0, step)) for step in (2, -1, 1))
     half_shapes = (((256, 1024), BF16), ((256 + TAIL, 1024), BF16))
     low, high = kernel(rows_kernel, half_shapes, place, block, back, ahead, far, name="rows")
     low_back, high_ahead = move(low, hop(1, 1)), move(high, hop(1, -1))
@@ -288,26 +285,30 @@
     row, own, sib = [low, high], 0, 1
     rows = [row, [sibling(low), sibling(high)]]
     total, early_grads = chunk(0, place, rows, ((own, 0), (sib, 0)), w, scale)
+    sums_wet = kernel(
+        early_kernel,
+        (((192, 2048), F32), ((192, 2048), F32), ((384, 2 * HALF), BF16)),
+        w, encoder.T, early_grads, name="early", flops=2 * 1024 * 1024 * 512,
+    )
     low_back, high_ahead = after([low_back, high_ahead], early_grads)
     far = [move(low_back, hop(1, 1)), move(high_ahead, hop(1, -1))]
     early = [sibling(low_back), sibling(high_ahead)]
-    high_back, low_ahead = after([high_back, low_ahead], *early)
+    high_back, low_ahead = after([high_back, low_ahead], *early, sums_wet[2])
     late = [sibling(high_back), sibling(low_ahead)]
     back, ahead = [low_back, high_back], [low_ahead, high_ahead]
-    sums, wet, total = chunk(
-        1, place, [back, ahead], ((own, 512), (own, 1024)), w, scale, total, encoder.T, early_grads
-    )
+    sums, wet = sums_wet[:2], sums_wet[2]
+    sums, total = chunk(1, place, [back, ahead], ((own, 512), (own, 1024)), w, scale, total, wet, sums)
     far = after(far, sums[own])
     back, ahead = [early[0], late[0]], [late[1], early[1]]
-    sums, total = chunk(2, place, [back, ahead], ((sib, 512), (sib, 1024)), w, scale, total, wet, None, sums)
+    sums, total = chunk(2, place, [back, ahead], ((sib, 512), (sib, 1024)), w, scale, total, wet, sums)
     far_sib = [sibling(f) for f in far]
-    sums, *outs = chunk(3, place, [far, far_sib], ((own, 1536), (sib, 1536)), w, scale, total, wet, None, sums)
+    sums, *outs = chunk(3, place, [far, far_sib], ((own, 1536), (sib, 1536)), w, scale, total, wet, sums)
 
     pick = lambda same, other: lambda z, y, x, c: same(z, y, x, c) if c == x % 2 else other(z, y, x, c)
     got = [
         move(outs[0], pick(lambda z, y, x, c: (z, y, x + 2, 1 - c), lambda z, y, x, c: (z, y, x + 1, c))),
+        move(outs[2], pick(lambda z, y, x, c: (z, y, x + 2, c), lambda z, y, x, c: (z, y, x + 1, 1 - c))),
         move(outs[1], pick(to_sibling, lambda z, y, x, c: (z, y, x - 1, c))),
-        move(outs[2], pick(lambda z, y, x, c: (z, y, x + 2, c), lambda z, y, x, c: (z, y, x + 1, 1 - c))),
         move(outs[3], pick(lambda z, y, x, c: (z, y, x, c), lambda z, y, x, c: (z, y, x - 1, 1 - c))),
     ]
 

time: 91.9 us -> 90.6 us (0.986)
  starting transfers between devices: 36.9 us -> 35.5 us
    pallas_call x4 -> x5, Pallas kernels: 4.51 us -> 6.18 us  [kernel(): pl.pallas_call(body, in_specs=[pl.BlockSpec(memory_space=place(a)) for a...]
    pallas_call x4, Pallas kernels: 25.9 us -> 24.4 us  [chunk(): pl.pallas_call(functools.partial(chunk_kernel, enc_at, stage, scale), in_...]
    ppermute x23, starting transfers between devices: 30.8 us -> 29.5 us  [move(): return lax.ppermute(array, AXES, pairs(target))]
where the time goes in v6:
time: 90.6 us; the launch traced here: 90.3 us
  starting transfers between devices  35.5 us (39%)
  Pallas kernels  30.6 us (34%)
  waiting for transfers between devices  21.5 us (24%)
  other arithmetic  1.84 us (2%)
    ppermute x23, starting transfers between devices, move(): return lax.ppermute(array, AXES, pairs(target))  29.5 us
    pallas_call x4, Pallas kernels, chunk(): pl.pallas_call(functools.partial(chunk_kernel, enc_at, stage, scale), in_...  24.4 us
    ppermute x23, waiting for transfers between devices, move(): return lax.ppermute(array, AXES, pairs(target))  21.5 us
    pallas_call x5, Pallas kernels, kernel(): pl.pallas_call(body, in_specs=[pl.BlockSpec(memory_space=place(a)) for a...  6.18 us
    all_to_all x1, starting transfers between devices, shards(): lax.all_to_all(packed, ('z', 'y'), split_axis=0, concat_axis=0, tiled=True)  6.01 us
  transfers between devices with their start and end apart: 24, of which 8 were waited for; matrix products, arithmetic and copies ran while one was open for 2% of the time, Pallas kernels for 25%

profile of v6, /device:TPU:1, one launch (start us, length us, event | category | flops | bytes accessed | tf_op | source)
XLA Modules:
  0.0 90.3 jit_solution(2340138834595711039)
XLA Ops:
  0.6 1.5 %collective-permute-start.7 = (bf16[1024,1024]{1,0:T(8,128)(2,1)}, bf16[1024,1024]{1,0:T(8,128)(2,1)S(1)}, u32[]{:S(2)}, u32[]{:S(2)}) collective-permute-start(bf16[1024,1024]{1,0:T(8,128)(2,1)} %param.9), channel_id=1, source_target_pairs={{0,4},{1,0},{4,5},{5,1},{2,6},{3,2},{6,7},{7,3},{8,12},{9,8},{12,1... | collective-permute-start | bytes 6291464 | tf_op jit(solution)/shard_map/ppermute | solution.py:26
  2.1 0.1 pad.3.clone
  2.2 0.7 fusion
  2.9 1.1 %maximum_maximum_fusion.own_ref = bf16[144,1024]{1,0:T(8,128)(2,1)S(1)} fusion(bf16[1,1024]{1,0:T(2,128)(2,1)S(1)} %get-tuple-element.54, bf16[1,1024]{1,0:T(2,128)(2,1)S(1)} %get-tuple-element.55, bf16[128,1024]{1,0:T(8,128)(2,1)} %param.6, bf16[144]{0:T(256)(128)(2,1)S(1)} %pad.3.clone), kind=kLoop, calls=%fused_computation | loop fusion | flops 1179648 | bytes 561440 | tf_op jit(solution)/shard_map/concatenate | solution.py:275
  4.0 1.4 %collective-permute-start = (bf16[144,1024]{1,0:T(8,128)(2,1)S(1)}, bf16[144,1024]{1,0:T(8,128)(2,1)S(1)}, u32[]{:S(2)}, u32[]{:S(2)}) collective-permute-start(bf16[144,1024]{1,0:T(8,128)(2,1)S(1)} %maximum_maximum_fusion.own_ref), channel_id=1, source_target_pairs={{0,32},{1,9},{4,36},{5,13},{2,34},{3,11},{6,38},{7,15},{8,40},{9,1... | collective-permute-start | bytes 884744 | tf_op jit(solution)/shard_map/ppermute | solution.py:26
  5.4 1.5 %collective-permute-start.1 = (bf16[144,1024]{1,0:T(8,128)(2,1)S(1)}, bf16[144,1024]{1,0:T(8,128)(2,1)S(1)}, u32[]{:S(2)}, u32[]{:S(2)}) collective-permute-start(bf16[144,1024]{1,0:T(8,128)(2,1)S(1)} %maximum_maximum_fusion.own_ref), channel_id=1, source_target_pairs={{0,96},{1,25},{4,100},{5,29},{2,98},{3,27},{6,102},{7,31},{8,104},... | collective-permute-start | bytes 884744 | tf_op jit(solution)/shard_map/ppermute | solution.py:26
  7.0 1.6 %collective-permute-start.2 = (bf16[144,1024]{1,0:T(8,128)(2,1)S(1)}, bf16[144,1024]{1,0:T(8,128)(2,1)S(1)}, u32[]{:S(2)}, u32[]{:S(2)}) collective-permute-start(bf16[144,1024]{1,0:T(8,128)(2,1)S(1)} %maximum_maximum_fusion.own_ref), channel_id=1, source_target_pairs={{0,64},{1,17},{4,68},{5,21},{2,66},{3,19},{6,70},{7,23},{8,72},{9,... | collective-permute-start | bytes 884744 | tf_op jit(solution)/shard_map/ppermute | solution.py:26
  8.5 0.1 pad_add_fusion.place.refs_0_
  8.6 2.7 %collective-permute-done.back_ref = bf16[144,1024]{1,0:T(8,128)(2,1)S(1)} collective-permute-done((bf16[144,1024]{1,0:T(8,128)(2,1)S(1)}, bf16[144,1024]{1,0:T(8,128)(2,1)S(1)}, u32[]{:S(2)}, u32[]{:S(2)}) %collective-permute-start) | collective-permute-done | bytes 294944 | tf_op jit(solution)/shard_map/ppermute | solution.py:26
  11.3 2.5 %collective-permute-done.1.ahead_ref = bf16[144,1024]{1,0:T(8,128)(2,1)S(1)} collective-permute-done((bf16[144,1024]{1,0:T(8,128)(2,1)S(1)}, bf16[144,1024]{1,0:T(8,128)(2,1)S(1)}, u32[]{:S(2)}, u32[]{:S(2)}) %collective-permute-start.1) | collective-permute-done | bytes 294944 | tf_op jit(solution)/shard_map/ppermute | solution.py:26
  13.8 1.8 %collective-permute-done.2.far_ref = bf16[144,1024]{1,0:T(8,128)(2,1)S(1)} collective-permute-done((bf16[144,1024]{1,0:T(8,128)(2,1)S(1)}, bf16[144,1024]{1,0:T(8,128)(2,1)S(1)}, u32[]{:S(2)}, u32[]{:S(2)}) %collective-permute-start.2) | collective-permute-done | bytes 294944 | tf_op jit(solution)/shard_map/ppermute | solution.py:26
  15.6 0.6 rows.1
  16.3 3.4 %collective-permute-start.6 = (bf16[272,1024]{1,0:T(8,128)(2,1)S(1)}, bf16[272,1024]{1,0:T(8,128)(2,1)S(1)}, u32[]{:S(2)}, u32[]{:S(2)}) collective-permute-start(bf16[272,1024]{1,0:T(8,128)(2,1)S(1)} %get-tuple-element.28.refs_2_), channel_id=1, source_target_pairs={{0,1},{1,0},{4,5},{5,4},{2,3},{3,2},{6,7},{7,6},{8,9},{9,8},{12,13... | collective-permute-start | bytes 1671176 | tf_op jit(solution)/shard_map/ppermute | solution.py:26
  19.7 0.1 collective-permute-start.5
  19.8 1.6 %collective-permute-start.4 = (bf16[272,1024]{1,0:T(8,128)(2,1)S(1)}, bf16[272,1024]{1,0:T(8,128)(2,1)S(1)}, u32[]{:S(2)}, u32[]{:S(2)}) collective-permute-start(bf16[272,1024]{1,0:T(8,128)(2,1)S(1)} %get-tuple-element.28.refs_2_), channel_id=1, source_target_pairs={{0,24},{1,97},{4,28},{5,101},{2,26},{3,99},{6,30},{7,103},{8,0},{9... | collective-permute-start | bytes 1671176 | tf_op jit(solution)/shard_map/ppermute | solution.py:26
  21.4 0.0 collective-permute-start.3
  21.4 0.7 collective-permute-done.5.refs_3_
  22.0 1.1 %collective-permute-start.10 = (bf16[272,1024]{1,0:T(8,128)(2,1)S(1)}, bf16[272,1024]{1,0:T(8,128)(2,1)S(1)}, u32[]{:S(2)}, u32[]{:S(2)}) collective-permute-start(bf16[272,1024]{1,0:T(8,128)(2,1)S(1)} %get-tuple-element.28.refs_2_), channel_id=1, source_target_pairs={{0,8},{1,33},{4,12},{5,37},{2,10},{3,35},{6,14},{7,39},{8,16},{9,4... | collective-permute-start | bytes 1671176 | tf_op jit(solution)/shard_map/ppermute | solution.py:26
  23.2 0.0 collective-permute-done.6.refs_4_
  23.2 1.5 %collective-permute-start.11 = (bf16[256,1024]{1,0:T(8,128)(2,1)S(1)}, bf16[256,1024]{1,0:T(8,128)(2,1)S(1)}, u32[]{:S(2)}, u32[]{:S(2)}) collective-permute-start(bf16[256,1024]{1,0:T(8,128)(2,1)S(1)} %get-tuple-element.27.refs_1_), channel_id=1, source_target_pairs={{0,24},{1,97},{4,28},{5,101},{2,26},{3,99},{6,30},{7,103},{8,0},{9... | collective-permute-start | bytes 1572872 | tf_op jit(solution)/shard_map/ppermute | solution.py:26
  24.7 2.0 %collective-permute-done.7.refs_5_.w_ref = bf16[1024,1024]{1,0:T(8,128)(2,1)S(1)} collective-permute-done((bf16[1024,1024]{1,0:T(8,128)(2,1)}, bf16[1024,1024]{1,0:T(8,128)(2,1)S(1)}, u32[]{:S(2)}, u32[]{:S(2)}) %collective-permute-start.7) | collective-permute-done | bytes 2097184 | tf_op jit(solution)/shard_map/ppermute | solution.py:26
  26.7 5.4 %chunk.4 = (f32[4,1024,256]{2,1,0:T(8,128)S(1)}, bf16[1024,1024]{1,0:T(8,128)(2,1)S(1)}) custom-call(s32[4]{0:T(128)S(1)} %pad_add_fusion.place.refs_0_, bf16[256,1024]{1,0:T(8,128)(2,1)S(1)} %get-tuple-element.27.refs_1_, bf16[272,1024]{1,0:T(8,128)(2,1)S(1)} %get-tuple-element.28.refs_2_, bf16[256,1024]{1,0:T(8,128)(2,1)S(1)} %collective-permute-done.5.refs_3_, ...), custom_call_target="tpu_custom_call" | custom-call | flops 5100273664 | bytes 1048576 | tf_op jit(solution)/shard_map/chunk/pallas_call | solution.py:177
  32.1 0.0 collective-permute-done.3.refs_0_
  32.1 0.0 collective-permute-done.4.refs_1_
  32.1 0.0 copy-start
  32.1 1.5 %collective-permute-start.13 = (bf16[272,1024]{1,0:T(8,128)(2,1)S(1)}, bf16[272,1024]{1,0:T(8,128)(2,1)S(1)}, u32[]{:S(2)}, u32[]{:S(2)}) collective-permute-start(bf16[272,1024]{1,0:T(8,128)(2,1)S(1)} %get-tuple-element.31.refs_4_), channel_id=1, source_target_pairs={{0,1},{1,0},{4,5},{5,4},{2,3},{3,2},{6,7},{7,6},{8,9},{9,8},{12,13... | collective-permute-start | bytes 1671176 | tf_op jit(solution)/shard_map/ppermute | solution.py:26
  33.6 0.1 collective-permute-start.12
  33.7 3.2 %collective-permute-start.9 = (bf16[272,1024]{1,0:T(8,128)(2,1)S(1)}, bf16[272,1024]{1,0:T(8,128)(2,1)S(1)}, u32[]{:S(2)}, u32[]{:S(2)}) collective-permute-start(bf16[272,1024]{1,0:T(8,128)(2,1)S(1)} %get-tuple-element.31.refs_4_), channel_id=1, source_target_pairs={{0,24},{1,97},{4,28},{5,101},{2,26},{3,99},{6,30},{7,103},{8,0},{9... | collective-permute-start | bytes 1671176 | tf_op jit(solution)/shard_map/ppermute | solution.py:26
  36.9 0.0 collective-permute-done.11.refs_1_
  37.0 0.0 collective-permute-start.8
  37.0 0.0 copy-done
  37.0 1.7 %early.1 = (f32[192,2048]{1,0:T(8,128)S(1)}, f32[192,2048]{1,0:T(8,128)S(1)}, bf16[384,1024]{1,0:T(8,128)(2,1)S(1)}) custom-call(bf16[1024,1024]{1,0:T(8,128)(2,1)S(1)} %collective-permute-done.7.refs_5_.w_ref, bf16[192,1024]{1,0:T(8,128)(2,1)S(1)} %bitcast.25, bf16[1024,1024]{1,0:T(8,128)(2,1)S(1)} %get-tuple-element.29.refs_2_.grads_ref), custom_call_target="tpu_custom_call" | custom-call | flops 1073741824 | bytes 1024 | tf_op jit(solution)/shard_map/early/pallas_call | solution.py:240
  38.6 0.0 collective-permute-done.10.refs_0_
  38.6 0.0 collective-permute-done.12.refs_2_.refs_1_
  38.7 0.0 collective-permute-done.13.refs_3_.refs_4_
  38.7 1.0 %collective-permute-start.16 = (bf16[272,1024]{1,0:T(8,128)(2,1)S(1)}, bf16[272,1024]{1,0:T(8,128)(2,1)S(1)}, u32[]{:S(2)}, u32[]{:S(2)}) collective-permute-start(bf16[272,1024]{1,0:T(8,128)(2,1)S(1)} %get-tuple-element.33.refs_2_), channel_id=1, source_target_pairs={{0,1},{1,0},{4,5},{5,4},{2,3},{3,2},{6,7},{7,6},{8,9},{9,8},{12,13... | collective-permute-start | bytes 1671176 | tf_op jit(solution)/shard_map/ppermute | solution.py:26
  39.7 0.3 collective-permute-start.17
  40.0 6.2 %chunk.5 = (f32[192,2048]{1,0:T(8,128)S(1)}, f32[4,1024,256]{2,1,0:T(8,128)S(1)}) custom-call(s32[4]{0:T(128)S(1)} %pad_add_fusion.place.refs_0_, bf16[256,1024]{1,0:T(8,128)(2,1)S(1)} %get-tuple-element.30.refs_1_, bf16[272,1024]{1,0:T(8,128)(2,1)S(1)} %get-tuple-element.33.refs_2_, ...), custom_call_target="tpu_custom_call", output_to_operand_aliasing={{0}: (8, {}), {1}: (6, {})} | custom-call | flops 5100273664 | bytes 1048576 | tf_op jit(solution)/shard_map/chunk/pallas_call | solution.py:177
  46.1 0.4 collective-permute-done.8.refs_0_
  46.5 0.0 collective-permute-done.9.refs_1_
  46.5 0.5 collective-permute-start.15
  47.0 0.1 collective-permute-start.14
  47.1 0.0 collective-permute-done.17.refs_3_
  47.1 0.0 collective-permute-done.16.refs_2_
  47.1 6.2 %chunk.6 = (f32[192,2048]{1,0:T(8,128)S(1)}, f32[4,1024,256]{2,1,0:T(8,128)S(1)}) custom-call(s32[4]{0:T(128)S(1)} %pad_add_fusion.place.refs_0_, bf16[256,1024]{1,0:T(8,128)(2,1)S(1)} %collective-permute-done.12.refs_2_.refs_1_, bf16[272,1024]{1,0:T(8,128)(2,1)S(1)} %collective-permute-done.16.refs_2_, ...), custom_call_target="tpu_custom_call", output_to_operand_aliasing={{0}: (8, {}), {1}: (6, {})} | custom-call | flops 5100273664 | bytes 1048576 | tf_op jit(solution)/shard_map/chunk/pallas_call | solution.py:177
  53.3 0.0 collective-permute-done.14.refs_3_
  53.3 0.0 collective-permute-done.15.refs_4_
  53.3 6.6 %chunk.7 = (f32[192,2048]{1,0:T(8,128)S(1)}, f32[192,2048]{1,0:T(8,128)S(1)}, bf16[1024,256]{1,0:T(8,128)(2,1)}, bf16[1024,256]{1,0:T(8,128)(2,1)}, bf16[1024,25...) custom-call(s32[4]{0:T(128)S(1)} %pad_add_fusion.place.refs_0_, ...), custom_call_target="tpu_custom_call", output_to_operand_aliasing={{0}: (8, {}), {1}: (9, {})} | custom-call | flops 5100273664 | bytes 1048576 | tf_op jit(solution)/shard_map/chunk/pallas_call | solution.py:177
  59.9 0.5 collective-permute-start.18
  60.5 2.1 %collective-permute-start.19 = (bf16[1024,256]{1,0:T(8,128)(2,1)}, bf16[1024,256]{1,0:T(8,128)(2,1)S(1)}, u32[]{:S(2)}, u32[]{:S(2)}) collective-permute-start(bf16[1024,256]{1,0:T(8,128)(2,1)} %get-tuple-element.46), channel_id=1, source_target_pairs={{0,3},{1,5},{4,2},{5,6},{2,1},{3,7},{6,0},{7,4},{8,11},{9,13},{12,... | collective-permute-start | bytes 1572872 | tf_op jit(solution)/shard_map/ppermute | solution.py:26
  62.6 0.3 collective-permute-start.20
  62.8 3.9 %collective-permute-start.21 = (bf16[1024,256]{1,0:T(8,128)(2,1)}, bf16[1024,256]{1,0:T(8,128)(2,1)S(1)}, u32[]{:S(2)}, u32[]{:S(2)}) collective-permute-start(bf16[1024,256]{1,0:T(8,128)(2,1)} %get-tuple-element.48), channel_id=1, source_target_pairs={{0,1},{1,7},{4,0},{5,4},{2,3},{3,5},{6,2},{7,6},{8,9},{9,15},{12,8... | collective-permute-start | bytes 1572872 | tf_op jit(solution)/shard_map/ppermute | solution.py:26
  66.8 2.1 %collective-permute-start.22 = (bf16[1024,256]{1,0:T(8,128)(2,1)}, bf16[1024,256]{1,0:T(8,128)(2,1)S(1)}, u32[]{:S(2)}, u32[]{:S(2)}) collective-permute-start(bf16[1024,256]{1,0:T(8,128)(2,1)} %get-tuple-element.49), channel_id=1, source_target_pairs={{0,0},{1,6},{4,1},{5,5},{2,2},{3,4},{6,3},{7,7},{8,8},{9,14},{12,9... | collective-permute-start | bytes 1572872 | tf_op jit(solution)/shard_map/ppermute | solution.py:26
  68.9 0.0 collective-permute-done.18.refs_1_
  68.9 1.6 %pack.1 = bf16[16,192,128]{2,1,0:T(8,128)(2,1)} custom-call(s32[4]{0:T(128)S(1)} %pad_add_fusion.place.refs_0_, f32[192,2048]{1,0:T(8,128)S(1)} %get-tuple-element.44.refs_0_, f32[192,2048]{1,0:T(8,128)S(1)} %collective-permute-done.18.refs_1_), custom_call_target="tpu_custom_call" | custom-call | flops 1000000 | bytes 1024 | tf_op jit(solution)/shard_map/pack/pallas_call | solution.py:240
  70.5 6.0 %all-to-all-start = ((bf16[16,192,128]{2,1,0:T(8,128)(2,1)}), bf16[16,192,128]{2,1,0:T(8,128)(2,1)S(1)}, u32[]{:S(2)}, u32[]{:S(2)}) async-start(bf16[16,192,128]{2,1,0:T(8,128)(2,1)} %pack.1), calls=%async_computation | async-start | bytes 1572864 | tf_op jit(solution)/shard_map/all_to_all | solution.py:316
  76.6 0.0 copy-start.1
  76.6 0.0 collective-permute-done.19.refs_0_
  76.6 11.0 %collective-permute-done.20.refs_1_ = bf16[1024,256]{1,0:T(8,128)(2,1)S(1)} collective-permute-done((bf16[1024,256]{1,0:T(8,128)(2,1)}, bf16[1024,256]{1,0:T(8,128)(2,1)S(1)}, u32[]{:S(2)}, u32[]{:S(2)}) %collective-permute-start.20) | collective-permute-done | bytes 524320 | tf_op jit(solution)/shard_map/ppermute | solution.py:26
  87.6 0.0 collective-permute-done.21.refs_2_
  87.6 0.4 collective-permute-done.22.refs_3_
  88.0 1.0 %join.1 = (bf16[1024,256]{1,0:T(8,128)(2,1)}, f32[8,128]{1,0:T(8,128)S(1)}) custom-call(bf16[1024,256]{1,0:T(8,128)(2,1)S(1)} %collective-permute-done.19.refs_0_, bf16[1024,256]{1,0:T(8,128)(2,1)S(1)} %collective-permute-done.20.refs_1_, bf16[1024,256]{1,0:T(8,128)(2,1)S(1)} %collective-permute-done.21.refs_2_, ...), custom_call_target="tpu_custom_call" | custom-call | flops 99999997952 | bytes 1024 | tf_op jit(solution)/shard_map/join/pallas_call | solution.py:240
  89.1 0.0 all-to-all-done.parts_ref
  89.1 1.2 %decode.1 = bf16[128,1024]{1,0:T(8,128)(2,1)} custom-call(bf16[16,192,128]{2,1,0:T(8,128)(2,1)S(1)} %all-to-all-done.parts_ref, bf16[192,1024]{1,0:T(8,128)(2,1)S(1)} %copy-done.1, f32[8,128]{1,0:T(8,128)S(1)} %get-tuple-element.50.after_ref), custom_call_target="tpu_custom_call" | custom-call | flops 1000000 | bytes 1024 | tf_op jit(solution)/shard_map/decode/pallas_call | solution.py:240
  (6 shorter events, 0.0 us)
Async XLA Ops:
  0.6 26.0 %collective-permute-start.7 = (bf16[1024,1024]{1,0:T(8,128)(2,1)}, bf16[1024,1024]{1,0:T(8,128)(2,1)S(1)}, u32[]{:S(2)}, u32[]{:S(2)}) collective-permute-start(bf16[1024,1024]{1,0:T(8,128)(2,1)} %param.9), channel_id=1, source_target_pairs={{0,4},{1,0},{4,5},{5,1},{2,6},{3,2},{6,7},{7,3},{8,12},{9,8},{12,1... | collective-permute-start | bytes 6291464 | tf_op jit(solution)/shard_map/ppermute | solution.py:26
  4.0 7.3 %collective-permute-start = (bf16[144,1024]{1,0:T(8,128)(2,1)S(1)}, bf16[144,1024]{1,0:T(8,128)(2,1)S(1)}, u32[]{:S(2)}, u32[]{:S(2)}) collective-permute-start(bf16[144,1024]{1,0:T(8,128)(2,1)S(1)} %maximum_maximum_fusion.own_ref), channel_id=1, source_target_pairs={{0,32},{1,9},{4,36},{5,13},{2,34},{3,11},{6,38},{7,15},{8,40},{9,1... | collective-permute-start | bytes 884744 | tf_op jit(solution)/shard_map/ppermute | solution.py:26
  5.4 8.3 %collective-permute-start.1 = (bf16[144,1024]{1,0:T(8,128)(2,1)S(1)}, bf16[144,1024]{1,0:T(8,128)(2,1)S(1)}, u32[]{:S(2)}, u32[]{:S(2)}) collective-permute-start(bf16[144,1024]{1,0:T(8,128)(2,1)S(1)} %maximum_maximum_fusion.own_ref), channel_id=1, source_target_pairs={{0,96},{1,25},{4,100},{5,29},{2,98},{3,27},{6,102},{7,31},{8,104},... | collective-permute-start | bytes 884744 | tf_op jit(solution)/shard_map/ppermute | solution.py:26
  7.0 8.7 %collective-permute-start.2 = (bf16[144,1024]{1,0:T(8,128)(2,1)S(1)}, bf16[144,1024]{1,0:T(8,128)(2,1)S(1)}, u32[]{:S(2)}, u32[]{:S(2)}) collective-permute-start(bf16[144,1024]{1,0:T(8,128)(2,1)S(1)} %maximum_maximum_fusion.own_ref), channel_id=1, source_target_pairs={{0,64},{1,17},{4,68},{5,21},{2,66},{3,19},{6,70},{7,23},{8,72},{9,... | collective-permute-start | bytes 884744 | tf_op jit(solution)/shard_map/ppermute | solution.py:26
  16.3 6.9 %collective-permute-start.6 = (bf16[272,1024]{1,0:T(8,128)(2,1)S(1)}, bf16[272,1024]{1,0:T(8,128)(2,1)S(1)}, u32[]{:S(2)}, u32[]{:S(2)}) collective-permute-start(bf16[272,1024]{1,0:T(8,128)(2,1)S(1)} %get-tuple-element.28.refs_2_), channel_id=1, source_target_pairs={{0,1},{1,0},{4,5},{5,4},{2,3},{3,2},{6,7},{7,6},{8,9},{9,8},{12,13... | collective-permute-start | bytes 1671176 | tf_op jit(solution)/shard_map/ppermute | solution.py:26
  19.7 2.3 %collective-permute-start.5 = (bf16[256,1024]{1,0:T(8,128)(2,1)S(1)}, bf16[256,1024]{1,0:T(8,128)(2,1)S(1)}, u32[]{:S(2)}, u32[]{:S(2)}) collective-permute-start(bf16[256,1024]{1,0:T(8,128)(2,1)S(1)} %get-tuple-element.27.refs_1_), channel_id=1, source_target_pairs={{0,1},{1,0},{4,5},{5,4},{2,3},{3,2},{6,7},{7,6},{8,9},{9,8},{12,13... | collective-permute-start | bytes 1572872 | tf_op jit(solution)/shard_map/ppermute | solution.py:26
  19.8 12.3 %collective-permute-start.4 = (bf16[272,1024]{1,0:T(8,128)(2,1)S(1)}, bf16[272,1024]{1,0:T(8,128)(2,1)S(1)}, u32[]{:S(2)}, u32[]{:S(2)}) collective-permute-start(bf16[272,1024]{1,0:T(8,128)(2,1)S(1)} %get-tuple-element.28.refs_2_), channel_id=1, source_target_pairs={{0,24},{1,97},{4,28},{5,101},{2,26},{3,99},{6,30},{7,103},{8,0},{9... | collective-permute-start | bytes 1671176 | tf_op jit(solution)/shard_map/ppermute | solution.py:26
  21.4 10.7 %collective-permute-start.3 = (bf16[256,1024]{1,0:T(8,128)(2,1)S(1)}, bf16[256,1024]{1,0:T(8,128)(2,1)S(1)}, u32[]{:S(2)}, u32[]{:S(2)}) collective-permute-start(bf16[256,1024]{1,0:T(8,128)(2,1)S(1)} %get-tuple-element.27.refs_1_), channel_id=1, source_target_pairs={{0,8},{1,33},{4,12},{5,37},{2,10},{3,35},{6,14},{7,39},{8,16},{9,4... | collective-permute-start | bytes 1572872 | tf_op jit(solution)/shard_map/ppermute | solution.py:26
  22.0 16.6 %collective-permute-start.10 = (bf16[272,1024]{1,0:T(8,128)(2,1)S(1)}, bf16[272,1024]{1,0:T(8,128)(2,1)S(1)}, u32[]{:S(2)}, u32[]{:S(2)}) collective-permute-start(bf16[272,1024]{1,0:T(8,128)(2,1)S(1)} %get-tuple-element.28.refs_2_), channel_id=1, source_target_pairs={{0,8},{1,33},{4,12},{5,37},{2,10},{3,35},{6,14},{7,39},{8,16},{9,4... | collective-permute-start | bytes 1671176 | tf_op jit(solution)/shard_map/ppermute | solution.py:26
  23.2 13.8 %collective-permute-start.11 = (bf16[256,1024]{1,0:T(8,128)(2,1)S(1)}, bf16[256,1024]{1,0:T(8,128)(2,1)S(1)}, u32[]{:S(2)}, u32[]{:S(2)}) collective-permute-start(bf16[256,1024]{1,0:T(8,128)(2,1)S(1)} %get-tuple-element.27.refs_1_), channel_id=1, source_target_pairs={{0,24},{1,97},{4,28},{5,101},{2,26},{3,99},{6,30},{7,103},{8,0},{9... | collective-permute-start | bytes 1572872 | tf_op jit(solution)/shard_map/ppermute | solution.py:26
  32.1 4.9 %copy-start = (bf16[1024,192]{0,1:T(8,128)(2,1)S(1)}, bf16[1024,192]{0,1:T(8,128)(2,1)}, u32[]{:S(2)}) copy-start(bf16[1024,192]{0,1:T(8,128)(2,1)} %param.10) | copy-start | bytes 1179652
  32.1 6.5 %collective-permute-start.13 = (bf16[272,1024]{1,0:T(8,128)(2,1)S(1)}, bf16[272,1024]{1,0:T(8,128)(2,1)S(1)}, u32[]{:S(2)}, u32[]{:S(2)}) collective-permute-start(bf16[272,1024]{1,0:T(8,128)(2,1)S(1)} %get-tuple-element.31.refs_4_), channel_id=1, source_target_pairs={{0,1},{1,0},{4,5},{5,4},{2,3},{3,2},{6,7},{7,6},{8,9},{9,8},{12,13... | collective-permute-start | bytes 1671176 | tf_op jit(solution)/shard_map/ppermute | solution.py:26
  33.6 5.0 %collective-permute-start.12 = (bf16[256,1024]{1,0:T(8,128)(2,1)S(1)}, bf16[256,1024]{1,0:T(8,128)(2,1)S(1)}, u32[]{:S(2)}, u32[]{:S(2)}) collective-permute-start(bf16[256,1024]{1,0:T(8,128)(2,1)S(1)} %get-tuple-element.30.refs_1_), channel_id=1, source_target_pairs={{0,1},{1,0},{4,5},{5,4},{2,3},{3,2},{6,7},{7,6},{8,9},{9,8},{12,13... | collective-permute-start | bytes 1572872 | tf_op jit(solution)/shard_map/ppermute | solution.py:26
  33.7 12.8 %collective-permute-start.9 = (bf16[272,1024]{1,0:T(8,128)(2,1)S(1)}, bf16[272,1024]{1,0:T(8,128)(2,1)S(1)}, u32[]{:S(2)}, u32[]{:S(2)}) collective-permute-start(bf16[272,1024]{1,0:T(8,128)(2,1)S(1)} %get-tuple-element.31.refs_4_), channel_id=1, source_target_pairs={{0,24},{1,97},{4,28},{5,101},{2,26},{3,99},{6,30},{7,103},{8,0},{9... | collective-permute-start | bytes 1671176 | tf_op jit(solution)/shard_map/ppermute | solution.py:26
  37.0 9.5 %collective-permute-start.8 = (bf16[256,1024]{1,0:T(8,128)(2,1)S(1)}, bf16[256,1024]{1,0:T(8,128)(2,1)S(1)}, u32[]{:S(2)}, u32[]{:S(2)}) collective-permute-start(bf16[256,1024]{1,0:T(8,128)(2,1)S(1)} %get-tuple-element.30.refs_1_), channel_id=1, source_target_pairs={{0,8},{1,33},{4,12},{5,37},{2,10},{3,35},{6,14},{7,39},{8,16},{9,4... | collective-permute-start | bytes 1572872 | tf_op jit(solution)/shard_map/ppermute | solution.py:26
  38.7 8.4 %collective-permute-start.16 = (bf16[272,1024]{1,0:T(8,128)(2,1)S(1)}, bf16[272,1024]{1,0:T(8,128)(2,1)S(1)}, u32[]{:S(2)}, u32[]{:S(2)}) collective-permute-start(bf16[272,1024]{1,0:T(8,128)(2,1)S(1)} %get-tuple-element.33.refs_2_), channel_id=1, source_target_pairs={{0,1},{1,0},{4,5},{5,4},{2,3},{3,2},{6,7},{7,6},{8,9},{9,8},{12,13... | collective-permute-start | bytes 1671176 | tf_op jit(solution)/shard_map/ppermute | solution.py:26
  39.7 7.4 %collective-permute-start.17 = (bf16[256,1024]{1,0:T(8,128)(2,1)S(1)}, bf16[256,1024]{1,0:T(8,128)(2,1)S(1)}, u32[]{:S(2)}, u32[]{:S(2)}) collective-permute-start(bf16[256,1024]{1,0:T(8,128)(2,1)S(1)} %get-tuple-element.34.refs_3_), channel_id=1, source_target_pairs={{0,1},{1,0},{4,5},{5,4},{2,3},{3,2},{6,7},{7,6},{8,9},{9,8},{12,13... | collective-permute-start | bytes 1572872 | tf_op jit(solution)/shard_map/ppermute | solution.py:26
  46.5 6.8 %collective-permute-start.15 = (bf16[272,1024]{1,0:T(8,128)(2,1)S(1)}, bf16[272,1024]{1,0:T(8,128)(2,1)S(1)}, u32[]{:S(2)}, u32[]{:S(2)}) collective-permute-start(bf16[272,1024]{1,0:T(8,128)(2,1)S(1)} %get-tuple-element.39.refs_2_), channel_id=1, source_target_pairs={{0,1},{1,0},{4,5},{5,4},{2,3},{3,2},{6,7},{7,6},{8,9},{9,8},{12,13... | collective-permute-start | bytes 1671176 | tf_op jit(solution)/shard_map/ppermute | solution.py:26
  47.0 6.3 %collective-permute-start.14 = (bf16[256,1024]{1,0:T(8,128)(2,1)S(1)}, bf16[256,1024]{1,0:T(8,128)(2,1)S(1)}, u32[]{:S(2)}, u32[]{:S(2)}) collective-permute-start(bf16[256,1024]{1,0:T(8,128)(2,1)S(1)} %get-tuple-element.38.refs_1_), channel_id=1, source_target_pairs={{0,1},{1,0},{4,5},{5,4},{2,3},{3,2},{6,7},{7,6},{8,9},{9,8},{12,13... | collective-permute-start | bytes 1572872 | tf_op jit(solution)/shard_map/ppermute | solution.py:26
  59.9 9.0 %collective-permute-start.18 = (f32[192,2048]{1,0:T(8,128)S(1)}, f32[192,2048]{1,0:T(8,128)S(1)}, u32[]{:S(2)}, u32[]{:S(2)}) collective-permute-start(f32[192,2048]{1,0:T(8,128)S(1)} %get-tuple-element.45), channel_id=1, source_target_pairs={{0,1},{1,0},{4,5},{5,4},{2,3},{3,2},{6,7},{7,6},{8,9},{9,8},{12,13... | collective-permute-start | bytes 4718600 | tf_op jit(solution)/shard_map/ppermute | solution.py:26
  60.5 16.1 %collective-permute-start.19 = (bf16[1024,256]{1,0:T(8,128)(2,1)}, bf16[1024,256]{1,0:T(8,128)(2,1)S(1)}, u32[]{:S(2)}, u32[]{:S(2)}) collective-permute-start(bf16[1024,256]{1,0:T(8,128)(2,1)} %get-tuple-element.46), channel_id=1, source_target_pairs={{0,3},{1,5},{4,2},{5,6},{2,1},{3,7},{6,0},{7,4},{8,11},{9,13},{12,... | collective-permute-start | bytes 1572872 | tf_op jit(solution)/shard_map/ppermute | solution.py:26
  62.6 25.1 %collective-permute-start.20 = (bf16[1024,256]{1,0:T(8,128)(2,1)}, bf16[1024,256]{1,0:T(8,128)(2,1)S(1)}, u32[]{:S(2)}, u32[]{:S(2)}) collective-permute-start(bf16[1024,256]{1,0:T(8,128)(2,1)} %get-tuple-element.47), channel_id=1, source_target_pairs={{0,2},{1,4},{4,3},{5,7},{2,0},{3,6},{6,1},{7,5},{8,10},{9,12},{12,... | collective-permute-start | bytes 1572872 | tf_op jit(solution)/shard_map/ppermute | solution.py:26
  62.8 24.8 %collective-permute-start.21 = (bf16[1024,256]{1,0:T(8,128)(2,1)}, bf16[1024,256]{1,0:T(8,128)(2,1)S(1)}, u32[]{:S(2)}, u32[]{:S(2)}) collective-permute-start(bf16[1024,256]{1,0:T(8,128)(2,1)} %get-tuple-element.48), channel_id=1, source_target_pairs={{0,1},{1,7},{4,0},{5,4},{2,3},{3,5},{6,2},{7,6},{8,9},{9,15},{12,8... | collective-permute-start | bytes 1572872 | tf_op jit(solution)/shard_map/ppermute | solution.py:26
  66.8 21.2 %collective-permute-start.22 = (bf16[1024,256]{1,0:T(8,128)(2,1)}, bf16[1024,256]{1,0:T(8,128)(2,1)S(1)}, u32[]{:S(2)}, u32[]{:S(2)}) collective-permute-start(bf16[1024,256]{1,0:T(8,128)(2,1)} %get-tuple-element.49), channel_id=1, source_target_pairs={{0,0},{1,6},{4,1},{5,5},{2,2},{3,4},{6,3},{7,7},{8,8},{9,14},{12,9... | collective-permute-start | bytes 1572872 | tf_op jit(solution)/shard_map/ppermute | solution.py:26
  70.5 18.5 %all-to-all-start = ((bf16[16,192,128]{2,1,0:T(8,128)(2,1)}), bf16[16,192,128]{2,1,0:T(8,128)(2,1)S(1)}, u32[]{:S(2)}, u32[]{:S(2)}) async-start(bf16[16,192,128]{2,1,0:T(8,128)(2,1)} %pack.1), calls=%async_computation | async-start | bytes 1572864 | tf_op jit(solution)/shard_map/all_to_all | solution.py:316
  76.6 12.5 %copy-start.1 = (bf16[192,1024]{1,0:T(8,128)(2,1)S(1)}, bf16[192,1024]{1,0:T(8,128)(2,1)}, u32[]{:S(2)}) copy-start(bf16[192,1024]{1,0:T(8,128)(2,1)} %dec_ref.1) | copy-start | bytes 1179652

commit v7 on v6

--- a/solution.py
+++ b/solution.py
@@ -38,11 +38,15 @@
     return (z, y, x ^ 1, c) if c == x % 2 else (z, y, x, 1 - c)
 
 
-def rows_kernel(place, own_ref, back_ref, ahead_ref, far_ref, low_ref, high_ref):
+def low_kernel(own_ref, back_ref, low_ref):
+    low_ref[:128, :] = own_ref[:128, :]
+    low_ref[128:, :] = back_ref[:128, :]
+
+
+def high_kernel(place, own_ref, back_ref, ahead_ref, far_ref, high_ref):
     refs = (own_ref, back_ref, ahead_ref, far_ref)
-    for i, ref in enumerate(refs):
-        half_ref = high_ref if i // 2 else low_ref
-        half_ref[i % 2 * 128 : i % 2 * 128 + 128, :] = ref[:128, :]
+    high_ref[:128, :] = ahead_ref[:128, :]
+    high_ref[128:256, :] = far_ref[:128, :]
     row = lax.broadcasted_iota(I32, (TAIL, 1024), 0)
     tail = jnp.zeros((TAIL, 1024), F32)
     for i, ref in enumerate(refs):
@@ -277,8 +281,8 @@
     place = jnp.stack([z, y, 2 * xh + xl, core]).astype(I32)
     w = move(weights, to_user)
     far, ahead, back = (move(block, hop(0, step)) for step in (2, -1, 1))
-    half_shapes = (((256, 1024), BF16), ((256 + TAIL, 1024), BF16))
-    low, high = kernel(rows_kernel, half_shapes, place, block, back, ahead, far, name="rows")
+    low = kernel(low_kernel, ((256, 1024), BF16), block, back, name="low")
+    high = kernel(high_kernel, ((256 + TAIL, 1024), BF16), place, block, back, ahead, far, name="high")
     low_back, high_ahead = move(low, hop(1, 1)), move(high, hop(1, -1))
     high_back, low_ahead = move(high, hop(1, 1)), move(low, hop(1, -1))
     sibling = lambda array: move(array, to_sibling)

time: 90.6 us -> 90.6 us (level)
    pallas_call x5 -> x6, Pallas kernels: 6.18 us -> 6.17 us  [kernel(): pl.pallas_call(body, in_specs=[pl.BlockSpec(memory_space=place(a)) for a...]
where the time goes in v7:
time: 90.6 us; the launch traced here: 90.3 us
  starting transfers between devices  35.7 us (39%)
  Pallas kernels  30.5 us (34%)
  waiting for transfers between devices  21.3 us (24%)
  other arithmetic  1.84 us (2%)
    ppermute x23, starting transfers between devices, move(): return lax.ppermute(array, AXES, pairs(target))  29.6 us
    pallas_call x4, Pallas kernels, chunk(): pl.pallas_call(functools.partial(chunk_kernel, enc_at, stage, scale), in_...  24.4 us
    ppermute x23, waiting for transfers between devices, move(): return lax.ppermute(array, AXES, pairs(target))  21.3 us
    pallas_call x6, Pallas kernels, kernel(): pl.pallas_call(body, in_specs=[pl.BlockSpec(memory_space=place(a)) for a...  6.17 us
    all_to_all x1, starting transfers between devices, shards(): lax.all_to_all(packed, ('z', 'y'), split_axis=0, concat_axis=0, tiled=True)  6.01 us
  transfers between devices with their start and end apart: 24, of which 8 were waited for; matrix products, arithmetic and copies ran while one was open for 2% of the time, Pallas kernels for 25%

profile of v7, /device:TPU:1, one launch (start us, length us, event | category | flops | bytes accessed | tf_op | source)
XLA Modules:
  0.0 90.3 jit_solution(13682834202760347008)
XLA Ops:
  0.6 1.5 %collective-permute-start.7 = (bf16[1024,1024]{1,0:T(8,128)(2,1)}, bf16[1024,1024]{1,0:T(8,128)(2,1)S(1)}, u32[]{:S(2)}, u32[]{:S(2)}) collective-permute-start(bf16[1024,1024]{1,0:T(8,128)(2,1)} %param.9), channel_id=1, source_target_pairs={{0,4},{1,0},{4,5},{5,1},{2,6},{3,2},{6,7},{7,3},{8,12},{9,8},{12,1... | collective-permute-start | bytes 6291464 | tf_op jit(solution)/shard_map/ppermute | solution.py:26
  2.1 0.1 pad.3.clone
  2.2 0.7 fusion
  2.9 1.1 %maximum_maximum_fusion.own_ref = bf16[144,1024]{1,0:T(8,128)(2,1)S(1)} fusion(bf16[1,1024]{1,0:T(2,128)(2,1)S(1)} %get-tuple-element.50, bf16[1,1024]{1,0:T(2,128)(2,1)S(1)} %get-tuple-element.51, bf16[128,1024]{1,0:T(8,128)(2,1)} %param.6, bf16[144]{0:T(256)(128)(2,1)S(1)} %pad.3.clone), kind=kLoop, calls=%fused_computation | loop fusion | flops 1179648 | bytes 561440 | tf_op jit(solution)/shard_map/concatenate | solution.py:279
  4.0 1.4 %collective-permute-start = (bf16[144,1024]{1,0:T(8,128)(2,1)S(1)}, bf16[144,1024]{1,0:T(8,128)(2,1)S(1)}, u32[]{:S(2)}, u32[]{:S(2)}) collective-permute-start(bf16[144,1024]{1,0:T(8,128)(2,1)S(1)} %maximum_maximum_fusion.own_ref), channel_id=1, source_target_pairs={{0,32},{1,9},{4,36},{5,13},{2,34},{3,11},{6,38},{7,15},{8,40},{9,1... | collective-permute-start | bytes 884744 | tf_op jit(solution)/shard_map/ppermute | solution.py:26
  5.4 1.5 %collective-permute-start.2 = (bf16[144,1024]{1,0:T(8,128)(2,1)S(1)}, bf16[144,1024]{1,0:T(8,128)(2,1)S(1)}, u32[]{:S(2)}, u32[]{:S(2)}) collective-permute-start(bf16[144,1024]{1,0:T(8,128)(2,1)S(1)} %maximum_maximum_fusion.own_ref), channel_id=1, source_target_pairs={{0,96},{1,25},{4,100},{5,29},{2,98},{3,27},{6,102},{7,31},{8,104},... | collective-permute-start | bytes 884744 | tf_op jit(solution)/shard_map/ppermute | solution.py:26
  7.0 1.6 %collective-permute-start.3 = (bf16[144,1024]{1,0:T(8,128)(2,1)S(1)}, bf16[144,1024]{1,0:T(8,128)(2,1)S(1)}, u32[]{:S(2)}, u32[]{:S(2)}) collective-permute-start(bf16[144,1024]{1,0:T(8,128)(2,1)S(1)} %maximum_maximum_fusion.own_ref), channel_id=1, source_target_pairs={{0,64},{1,17},{4,68},{5,21},{2,66},{3,19},{6,70},{7,23},{8,72},{9,... | collective-permute-start | bytes 884744 | tf_op jit(solution)/shard_map/ppermute | solution.py:26
  8.5 0.1 pad_add_fusion.place.refs_0_
  8.6 2.7 %collective-permute-done.back_ref = bf16[144,1024]{1,0:T(8,128)(2,1)S(1)} collective-permute-done((bf16[144,1024]{1,0:T(8,128)(2,1)S(1)}, bf16[144,1024]{1,0:T(8,128)(2,1)S(1)}, u32[]{:S(2)}, u32[]{:S(2)}) %collective-permute-start) | collective-permute-done | bytes 294944 | tf_op jit(solution)/shard_map/ppermute | solution.py:26
  11.3 2.5 %collective-permute-done.2.ahead_ref = bf16[144,1024]{1,0:T(8,128)(2,1)S(1)} collective-permute-done((bf16[144,1024]{1,0:T(8,128)(2,1)S(1)}, bf16[144,1024]{1,0:T(8,128)(2,1)S(1)}, u32[]{:S(2)}, u32[]{:S(2)}) %collective-permute-start.2) | collective-permute-done | bytes 294944 | tf_op jit(solution)/shard_map/ppermute | solution.py:26
  13.8 1.8 %collective-permute-done.3.far_ref = bf16[144,1024]{1,0:T(8,128)(2,1)S(1)} collective-permute-done((bf16[144,1024]{1,0:T(8,128)(2,1)S(1)}, bf16[144,1024]{1,0:T(8,128)(2,1)S(1)}, u32[]{:S(2)}, u32[]{:S(2)}) %collective-permute-start.3) | collective-permute-done | bytes 294944 | tf_op jit(solution)/shard_map/ppermute | solution.py:26
  15.6 0.6 high.1.refs_2_
  16.2 3.4 %collective-permute-start.6 = (bf16[272,1024]{1,0:T(8,128)(2,1)S(1)}, bf16[272,1024]{1,0:T(8,128)(2,1)S(1)}, u32[]{:S(2)}, u32[]{:S(2)}) collective-permute-start(bf16[272,1024]{1,0:T(8,128)(2,1)S(1)} %high.1.refs_2_), channel_id=1, source_target_pairs={{0,1},{1,0},{4,5},{5,4},{2,3},{3,2},{6,7},{7,6},{8,9},{9,8},{12,13... | collective-permute-start | bytes 1671176 | tf_op jit(solution)/shard_map/ppermute | solution.py:26
  19.7 0.1 collective-permute-start.5
  19.8 1.6 %collective-permute-start.4 = (bf16[272,1024]{1,0:T(8,128)(2,1)S(1)}, bf16[272,1024]{1,0:T(8,128)(2,1)S(1)}, u32[]{:S(2)}, u32[]{:S(2)}) collective-permute-start(bf16[272,1024]{1,0:T(8,128)(2,1)S(1)} %high.1.refs_2_), channel_id=1, source_target_pairs={{0,24},{1,97},{4,28},{5,101},{2,26},{3,99},{6,30},{7,103},{8,0},{9... | collective-permute-start | bytes 1671176 | tf_op jit(solution)/shard_map/ppermute | solution.py:26
  21.5 0.0 collective-permute-start.1
  21.5 0.6 collective-permute-done.5.refs_3_
  22.0 1.1 %collective-permute-start.10 = (bf16[272,1024]{1,0:T(8,128)(2,1)S(1)}, bf16[272,1024]{1,0:T(8,128)(2,1)S(1)}, u32[]{:S(2)}, u32[]{:S(2)}) collective-permute-start(bf16[272,1024]{1,0:T(8,128)(2,1)S(1)} %high.1.refs_2_), channel_id=1, source_target_pairs={{0,8},{1,33},{4,12},{5,37},{2,10},{3,35},{6,14},{7,39},{8,16},{9,4... | collective-permute-start | bytes 1671176 | tf_op jit(solution)/shard_map/ppermute | solution.py:26
  23.2 0.0 collective-permute-done.6.refs_4_
  23.2 1.5 %collective-permute-start.11 = (bf16[256,1024]{1,0:T(8,128)(2,1)S(1)}, bf16[256,1024]{1,0:T(8,128)(2,1)S(1)}, u32[]{:S(2)}, u32[]{:S(2)}) collective-permute-start(bf16[256,1024]{1,0:T(8,128)(2,1)S(1)} %low.1.refs_1_), channel_id=1, source_target_pairs={{0,24},{1,97},{4,28},{5,101},{2,26},{3,99},{6,30},{7,103},{8,0},{9... | collective-permute-start | bytes 1572872 | tf_op jit(solution)/shard_map/ppermute | solution.py:26
  24.7 2.0 %collective-permute-done.7.refs_5_.w_ref = bf16[1024,1024]{1,0:T(8,128)(2,1)S(1)} collective-permute-done((bf16[1024,1024]{1,0:T(8,128)(2,1)}, bf16[1024,1024]{1,0:T(8,128)(2,1)S(1)}, u32[]{:S(2)}, u32[]{:S(2)}) %collective-permute-start.7) | collective-permute-done | bytes 2097184 | tf_op jit(solution)/shard_map/ppermute | solution.py:26
  26.7 5.4 %chunk.4 = (f32[4,1024,256]{2,1,0:T(8,128)S(1)}, bf16[1024,1024]{1,0:T(8,128)(2,1)S(1)}) custom-call(s32[4]{0:T(128)S(1)} %pad_add_fusion.place.refs_0_, bf16[256,1024]{1,0:T(8,128)(2,1)S(1)} %low.1.refs_1_, bf16[272,1024]{1,0:T(8,128)(2,1)S(1)} %high.1.refs_2_, bf16[256,1024]{1,0:T(8,128)(2,1)S(1)} %collective-permute-done.5.refs_3_, ...), custom_call_target="tpu_custom_call" | custom-call | flops 5100273664 | bytes 1048576 | tf_op jit(solution)/shard_map/chunk/pallas_call | solution.py:181
  32.1 0.0 collective-permute-done.1.refs_0_
  32.1 0.0 collective-permute-done.4.refs_1_
  32.1 0.0 copy-start
  32.1 1.6 %collective-permute-start.13 = (bf16[272,1024]{1,0:T(8,128)(2,1)S(1)}, bf16[272,1024]{1,0:T(8,128)(2,1)S(1)}, u32[]{:S(2)}, u32[]{:S(2)}) collective-permute-start(bf16[272,1024]{1,0:T(8,128)(2,1)S(1)} %get-tuple-element.27.refs_4_), channel_id=1, source_target_pairs={{0,1},{1,0},{4,5},{5,4},{2,3},{3,2},{6,7},{7,6},{8,9},{9,8},{12,13... | collective-permute-start | bytes 1671176 | tf_op jit(solution)/shard_map/ppermute | solution.py:26
  33.7 0.1 collective-permute-start.12
  33.8 3.1 %collective-permute-start.9 = (bf16[272,1024]{1,0:T(8,128)(2,1)S(1)}, bf16[272,1024]{1,0:T(8,128)(2,1)S(1)}, u32[]{:S(2)}, u32[]{:S(2)}) collective-permute-start(bf16[272,1024]{1,0:T(8,128)(2,1)S(1)} %get-tuple-element.27.refs_4_), channel_id=1, source_target_pairs={{0,24},{1,97},{4,28},{5,101},{2,26},{3,99},{6,30},{7,103},{8,0},{9... | collective-permute-start | bytes 1671176 | tf_op jit(solution)/shard_map/ppermute | solution.py:26
  36.9 0.0 collective-permute-done.11.refs_1_
  36.9 0.0 collective-permute-start.8
  36.9 0.0 copy-done
  37.0 1.7 %early.1 = (f32[192,2048]{1,0:T(8,128)S(1)}, f32[192,2048]{1,0:T(8,128)S(1)}, bf16[384,1024]{1,0:T(8,128)(2,1)S(1)}) custom-call(bf16[1024,1024]{1,0:T(8,128)(2,1)S(1)} %collective-permute-done.7.refs_5_.w_ref, bf16[192,1024]{1,0:T(8,128)(2,1)S(1)} %bitcast.25, bf16[1024,1024]{1,0:T(8,128)(2,1)S(1)} %get-tuple-element.25.refs_2_.grads_ref), custom_call_target="tpu_custom_call" | custom-call | flops 1073741824 | bytes 1024 | tf_op jit(solution)/shard_map/early/pallas_call | solution.py:244
  38.6 0.0 collective-permute-done.10.refs_0_
  38.6 0.0 collective-permute-done.12.refs_2_.refs_1_
  38.6 0.0 collective-permute-done.13.refs_3_.refs_4_
  38.7 1.1 %collective-permute-start.16 = (bf16[272,1024]{1,0:T(8,128)(2,1)S(1)}, bf16[272,1024]{1,0:T(8,128)(2,1)S(1)}, u32[]{:S(2)}, u32[]{:S(2)}) collective-permute-start(bf16[272,1024]{1,0:T(8,128)(2,1)S(1)} %get-tuple-element.29.refs_2_), channel_id=1, source_target_pairs={{0,1},{1,0},{4,5},{5,4},{2,3},{3,2},{6,7},{7,6},{8,9},{9,8},{12,13... | collective-permute-start | bytes 1671176 | tf_op jit(solution)/shard_map/ppermute | solution.py:26
  39.8 0.3 collective-permute-start.17
  40.0 6.2 %chunk.5 = (f32[192,2048]{1,0:T(8,128)S(1)}, f32[4,1024,256]{2,1,0:T(8,128)S(1)}) custom-call(s32[4]{0:T(128)S(1)} %pad_add_fusion.place.refs_0_, bf16[256,1024]{1,0:T(8,128)(2,1)S(1)} %get-tuple-element.26.refs_1_, bf16[272,1024]{1,0:T(8,128)(2,1)S(1)} %get-tuple-element.29.refs_2_, ...), custom_call_target="tpu_custom_call", output_to_operand_aliasing={{0}: (8, {}), {1}: (6, {})} | custom-call | flops 5100273664 | bytes 1048576 | tf_op jit(solution)/shard_map/chunk/pallas_call | solution.py:181
  46.2 0.3 collective-permute-done.8.refs_0_
  46.5 0.0 collective-permute-done.9.refs_1_
  46.5 0.5 collective-permute-start.15
  47.0 0.1 collective-permute-start.14
  47.1 0.0 collective-permute-done.17.refs_3_
  47.1 0.0 collective-permute-done.16.refs_2_
  47.1 6.2 %chunk.6 = (f32[192,2048]{1,0:T(8,128)S(1)}, f32[4,1024,256]{2,1,0:T(8,128)S(1)}) custom-call(s32[4]{0:T(128)S(1)} %pad_add_fusion.place.refs_0_, bf16[256,1024]{1,0:T(8,128)(2,1)S(1)} %collective-permute-done.12.refs_2_.refs_1_, bf16[272,1024]{1,0:T(8,128)(2,1)S(1)} %collective-permute-done.16.refs_2_, ...), custom_call_target="tpu_custom_call", output_to_operand_aliasing={{0}: (8, {}), {1}: (6, {})} | custom-call | flops 5100273664 | bytes 1048576 | tf_op jit(solution)/shard_map/chunk/pallas_call | solution.py:181
  53.3 0.0 collective-permute-done.14.refs_3_
  53.3 0.0 collective-permute-done.15.refs_4_
  53.3 6.6 %chunk.7 = (f32[192,2048]{1,0:T(8,128)S(1)}, f32[192,2048]{1,0:T(8,128)S(1)}, bf16[1024,256]{1,0:T(8,128)(2,1)}, bf16[1024,256]{1,0:T(8,128)(2,1)}, bf16[1024,25...) custom-call(s32[4]{0:T(128)S(1)} %pad_add_fusion.place.refs_0_, ...), custom_call_target="tpu_custom_call", output_to_operand_aliasing={{0}: (8, {}), {1}: (9, {})} | custom-call | flops 5100273664 | bytes 1048576 | tf_op jit(solution)/shard_map/chunk/pallas_call | solution.py:181
  59.9 0.5 collective-permute-start.18
  60.4 2.1 %collective-permute-start.19 = (bf16[1024,256]{1,0:T(8,128)(2,1)}, bf16[1024,256]{1,0:T(8,128)(2,1)S(1)}, u32[]{:S(2)}, u32[]{:S(2)}) collective-permute-start(bf16[1024,256]{1,0:T(8,128)(2,1)} %get-tuple-element.42), channel_id=1, source_target_pairs={{0,3},{1,5},{4,2},{5,6},{2,1},{3,7},{6,0},{7,4},{8,11},{9,13},{12,... | collective-permute-start | bytes 1572872 | tf_op jit(solution)/shard_map/ppermute | solution.py:26
  62.6 0.3 collective-permute-start.20
  62.8 3.9 %collective-permute-start.21 = (bf16[1024,256]{1,0:T(8,128)(2,1)}, bf16[1024,256]{1,0:T(8,128)(2,1)S(1)}, u32[]{:S(2)}, u32[]{:S(2)}) collective-permute-start(bf16[1024,256]{1,0:T(8,128)(2,1)} %get-tuple-element.44), channel_id=1, source_target_pairs={{0,1},{1,7},{4,0},{5,4},{2,3},{3,5},{6,2},{7,6},{8,9},{9,15},{12,8... | collective-permute-start | bytes 1572872 | tf_op jit(solution)/shard_map/ppermute | solution.py:26
  66.8 2.1 %collective-permute-start.22 = (bf16[1024,256]{1,0:T(8,128)(2,1)}, bf16[1024,256]{1,0:T(8,128)(2,1)S(1)}, u32[]{:S(2)}, u32[]{:S(2)}) collective-permute-start(bf16[1024,256]{1,0:T(8,128)(2,1)} %get-tuple-element.45), channel_id=1, source_target_pairs={{0,0},{1,6},{4,1},{5,5},{2,2},{3,4},{6,3},{7,7},{8,8},{9,14},{12,9... | collective-permute-start | bytes 1572872 | tf_op jit(solution)/shard_map/ppermute | solution.py:26
  68.9 0.0 collective-permute-done.18.refs_1_
  68.9 1.6 %pack.1 = bf16[16,192,128]{2,1,0:T(8,128)(2,1)} custom-call(s32[4]{0:T(128)S(1)} %pad_add_fusion.place.refs_0_, f32[192,2048]{1,0:T(8,128)S(1)} %get-tuple-element.40.refs_0_, f32[192,2048]{1,0:T(8,128)S(1)} %collective-permute-done.18.refs_1_), custom_call_target="tpu_custom_call" | custom-call | flops 1000000 | bytes 1024 | tf_op jit(solution)/shard_map/pack/pallas_call | solution.py:244
  70.5 6.0 %all-to-all-start = ((bf16[16,192,128]{2,1,0:T(8,128)(2,1)}), bf16[16,192,128]{2,1,0:T(8,128)(2,1)S(1)}, u32[]{:S(2)}, u32[]{:S(2)}) async-start(bf16[16,192,128]{2,1,0:T(8,128)(2,1)} %pack.1), calls=%async_computation | async-start | bytes 1572864 | tf_op jit(solution)/shard_map/all_to_all | solution.py:320
  76.6 0.0 copy-start.1
  76.6 0.0 collective-permute-done.19.refs_0_
  76.6 11.0 %collective-permute-done.20.refs_1_ = bf16[1024,256]{1,0:T(8,128)(2,1)S(1)} collective-permute-done((bf16[1024,256]{1,0:T(8,128)(2,1)}, bf16[1024,256]{1,0:T(8,128)(2,1)S(1)}, u32[]{:S(2)}, u32[]{:S(2)}) %collective-permute-start.20) | collective-permute-done | bytes 524320 | tf_op jit(solution)/shard_map/ppermute | solution.py:26
  87.6 0.0 collective-permute-done.21.refs_2_
  87.6 0.4 collective-permute-done.22.refs_3_
  88.0 1.0 %join.1 = (bf16[1024,256]{1,0:T(8,128)(2,1)}, f32[8,128]{1,0:T(8,128)S(1)}) custom-call(bf16[1024,256]{1,0:T(8,128)(2,1)S(1)} %collective-permute-done.19.refs_0_, bf16[1024,256]{1,0:T(8,128)(2,1)S(1)} %collective-permute-done.20.refs_1_, bf16[1024,256]{1,0:T(8,128)(2,1)S(1)} %collective-permute-done.21.refs_2_, ...), custom_call_target="tpu_custom_call" | custom-call | flops 99999997952 | bytes 1024 | tf_op jit(solution)/shard_map/join/pallas_call | solution.py:244
  89.1 0.0 all-to-all-done.parts_ref
  89.1 1.2 %decode.1 = bf16[128,1024]{1,0:T(8,128)(2,1)} custom-call(bf16[16,192,128]{2,1,0:T(8,128)(2,1)S(1)} %all-to-all-done.parts_ref, bf16[192,1024]{1,0:T(8,128)(2,1)S(1)} %copy-done.1, f32[8,128]{1,0:T(8,128)S(1)} %get-tuple-element.46.after_ref), custom_call_target="tpu_custom_call" | custom-call | flops 1000000 | bytes 1024 | tf_op jit(solution)/shard_map/decode/pallas_call | solution.py:244
  (7 shorter events, 0.1 us)
Async XLA Ops:
  0.6 26.0 %collective-permute-start.7 = (bf16[1024,1024]{1,0:T(8,128)(2,1)}, bf16[1024,1024]{1,0:T(8,128)(2,1)S(1)}, u32[]{:S(2)}, u32[]{:S(2)}) collective-permute-start(bf16[1024,1024]{1,0:T(8,128)(2,1)} %param.9), channel_id=1, source_target_pairs={{0,4},{1,0},{4,5},{5,1},{2,6},{3,2},{6,7},{7,3},{8,12},{9,8},{12,1... | collective-permute-start | bytes 6291464 | tf_op jit(solution)/shard_map/ppermute | solution.py:26
  4.0 7.3 %collective-permute-start = (bf16[144,1024]{1,0:T(8,128)(2,1)S(1)}, bf16[144,1024]{1,0:T(8,128)(2,1)S(1)}, u32[]{:S(2)}, u32[]{:S(2)}) collective-permute-start(bf16[144,1024]{1,0:T(8,128)(2,1)S(1)} %maximum_maximum_fusion.own_ref), channel_id=1, source_target_pairs={{0,32},{1,9},{4,36},{5,13},{2,34},{3,11},{6,38},{7,15},{8,40},{9,1... | collective-permute-start | bytes 884744 | tf_op jit(solution)/shard_map/ppermute | solution.py:26
  5.4 8.3 %collective-permute-start.2 = (bf16[144,1024]{1,0:T(8,128)(2,1)S(1)}, bf16[144,1024]{1,0:T(8,128)(2,1)S(1)}, u32[]{:S(2)}, u32[]{:S(2)}) collective-permute-start(bf16[144,1024]{1,0:T(8,128)(2,1)S(1)} %maximum_maximum_fusion.own_ref), channel_id=1, source_target_pairs={{0,96},{1,25},{4,100},{5,29},{2,98},{3,27},{6,102},{7,31},{8,104},... | collective-permute-start | bytes 884744 | tf_op jit(solution)/shard_map/ppermute | solution.py:26
  7.0 8.7 %collective-permute-start.3 = (bf16[144,1024]{1,0:T(8,128)(2,1)S(1)}, bf16[144,1024]{1,0:T(8,128)(2,1)S(1)}, u32[]{:S(2)}, u32[]{:S(2)}) collective-permute-start(bf16[144,1024]{1,0:T(8,128)(2,1)S(1)} %maximum_maximum_fusion.own_ref), channel_id=1, source_target_pairs={{0,64},{1,17},{4,68},{5,21},{2,66},{3,19},{6,70},{7,23},{8,72},{9,... | collective-permute-start | bytes 884744 | tf_op jit(solution)/shard_map/ppermute | solution.py:26
  16.2 6.9 %collective-permute-start.6 = (bf16[272,1024]{1,0:T(8,128)(2,1)S(1)}, bf16[272,1024]{1,0:T(8,128)(2,1)S(1)}, u32[]{:S(2)}, u32[]{:S(2)}) collective-permute-start(bf16[272,1024]{1,0:T(8,128)(2,1)S(1)} %high.1.refs_2_), channel_id=1, source_target_pairs={{0,1},{1,0},{4,5},{5,4},{2,3},{3,2},{6,7},{7,6},{8,9},{9,8},{12,13... | collective-permute-start | bytes 1671176 | tf_op jit(solution)/shard_map/ppermute | solution.py:26
  19.7 2.3 %collective-permute-start.5 = (bf16[256,1024]{1,0:T(8,128)(2,1)S(1)}, bf16[256,1024]{1,0:T(8,128)(2,1)S(1)}, u32[]{:S(2)}, u32[]{:S(2)}) collective-permute-start(bf16[256,1024]{1,0:T(8,128)(2,1)S(1)} %low.1.refs_1_), channel_id=1, source_target_pairs={{0,1},{1,0},{4,5},{5,4},{2,3},{3,2},{6,7},{7,6},{8,9},{9,8},{12,13... | collective-permute-start | bytes 1572872 | tf_op jit(solution)/shard_map/ppermute | solution.py:26
  19.8 12.3 %collective-permute-start.4 = (bf16[272,1024]{1,0:T(8,128)(2,1)S(1)}, bf16[272,1024]{1,0:T(8,128)(2,1)S(1)}, u32[]{:S(2)}, u32[]{:S(2)}) collective-permute-start(bf16[272,1024]{1,0:T(8,128)(2,1)S(1)} %high.1.refs_2_), channel_id=1, source_target_pairs={{0,24},{1,97},{4,28},{5,101},{2,26},{3,99},{6,30},{7,103},{8,0},{9... | collective-permute-start | bytes 1671176 | tf_op jit(solution)/shard_map/ppermute | solution.py:26
  21.5 10.6 %collective-permute-start.1 = (bf16[256,1024]{1,0:T(8,128)(2,1)S(1)}, bf16[256,1024]{1,0:T(8,128)(2,1)S(1)}, u32[]{:S(2)}, u32[]{:S(2)}) collective-permute-start(bf16[256,1024]{1,0:T(8,128)(2,1)S(1)} %low.1.refs_1_), channel_id=1, source_target_pairs={{0,8},{1,33},{4,12},{5,37},{2,10},{3,35},{6,14},{7,39},{8,16},{9,4... | collective-permute-start | bytes 1572872 | tf_op jit(solution)/shard_map/ppermute | solution.py:26
  22.0 16.6 %collective-permute-start.10 = (bf16[272,1024]{1,0:T(8,128)(2,1)S(1)}, bf16[272,1024]{1,0:T(8,128)(2,1)S(1)}, u32[]{:S(2)}, u32[]{:S(2)}) collective-permute-start(bf16[272,1024]{1,0:T(8,128)(2,1)S(1)} %high.1.refs_2_), channel_id=1, source_target_pairs={{0,8},{1,33},{4,12},{5,37},{2,10},{3,35},{6,14},{7,39},{8,16},{9,4... | collective-permute-start | bytes 1671176 | tf_op jit(solution)/shard_map/ppermute | solution.py:26
  23.2 13.8 %collective-permute-start.11 = (bf16[256,1024]{1,0:T(8,128)(2,1)S(1)}, bf16[256,1024]{1,0:T(8,128)(2,1)S(1)}, u32[]{:S(2)}, u32[]{:S(2)}) collective-permute-start(bf16[256,1024]{1,0:T(8,128)(2,1)S(1)} %low.1.refs_1_), channel_id=1, source_target_pairs={{0,24},{1,97},{4,28},{5,101},{2,26},{3,99},{6,30},{7,103},{8,0},{9... | collective-permute-start | bytes 1572872 | tf_op jit(solution)/shard_map/ppermute | solution.py:26
  32.1 4.9 %copy-start = (bf16[1024,192]{0,1:T(8,128)(2,1)S(1)}, bf16[1024,192]{0,1:T(8,128)(2,1)}, u32[]{:S(2)}) copy-start(bf16[1024,192]{0,1:T(8,128)(2,1)} %param.10) | copy-start | bytes 1179652
  32.1 6.5 %collective-permute-start.13 = (bf16[272,1024]{1,0:T(8,128)(2,1)S(1)}, bf16[272,1024]{1,0:T(8,128)(2,1)S(1)}, u32[]{:S(2)}, u32[]{:S(2)}) collective-permute-start(bf16[272,1024]{1,0:T(8,128)(2,1)S(1)} %get-tuple-element.27.refs_4_), channel_id=1, source_target_pairs={{0,1},{1,0},{4,5},{5,4},{2,3},{3,2},{6,7},{7,6},{8,9},{9,8},{12,13... | collective-permute-start | bytes 1671176 | tf_op jit(solution)/shard_map/ppermute | solution.py:26
  33.7 4.9 %collective-permute-start.12 = (bf16[256,1024]{1,0:T(8,128)(2,1)S(1)}, bf16[256,1024]{1,0:T(8,128)(2,1)S(1)}, u32[]{:S(2)}, u32[]{:S(2)}) collective-permute-start(bf16[256,1024]{1,0:T(8,128)(2,1)S(1)} %get-tuple-element.26.refs_1_), channel_id=1, source_target_pairs={{0,1},{1,0},{4,5},{5,4},{2,3},{3,2},{6,7},{7,6},{8,9},{9,8},{12,13... | collective-permute-start | bytes 1572872 | tf_op jit(solution)/shard_map/ppermute | solution.py:26
  33.8 12.7 %collective-permute-start.9 = (bf16[272,1024]{1,0:T(8,128)(2,1)S(1)}, bf16[272,1024]{1,0:T(8,128)(2,1)S(1)}, u32[]{:S(2)}, u32[]{:S(2)}) collective-permute-start(bf16[272,1024]{1,0:T(8,128)(2,1)S(1)} %get-tuple-element.27.refs_4_), channel_id=1, source_target_pairs={{0,24},{1,97},{4,28},{5,101},{2,26},{3,99},{6,30},{7,103},{8,0},{9... | collective-permute-start | bytes 1671176 | tf_op jit(solution)/shard_map/ppermute | solution.py:26
  36.9 9.5 %collective-permute-start.8 = (bf16[256,1024]{1,0:T(8,128)(2,1)S(1)}, bf16[256,1024]{1,0:T(8,128)(2,1)S(1)}, u32[]{:S(2)}, u32[]{:S(2)}) collective-permute-start(bf16[256,1024]{1,0:T(8,128)(2,1)S(1)} %get-tuple-element.26.refs_1_), channel_id=1, source_target_pairs={{0,8},{1,33},{4,12},{5,37},{2,10},{3,35},{6,14},{7,39},{8,16},{9,4... | collective-permute-start | bytes 1572872 | tf_op jit(solution)/shard_map/ppermute | solution.py:26
  38.7 8.4 %collective-permute-start.16 = (bf16[272,1024]{1,0:T(8,128)(2,1)S(1)}, bf16[272,1024]{1,0:T(8,128)(2,1)S(1)}, u32[]{:S(2)}, u32[]{:S(2)}) collective-permute-start(bf16[272,1024]{1,0:T(8,128)(2,1)S(1)} %get-tuple-element.29.refs_2_), channel_id=1, source_target_pairs={{0,1},{1,0},{4,5},{5,4},{2,3},{3,2},{6,7},{7,6},{8,9},{9,8},{12,13... | collective-permute-start | bytes 1671176 | tf_op jit(solution)/shard_map/ppermute | solution.py:26
  39.8 7.3 %collective-permute-start.17 = (bf16[256,1024]{1,0:T(8,128)(2,1)S(1)}, bf16[256,1024]{1,0:T(8,128)(2,1)S(1)}, u32[]{:S(2)}, u32[]{:S(2)}) collective-permute-start(bf16[256,1024]{1,0:T(8,128)(2,1)S(1)} %get-tuple-element.30.refs_3_), channel_id=1, source_target_pairs={{0,1},{1,0},{4,5},{5,4},{2,3},{3,2},{6,7},{7,6},{8,9},{9,8},{12,13... | collective-permute-start | bytes 1572872 | tf_op jit(solution)/shard_map/ppermute | solution.py:26
  46.5 6.8 %collective-permute-start.15 = (bf16[272,1024]{1,0:T(8,128)(2,1)S(1)}, bf16[272,1024]{1,0:T(8,128)(2,1)S(1)}, u32[]{:S(2)}, u32[]{:S(2)}) collective-permute-start(bf16[272,1024]{1,0:T(8,128)(2,1)S(1)} %get-tuple-element.35.refs_2_), channel_id=1, source_target_pairs={{0,1},{1,0},{4,5},{5,4},{2,3},{3,2},{6,7},{7,6},{8,9},{9,8},{12,13... | collective-permute-start | bytes 1671176 | tf_op jit(solution)/shard_map/ppermute | solution.py:26
  47.0 6.3 %collective-permute-start.14 = (bf16[256,1024]{1,0:T(8,128)(2,1)S(1)}, bf16[256,1024]{1,0:T(8,128)(2,1)S(1)}, u32[]{:S(2)}, u32[]{:S(2)}) collective-permute-start(bf16[256,1024]{1,0:T(8,128)(2,1)S(1)} %get-tuple-element.34.refs_1_), channel_id=1, source_target_pairs={{0,1},{1,0},{4,5},{5,4},{2,3},{3,2},{6,7},{7,6},{8,9},{9,8},{12,13... | collective-permute-start | bytes 1572872 | tf_op jit(solution)/shard_map/ppermute | solution.py:26
  59.9 9.0 %collective-permute-start.18 = (f32[192,2048]{1,0:T(8,128)S(1)}, f32[192,2048]{1,0:T(8,128)S(1)}, u32[]{:S(2)}, u32[]{:S(2)}) collective-permute-start(f32[192,2048]{1,0:T(8,128)S(1)} %get-tuple-element.41), channel_id=1, source_target_pairs={{0,1},{1,0},{4,5},{5,4},{2,3},{3,2},{6,7},{7,6},{8,9},{9,8},{12,13... | collective-permute-start | bytes 4718600 | tf_op jit(solution)/shard_map/ppermute | solution.py:26
  60.4 16.1 %collective-permute-start.19 = (bf16[1024,256]{1,0:T(8,128)(2,1)}, bf16[1024,256]{1,0:T(8,128)(2,1)S(1)}, u32[]{:S(2)}, u32[]{:S(2)}) collective-permute-start(bf16[1024,256]{1,0:T(8,128)(2,1)} %get-tuple-element.42), channel_id=1, source_target_pairs={{0,3},{1,5},{4,2},{5,6},{2,1},{3,7},{6,0},{7,4},{8,11},{9,13},{12,... | collective-permute-start | bytes 1572872 | tf_op jit(solution)/shard_map/ppermute | solution.py:26
  62.6 25.1 %collective-permute-start.20 = (bf16[1024,256]{1,0:T(8,128)(2,1)}, bf16[1024,256]{1,0:T(8,128)(2,1)S(1)}, u32[]{:S(2)}, u32[]{:S(2)}) collective-permute-start(bf16[1024,256]{1,0:T(8,128)(2,1)} %get-tuple-element.43), channel_id=1, source_target_pairs={{0,2},{1,4},{4,3},{5,7},{2,0},{3,6},{6,1},{7,5},{8,10},{9,12},{12,... | collective-permute-start | bytes 1572872 | tf_op jit(solution)/shard_map/ppermute | solution.py:26
  62.8 24.8 %collective-permute-start.21 = (bf16[1024,256]{1,0:T(8,128)(2,1)}, bf16[1024,256]{1,0:T(8,128)(2,1)S(1)}, u32[]{:S(2)}, u32[]{:S(2)}) collective-permute-start(bf16[1024,256]{1,0:T(8,128)(2,1)} %get-tuple-element.44), channel_id=1, source_target_pairs={{0,1},{1,7},{4,0},{5,4},{2,3},{3,5},{6,2},{7,6},{8,9},{9,15},{12,8... | collective-permute-start | bytes 1572872 | tf_op jit(solution)/shard_map/ppermute | solution.py:26
  66.8 21.2 %collective-permute-start.22 = (bf16[1024,256]{1,0:T(8,128)(2,1)}, bf16[1024,256]{1,0:T(8,128)(2,1)S(1)}, u32[]{:S(2)}, u32[]{:S(2)}) collective-permute-start(bf16[1024,256]{1,0:T(8,128)(2,1)} %get-tuple-element.45), channel_id=1, source_target_pairs={{0,0},{1,6},{4,1},{5,5},{2,2},{3,4},{6,3},{7,7},{8,8},{9,14},{12,9... | collective-permute-start | bytes 1572872 | tf_op jit(solution)/shard_map/ppermute | solution.py:26
  70.5 18.5 %all-to-all-start = ((bf16[16,192,128]{2,1,0:T(8,128)(2,1)}), bf16[16,192,128]{2,1,0:T(8,128)(2,1)S(1)}, u32[]{:S(2)}, u32[]{:S(2)}) async-start(bf16[16,192,128]{2,1,0:T(8,128)(2,1)} %pack.1), calls=%async_computation | async-start | bytes 1572864 | tf_op jit(solution)/shard_map/all_to_all | solution.py:320
  76.6 12.5 %copy-start.1 = (bf16[192,1024]{1,0:T(8,128)(2,1)S(1)}, bf16[192,1024]{1,0:T(8,128)(2,1)}, u32[]{:S(2)}) copy-start(bf16[192,1024]{1,0:T(8,128)(2,1)} %dec_ref.1) | copy-start | bytes 1179652

commit v8 on v7

--- a/solution.py
+++ b/solution.py
@@ -282,12 +282,14 @@
     w = move(weights, to_user)
     far, ahead, back = (move(block, hop(0, step)) for step in (2, -1, 1))
     low = kernel(low_kernel, ((256, 1024), BF16), block, back, name="low")
+    low_sib = move(low, to_sibling)
+    ahead, far = after([ahead, far], low_sib)
     high = kernel(high_kernel, ((256 + TAIL, 1024), BF16), place, block, back, ahead, far, name="high")
     low_back, high_ahead = move(low, hop(1, 1)), move(high, hop(1, -1))
     high_back, low_ahead = move(high, hop(1, 1)), move(low, hop(1, -1))
     sibling = lambda array: move(array, to_sibling)
     row, own, sib = [low, high], 0, 1
-    rows = [row, [sibling(low), sibling(high)]]
+    rows = [row, [low_sib, sibling(high)]]
     total, early_grads = chunk(0, place, rows, ((own, 0), (sib, 0)), w, scale)
     sums_wet = kernel(
         early_kernel,

time: 90.6 us -> 96.4 us (1.064)
  waiting for transfers between devices: 21.3 us -> 25 us
  Pallas kernels: 30.5 us -> 32 us
    ppermute x23, waiting for transfers between devices: 21.3 us -> 24.5 us  [move(): return lax.ppermute(array, AXES, pairs(target))]
  transfers between devices with their start and end apart: 24 -> 24, of which waited for: 8 -> 7; matrix products, arithmetic and copies ran while one was open for 2% -> 2% of each run, Pallas kernels for 25% -> 25%
where the time goes in v8:
time: 96.4 us; the launch traced here: 96.1 us
  starting transfers between devices  36.3 us (38%)
  Pallas kernels  32 us (33%)
  waiting for transfers between devices  25 us (26%)
  other arithmetic  1.84 us (2%)
    ppermute x23, starting transfers between devices, move(): return lax.ppermute(array, AXES, pairs(target))  30.2 us
    pallas_call x4, Pallas kernels, chunk(): pl.pallas_call(functools.partial(chunk_kernel, enc_at, stage, scale), in_...  25 us
    ppermute x23, waiting for transfers between devices, move(): return lax.ppermute(array, AXES, pairs(target))  24.5 us
    pallas_call x6, Pallas kernels, kernel(): pl.pallas_call(body, in_specs=[pl.BlockSpec(memory_space=place(a)) for a...  6.97 us
    all_to_all x1, starting transfers between devices, shards(): lax.all_to_all(packed, ('z', 'y'), split_axis=0, concat_axis=0, tiled=True)  6.13 us
  transfers between devices with their start and end apart: 24, of which 7 were waited for; matrix products, arithmetic and copies ran while one was open for 2% of the time, Pallas kernels for 25%

profile of v8, /device:TPU:1, one launch (start us, length us, event | category | flops | bytes accessed | tf_op | source)
XLA Modules:
  0.0 96.1 jit_solution(6894718777938023703)
XLA Ops:
  0.6 1.5 %collective-permute-start.7 = (bf16[1024,1024]{1,0:T(8,128)(2,1)}, bf16[1024,1024]{1,0:T(8,128)(2,1)S(1)}, u32[]{:S(2)}, u32[]{:S(2)}) collective-permute-start(bf16[1024,1024]{1,0:T(8,128)(2,1)} %param.9), channel_id=1, source_target_pairs={{0,4},{1,0},{4,5},{5,1},{2,6},{3,2},{6,7},{7,3},{8,12},{9,8},{12,1... | collective-permute-start | bytes 6291464 | tf_op jit(solution)/shard_map/ppermute | solution.py:26
  2.1 0.1 pad.3.clone
  2.2 0.7 fusion
  2.9 1.1 %maximum_maximum_fusion.own_ref = bf16[144,1024]{1,0:T(8,128)(2,1)S(1)} fusion(bf16[1,1024]{1,0:T(2,128)(2,1)S(1)} %get-tuple-element.54, bf16[1,1024]{1,0:T(2,128)(2,1)S(1)} %get-tuple-element.55, bf16[128,1024]{1,0:T(8,128)(2,1)} %param.6, bf16[144]{0:T(256)(128)(2,1)S(1)} %pad.3.clone), kind=kLoop, calls=%fused_computation | loop fusion | flops 1179648 | bytes 561440 | tf_op jit(solution)/shard_map/concatenate | solution.py:279
  4.0 1.4 %collective-permute-start = (bf16[144,1024]{1,0:T(8,128)(2,1)S(1)}, bf16[144,1024]{1,0:T(8,128)(2,1)S(1)}, u32[]{:S(2)}, u32[]{:S(2)}) collective-permute-start(bf16[144,1024]{1,0:T(8,128)(2,1)S(1)} %maximum_maximum_fusion.own_ref), channel_id=1, source_target_pairs={{0,32},{1,9},{4,36},{5,13},{2,34},{3,11},{6,38},{7,15},{8,40},{9,1... | collective-permute-start | bytes 884744 | tf_op jit(solution)/shard_map/ppermute | solution.py:26
  5.4 5.8 %collective-permute-done.back_ref = bf16[144,1024]{1,0:T(8,128)(2,1)S(1)} collective-permute-done((bf16[144,1024]{1,0:T(8,128)(2,1)S(1)}, bf16[144,1024]{1,0:T(8,128)(2,1)S(1)}, u32[]{:S(2)}, u32[]{:S(2)}) %collective-permute-start) | collective-permute-done | bytes 294944 | tf_op jit(solution)/shard_map/ppermute | solution.py:26
  11.3 0.8 low.1.refs_1_
  12.1 3.1 %collective-permute-start.4 = (bf16[256,1024]{1,0:T(8,128)(2,1)}, bf16[256,1024]{1,0:T(8,128)(2,1)}, u32[]{:S(2)}, u32[]{:S(2)}) collective-permute-start(bf16[256,1024]{1,0:T(8,128)(2,1)} %low.1.refs_1_), channel_id=1, source_target_pairs={{0,1},{1,0},{4,5},{5,4},{2,3},{3,2},{6,7},{7,6},{8,9},{9,8},{12,13... | collective-permute-start | bytes 1572872 | tf_op jit(solution)/shard_map/ppermute | solution.py:26
  15.2 2.7 %collective-permute-start.2 = (bf16[144,1024]{1,0:T(8,128)(2,1)S(1)}, bf16[144,1024]{1,0:T(8,128)(2,1)S(1)}, u32[]{:S(2)}, u32[]{:S(2)}) collective-permute-start(bf16[144,1024]{1,0:T(8,128)(2,1)S(1)} %maximum_maximum_fusion.own_ref), channel_id=1, source_target_pairs={{0,96},{1,25},{4,100},{5,29},{2,98},{3,27},{6,102},{7,31},{8,104},... | collective-permute-start | bytes 884744 | tf_op jit(solution)/shard_map/ppermute | solution.py:26
  17.9 0.3 collective-permute-start.3
  18.3 0.1 pad_add_fusion.place.refs_0_
  18.4 6.4 %collective-permute-done.2.refs_0_ = bf16[144,1024]{1,0:T(8,128)(2,1)S(1)} collective-permute-done((bf16[144,1024]{1,0:T(8,128)(2,1)S(1)}, bf16[144,1024]{1,0:T(8,128)(2,1)S(1)}, u32[]{:S(2)}, u32[]{:S(2)}) %collective-permute-start.2) | collective-permute-done | bytes 294944 | tf_op jit(solution)/shard_map/ppermute | solution.py:26
  24.8 0.3 collective-permute-done.3.refs_1_
  25.1 0.0 collective-permute-done.4.refs_2_.refs_3_
  25.1 0.6 high.1.refs_2_
  25.7 0.5 collective-permute-start.6
  26.1 2.6 %collective-permute-start.5 = (bf16[272,1024]{1,0:T(8,128)(2,1)S(1)}, bf16[272,1024]{1,0:T(8,128)(2,1)S(1)}, u32[]{:S(2)}, u32[]{:S(2)}) collective-permute-start(bf16[272,1024]{1,0:T(8,128)(2,1)S(1)} %high.1.refs_2_), channel_id=1, source_target_pairs={{0,24},{1,97},{4,28},{5,101},{2,26},{3,99},{6,30},{7,103},{8,0},{9... | collective-permute-start | bytes 1671176 | tf_op jit(solution)/shard_map/ppermute | solution.py:26
  28.7 0.0 collective-permute-start.1
  28.7 2.7 %collective-permute-start.11 = (bf16[256,1024]{1,0:T(8,128)(2,1)}, bf16[256,1024]{1,0:T(8,128)(2,1)S(1)}, u32[]{:S(2)}, u32[]{:S(2)}) collective-permute-start(bf16[256,1024]{1,0:T(8,128)(2,1)} %low.1.refs_1_), channel_id=1, source_target_pairs={{0,24},{1,97},{4,28},{5,101},{2,26},{3,99},{6,30},{7,103},{8,0},{9... | collective-permute-start | bytes 1572872 | tf_op jit(solution)/shard_map/ppermute | solution.py:26
  31.4 0.0 collective-permute-done.6.refs_4_
  31.4 0.0 collective-permute-start.10
  31.4 0.0 collective-permute-done.7.refs_5_.w_ref
  31.4 6.1 %chunk.4 = (f32[4,1024,256]{2,1,0:T(8,128)S(1)}, bf16[1024,1024]{1,0:T(8,128)(2,1)S(1)}) custom-call(s32[4]{0:T(128)S(1)} %pad_add_fusion.place.refs_0_, bf16[256,1024]{1,0:T(8,128)(2,1)} %low.1.refs_1_, bf16[272,1024]{1,0:T(8,128)(2,1)S(1)} %high.1.refs_2_, bf16[256,1024]{1,0:T(8,128)(2,1)} %collective-permute-done.4.refs_2_.refs_3_, ...), custom_call_target="tpu_custom_call" | custom-call | flops 5100273664 | bytes 1048576 | tf_op jit(solution)/shard_map/chunk/pallas_call | solution.py:181
  37.5 1.0 %collective-permute-done.1.refs_0_ = bf16[256,1024]{1,0:T(8,128)(2,1)S(1)} collective-permute-done((bf16[256,1024]{1,0:T(8,128)(2,1)}, bf16[256,1024]{1,0:T(8,128)(2,1)S(1)}, u32[]{:S(2)}, u32[]{:S(2)}) %collective-permute-start.1) | collective-permute-done | bytes 524320 | tf_op jit(solution)/shard_map/ppermute | solution.py:26
  38.5 0.0 collective-permute-done.5.refs_1_
  38.5 1.5 %collective-permute-start.13 = (bf16[272,1024]{1,0:T(8,128)(2,1)S(1)}, bf16[272,1024]{1,0:T(8,128)(2,1)S(1)}, u32[]{:S(2)}, u32[]{:S(2)}) collective-permute-start(bf16[272,1024]{1,0:T(8,128)(2,1)S(1)} %get-tuple-element.31.refs_4_), channel_id=1, source_target_pairs={{0,1},{1,0},{4,5},{5,4},{2,3},{3,2},{6,7},{7,6},{8,9},{9,8},{12,13... | collective-permute-start | bytes 1671176 | tf_op jit(solution)/shard_map/ppermute | solution.py:26
  40.0 0.1 collective-permute-start.12
  40.1 2.5 %collective-permute-start.9 = (bf16[272,1024]{1,0:T(8,128)(2,1)S(1)}, bf16[272,1024]{1,0:T(8,128)(2,1)S(1)}, u32[]{:S(2)}, u32[]{:S(2)}) collective-permute-start(bf16[272,1024]{1,0:T(8,128)(2,1)S(1)} %get-tuple-element.31.refs_4_), channel_id=1, source_target_pairs={{0,24},{1,97},{4,28},{5,101},{2,26},{3,99},{6,30},{7,103},{8,0},{9... | collective-permute-start | bytes 1671176 | tf_op jit(solution)/shard_map/ppermute | solution.py:26
  42.5 0.0 collective-permute-done.11.refs_1_
  42.5 0.0 collective-permute-start.8
  42.5 0.0 copy-done
  42.5 1.7 %early.1 = (f32[192,2048]{1,0:T(8,128)S(1)}, f32[192,2048]{1,0:T(8,128)S(1)}, bf16[384,1024]{1,0:T(8,128)(2,1)S(1)}) custom-call(bf16[1024,1024]{1,0:T(8,128)(2,1)S(1)} %collective-permute-done.7.refs_5_.w_ref, bf16[192,1024]{1,0:T(8,128)(2,1)S(1)} %bitcast.25, bf16[1024,1024]{1,0:T(8,128)(2,1)S(1)} %get-tuple-element.29.refs_2_.grads_ref), custom_call_target="tpu_custom_call" | custom-call | flops 1073741824 | bytes 1024 | tf_op jit(solution)/shard_map/early/pallas_call | solution.py:244
  44.2 0.2 collective-permute-done.10.refs_0_
  44.5 0.0 collective-permute-done.12.refs_2_.refs_1_
  44.5 0.0 collective-permute-done.13.refs_3_.refs_4_
  44.5 1.6 %collective-permute-start.16 = (bf16[272,1024]{1,0:T(8,128)(2,1)S(1)}, bf16[272,1024]{1,0:T(8,128)(2,1)S(1)}, u32[]{:S(2)}, u32[]{:S(2)}) collective-permute-start(bf16[272,1024]{1,0:T(8,128)(2,1)S(1)} %get-tuple-element.33.refs_2_), channel_id=1, source_target_pairs={{0,1},{1,0},{4,5},{5,4},{2,3},{3,2},{6,7},{7,6},{8,9},{9,8},{12,13... | collective-permute-start | bytes 1671176 | tf_op jit(solution)/shard_map/ppermute | solution.py:26
  46.0 0.3 collective-permute-start.17
  46.3 6.2 %chunk.5 = (f32[192,2048]{1,0:T(8,128)S(1)}, f32[4,1024,256]{2,1,0:T(8,128)S(1)}) custom-call(s32[4]{0:T(128)S(1)} %pad_add_fusion.place.refs_0_, bf16[256,1024]{1,0:T(8,128)(2,1)S(1)} %get-tuple-element.30.refs_1_, bf16[272,1024]{1,0:T(8,128)(2,1)S(1)} %get-tuple-element.33.refs_2_, ...), custom_call_target="tpu_custom_call", output_to_operand_aliasing={{0}: (8, {}), {1}: (6, {})} | custom-call | flops 5100273664 | bytes 1048576 | tf_op jit(solution)/shard_map/chunk/pallas_call | solution.py:181
  52.5 0.0 collective-permute-done.8.refs_0_
  52.5 0.0 collective-permute-done.9.refs_1_
  52.5 0.4 collective-permute-start.15
  52.9 0.2 collective-permute-start.14
  53.1 0.0 collective-permute-done.17.refs_3_
  53.1 0.0 collective-permute-done.16.refs_2_
  53.1 6.2 %chunk.6 = (f32[192,2048]{1,0:T(8,128)S(1)}, f32[4,1024,256]{2,1,0:T(8,128)S(1)}) custom-call(s32[4]{0:T(128)S(1)} %pad_add_fusion.place.refs_0_, bf16[256,1024]{1,0:T(8,128)(2,1)S(1)} %collective-permute-done.12.refs_2_.refs_1_, bf16[272,1024]{1,0:T(8,128)(2,1)S(1)} %collective-permute-done.16.refs_2_, ...), custom_call_target="tpu_custom_call", output_to_operand_aliasing={{0}: (8, {}), {1}: (6, {})} | custom-call | flops 5100273664 | bytes 1048576 | tf_op jit(solution)/shard_map/chunk/pallas_call | solution.py:181
  59.3 0.0 collective-permute-done.14.refs_3_
  59.3 0.0 collective-permute-done.15.refs_4_
  59.3 6.6 %chunk.7 = (f32[192,2048]{1,0:T(8,128)S(1)}, f32[192,2048]{1,0:T(8,128)S(1)}, bf16[1024,256]{1,0:T(8,128)(2,1)}, bf16[1024,256]{1,0:T(8,128)(2,1)}, bf16[1024,25...) custom-call(s32[4]{0:T(128)S(1)} %pad_add_fusion.place.refs_0_, ...), custom_call_target="tpu_custom_call", output_to_operand_aliasing={{0}: (8, {}), {1}: (9, {})} | custom-call | flops 5100273664 | bytes 1048576 | tf_op jit(solution)/shard_map/chunk/pallas_call | solution.py:181
  65.9 0.4 collective-permute-start.18
  66.4 0.0 collective-permute-start.19
  66.4 2.5 %collective-permute-start.20 = (bf16[1024,256]{1,0:T(8,128)(2,1)}, bf16[1024,256]{1,0:T(8,128)(2,1)S(1)}, u32[]{:S(2)}, u32[]{:S(2)}) collective-permute-start(bf16[1024,256]{1,0:T(8,128)(2,1)} %get-tuple-element.47), channel_id=1, source_target_pairs={{0,2},{1,4},{4,3},{5,7},{2,0},{3,6},{6,1},{7,5},{8,10},{9,12},{12,... | collective-permute-start | bytes 1572872 | tf_op jit(solution)/shard_map/ppermute | solution.py:26
  68.8 1.6 %collective-permute-start.21 = (bf16[1024,256]{1,0:T(8,128)(2,1)}, bf16[1024,256]{1,0:T(8,128)(2,1)S(1)}, u32[]{:S(2)}, u32[]{:S(2)}) collective-permute-start(bf16[1024,256]{1,0:T(8,128)(2,1)} %get-tuple-element.48), channel_id=1, source_target_pairs={{0,1},{1,7},{4,0},{5,4},{2,3},{3,5},{6,2},{7,6},{8,9},{9,15},{12,8... | collective-permute-start | bytes 1572872 | tf_op jit(solution)/shard_map/ppermute | solution.py:26
  70.4 4.4 %collective-permute-start.22 = (bf16[1024,256]{1,0:T(8,128)(2,1)}, bf16[1024,256]{1,0:T(8,128)(2,1)S(1)}, u32[]{:S(2)}, u32[]{:S(2)}) collective-permute-start(bf16[1024,256]{1,0:T(8,128)(2,1)} %get-tuple-element.49), channel_id=1, source_target_pairs={{0,0},{1,6},{4,1},{5,5},{2,2},{3,4},{6,3},{7,7},{8,8},{9,14},{12,9... | collective-permute-start | bytes 1572872 | tf_op jit(solution)/shard_map/ppermute | solution.py:26
  74.8 0.0 collective-permute-done.18.refs_1_
  74.8 1.6 %pack.1 = bf16[16,192,128]{2,1,0:T(8,128)(2,1)} custom-call(s32[4]{0:T(128)S(1)} %pad_add_fusion.place.refs_0_, f32[192,2048]{1,0:T(8,128)S(1)} %get-tuple-element.44.refs_0_, f32[192,2048]{1,0:T(8,128)S(1)} %collective-permute-done.18.refs_1_), custom_call_target="tpu_custom_call" | custom-call | flops 1000000 | bytes 1024 | tf_op jit(solution)/shard_map/pack/pallas_call | solution.py:244
  76.5 6.1 %all-to-all-start = ((bf16[16,192,128]{2,1,0:T(8,128)(2,1)}), bf16[16,192,128]{2,1,0:T(8,128)(2,1)S(1)}, u32[]{:S(2)}, u32[]{:S(2)}) async-start(bf16[16,192,128]{2,1,0:T(8,128)(2,1)} %pack.1), calls=%async_computation | async-start | bytes 1572864 | tf_op jit(solution)/shard_map/all_to_all | solution.py:322
  82.6 0.0 copy-start.1
  82.6 0.0 collective-permute-done.19.refs_0_
  82.6 10.7 %collective-permute-done.20.refs_1_ = bf16[1024,256]{1,0:T(8,128)(2,1)S(1)} collective-permute-done((bf16[1024,256]{1,0:T(8,128)(2,1)}, bf16[1024,256]{1,0:T(8,128)(2,1)S(1)}, u32[]{:S(2)}, u32[]{:S(2)}) %collective-permute-start.20) | collective-permute-done | bytes 524320 | tf_op jit(solution)/shard_map/ppermute | solution.py:26
  93.3 0.0 collective-permute-done.21.refs_2_
  93.3 0.0 collective-permute-done.22.refs_3_
  93.3 1.1 %join.1 = (bf16[1024,256]{1,0:T(8,128)(2,1)}, f32[8,128]{1,0:T(8,128)S(1)}) custom-call(bf16[1024,256]{1,0:T(8,128)(2,1)S(1)} %collective-permute-done.19.refs_0_, bf16[1024,256]{1,0:T(8,128)(2,1)S(1)} %collective-permute-done.20.refs_1_, bf16[1024,256]{1,0:T(8,128)(2,1)S(1)} %collective-permute-done.21.refs_2_, ...), custom_call_target="tpu_custom_call" | custom-call | flops 99999997952 | bytes 1024 | tf_op jit(solution)/shard_map/join/pallas_call | solution.py:244
  94.4 0.5 all-to-all-done.parts_ref
  94.9 1.2 %decode.1 = bf16[128,1024]{1,0:T(8,128)(2,1)} custom-call(bf16[16,192,128]{2,1,0:T(8,128)(2,1)S(1)} %all-to-all-done.parts_ref, bf16[192,1024]{1,0:T(8,128)(2,1)S(1)} %copy-done.1, f32[8,128]{1,0:T(8,128)S(1)} %get-tuple-element.50.after_ref), custom_call_target="tpu_custom_call" | custom-call | flops 1000000 | bytes 1024 | tf_op jit(solution)/shard_map/decode/pallas_call | solution.py:244
  (8 shorter events, 0.0 us)
Async XLA Ops:
  0.6 30.8 %collective-permute-start.7 = (bf16[1024,1024]{1,0:T(8,128)(2,1)}, bf16[1024,1024]{1,0:T(8,128)(2,1)S(1)}, u32[]{:S(2)}, u32[]{:S(2)}) collective-permute-start(bf16[1024,1024]{1,0:T(8,128)(2,1)} %param.9), channel_id=1, source_target_pairs={{0,4},{1,0},{4,5},{5,1},{2,6},{3,2},{6,7},{7,3},{8,12},{9,8},{12,1... | collective-permute-start | bytes 6291464 | tf_op jit(solution)/shard_map/ppermute | solution.py:26
  4.0 7.3 %collective-permute-start = (bf16[144,1024]{1,0:T(8,128)(2,1)S(1)}, bf16[144,1024]{1,0:T(8,128)(2,1)S(1)}, u32[]{:S(2)}, u32[]{:S(2)}) collective-permute-start(bf16[144,1024]{1,0:T(8,128)(2,1)S(1)} %maximum_maximum_fusion.own_ref), channel_id=1, source_target_pairs={{0,32},{1,9},{4,36},{5,13},{2,34},{3,11},{6,38},{7,15},{8,40},{9,1... | collective-permute-start | bytes 884744 | tf_op jit(solution)/shard_map/ppermute | solution.py:26
  12.1 12.9 %collective-permute-start.4 = (bf16[256,1024]{1,0:T(8,128)(2,1)}, bf16[256,1024]{1,0:T(8,128)(2,1)}, u32[]{:S(2)}, u32[]{:S(2)}) collective-permute-start(bf16[256,1024]{1,0:T(8,128)(2,1)} %low.1.refs_1_), channel_id=1, source_target_pairs={{0,1},{1,0},{4,5},{5,4},{2,3},{3,2},{6,7},{7,6},{8,9},{9,8},{12,13... | collective-permute-start | bytes 1572872 | tf_op jit(solution)/shard_map/ppermute | solution.py:26
  15.2 9.6 %collective-permute-start.2 = (bf16[144,1024]{1,0:T(8,128)(2,1)S(1)}, bf16[144,1024]{1,0:T(8,128)(2,1)S(1)}, u32[]{:S(2)}, u32[]{:S(2)}) collective-permute-start(bf16[144,1024]{1,0:T(8,128)(2,1)S(1)} %maximum_maximum_fusion.own_ref), channel_id=1, source_target_pairs={{0,96},{1,25},{4,100},{5,29},{2,98},{3,27},{6,102},{7,31},{8,104},... | collective-permute-start | bytes 884744 | tf_op jit(solution)/shard_map/ppermute | solution.py:26
  17.9 7.1 %collective-permute-start.3 = (bf16[144,1024]{1,0:T(8,128)(2,1)S(1)}, bf16[144,1024]{1,0:T(8,128)(2,1)S(1)}, u32[]{:S(2)}, u32[]{:S(2)}) collective-permute-start(bf16[144,1024]{1,0:T(8,128)(2,1)S(1)} %maximum_maximum_fusion.own_ref), channel_id=1, source_target_pairs={{0,64},{1,17},{4,68},{5,21},{2,66},{3,19},{6,70},{7,23},{8,72},{9,... | collective-permute-start | bytes 884744 | tf_op jit(solution)/shard_map/ppermute | solution.py:26
  25.7 5.7 %collective-permute-start.6 = (bf16[272,1024]{1,0:T(8,128)(2,1)S(1)}, bf16[272,1024]{1,0:T(8,128)(2,1)S(1)}, u32[]{:S(2)}, u32[]{:S(2)}) collective-permute-start(bf16[272,1024]{1,0:T(8,128)(2,1)S(1)} %high.1.refs_2_), channel_id=1, source_target_pairs={{0,1},{1,0},{4,5},{5,4},{2,3},{3,2},{6,7},{7,6},{8,9},{9,8},{12,13... | collective-permute-start | bytes 1671176 | tf_op jit(solution)/shard_map/ppermute | solution.py:26
  26.1 12.3 %collective-permute-start.5 = (bf16[272,1024]{1,0:T(8,128)(2,1)S(1)}, bf16[272,1024]{1,0:T(8,128)(2,1)S(1)}, u32[]{:S(2)}, u32[]{:S(2)}) collective-permute-start(bf16[272,1024]{1,0:T(8,128)(2,1)S(1)} %high.1.refs_2_), channel_id=1, source_target_pairs={{0,24},{1,97},{4,28},{5,101},{2,26},{3,99},{6,30},{7,103},{8,0},{9... | collective-permute-start | bytes 1671176 | tf_op jit(solution)/shard_map/ppermute | solution.py:26
  28.7 9.7 %collective-permute-start.1 = (bf16[256,1024]{1,0:T(8,128)(2,1)}, bf16[256,1024]{1,0:T(8,128)(2,1)S(1)}, u32[]{:S(2)}, u32[]{:S(2)}) collective-permute-start(bf16[256,1024]{1,0:T(8,128)(2,1)} %low.1.refs_1_), channel_id=1, source_target_pairs={{0,8},{1,33},{4,12},{5,37},{2,10},{3,35},{6,14},{7,39},{8,16},{9,4... | collective-permute-start | bytes 1572872 | tf_op jit(solution)/shard_map/ppermute | solution.py:26
  28.7 13.8 %collective-permute-start.11 = (bf16[256,1024]{1,0:T(8,128)(2,1)}, bf16[256,1024]{1,0:T(8,128)(2,1)S(1)}, u32[]{:S(2)}, u32[]{:S(2)}) collective-permute-start(bf16[256,1024]{1,0:T(8,128)(2,1)} %low.1.refs_1_), channel_id=1, source_target_pairs={{0,24},{1,97},{4,28},{5,101},{2,26},{3,99},{6,30},{7,103},{8,0},{9... | collective-permute-start | bytes 1572872 | tf_op jit(solution)/shard_map/ppermute | solution.py:26
  31.4 13.0 %collective-permute-start.10 = (bf16[272,1024]{1,0:T(8,128)(2,1)S(1)}, bf16[272,1024]{1,0:T(8,128)(2,1)S(1)}, u32[]{:S(2)}, u32[]{:S(2)}) collective-permute-start(bf16[272,1024]{1,0:T(8,128)(2,1)S(1)} %high.1.refs_2_), channel_id=1, source_target_pairs={{0,8},{1,33},{4,12},{5,37},{2,10},{3,35},{6,14},{7,39},{8,16},{9,4... | collective-permute-start | bytes 1671176 | tf_op jit(solution)/shard_map/ppermute | solution.py:26
  38.5 4.1 %copy-start = (bf16[1024,192]{0,1:T(8,128)(2,1)S(1)}, bf16[1024,192]{0,1:T(8,128)(2,1)}, u32[]{:S(2)}) copy-start(bf16[1024,192]{0,1:T(8,128)(2,1)} %param.10) | copy-start | bytes 1179652
  38.5 6.0 %collective-permute-start.13 = (bf16[272,1024]{1,0:T(8,128)(2,1)S(1)}, bf16[272,1024]{1,0:T(8,128)(2,1)S(1)}, u32[]{:S(2)}, u32[]{:S(2)}) collective-permute-start(bf16[272,1024]{1,0:T(8,128)(2,1)S(1)} %get-tuple-element.31.refs_4_), channel_id=1, source_target_pairs={{0,1},{1,0},{4,5},{5,4},{2,3},{3,2},{6,7},{7,6},{8,9},{9,8},{12,13... | collective-permute-start | bytes 1671176 | tf_op jit(solution)/shard_map/ppermute | solution.py:26
  40.0 4.5 %collective-permute-start.12 = (bf16[256,1024]{1,0:T(8,128)(2,1)S(1)}, bf16[256,1024]{1,0:T(8,128)(2,1)S(1)}, u32[]{:S(2)}, u32[]{:S(2)}) collective-permute-start(bf16[256,1024]{1,0:T(8,128)(2,1)S(1)} %get-tuple-element.30.refs_1_), channel_id=1, source_target_pairs={{0,1},{1,0},{4,5},{5,4},{2,3},{3,2},{6,7},{7,6},{8,9},{9,8},{12,13... | collective-permute-start | bytes 1572872 | tf_op jit(solution)/shard_map/ppermute | solution.py:26
  40.1 12.4 %collective-permute-start.9 = (bf16[272,1024]{1,0:T(8,128)(2,1)S(1)}, bf16[272,1024]{1,0:T(8,128)(2,1)S(1)}, u32[]{:S(2)}, u32[]{:S(2)}) collective-permute-start(bf16[272,1024]{1,0:T(8,128)(2,1)S(1)} %get-tuple-element.31.refs_4_), channel_id=1, source_target_pairs={{0,24},{1,97},{4,28},{5,101},{2,26},{3,99},{6,30},{7,103},{8,0},{9... | collective-permute-start | bytes 1671176 | tf_op jit(solution)/shard_map/ppermute | solution.py:26
  42.5 9.9 %collective-permute-start.8 = (bf16[256,1024]{1,0:T(8,128)(2,1)S(1)}, bf16[256,1024]{1,0:T(8,128)(2,1)S(1)}, u32[]{:S(2)}, u32[]{:S(2)}) collective-permute-start(bf16[256,1024]{1,0:T(8,128)(2,1)S(1)} %get-tuple-element.30.refs_1_), channel_id=1, source_target_pairs={{0,8},{1,33},{4,12},{5,37},{2,10},{3,35},{6,14},{7,39},{8,16},{9,4... | collective-permute-start | bytes 1572872 | tf_op jit(solution)/shard_map/ppermute | solution.py:26
  44.5 8.6 %collective-permute-start.16 = (bf16[272,1024]{1,0:T(8,128)(2,1)S(1)}, bf16[272,1024]{1,0:T(8,128)(2,1)S(1)}, u32[]{:S(2)}, u32[]{:S(2)}) collective-permute-start(bf16[272,1024]{1,0:T(8,128)(2,1)S(1)} %get-tuple-element.33.refs_2_), channel_id=1, source_target_pairs={{0,1},{1,0},{4,5},{5,4},{2,3},{3,2},{6,7},{7,6},{8,9},{9,8},{12,13... | collective-permute-start | bytes 1671176 | tf_op jit(solution)/shard_map/ppermute | solution.py:26
  46.0 7.1 %collective-permute-start.17 = (bf16[256,1024]{1,0:T(8,128)(2,1)S(1)}, bf16[256,1024]{1,0:T(8,128)(2,1)S(1)}, u32[]{:S(2)}, u32[]{:S(2)}) collective-permute-start(bf16[256,1024]{1,0:T(8,128)(2,1)S(1)} %get-tuple-element.34.refs_3_), channel_id=1, source_target_pairs={{0,1},{1,0},{4,5},{5,4},{2,3},{3,2},{6,7},{7,6},{8,9},{9,8},{12,13... | collective-permute-start | bytes 1572872 | tf_op jit(solution)/shard_map/ppermute | solution.py:26
  52.5 6.8 %collective-permute-start.15 = (bf16[272,1024]{1,0:T(8,128)(2,1)S(1)}, bf16[272,1024]{1,0:T(8,128)(2,1)S(1)}, u32[]{:S(2)}, u32[]{:S(2)}) collective-permute-start(bf16[272,1024]{1,0:T(8,128)(2,1)S(1)} %get-tuple-element.39.refs_2_), channel_id=1, source_target_pairs={{0,1},{1,0},{4,5},{5,4},{2,3},{3,2},{6,7},{7,6},{8,9},{9,8},{12,13... | collective-permute-start | bytes 1671176 | tf_op jit(solution)/shard_map/ppermute | solution.py:26
  52.9 6.3 %collective-permute-start.14 = (bf16[256,1024]{1,0:T(8,128)(2,1)S(1)}, bf16[256,1024]{1,0:T(8,128)(2,1)S(1)}, u32[]{:S(2)}, u32[]{:S(2)}) collective-permute-start(bf16[256,1024]{1,0:T(8,128)(2,1)S(1)} %get-tuple-element.38.refs_1_), channel_id=1, source_target_pairs={{0,1},{1,0},{4,5},{5,4},{2,3},{3,2},{6,7},{7,6},{8,9},{9,8},{12,13... | collective-permute-start | bytes 1572872 | tf_op jit(solution)/shard_map/ppermute | solution.py:26
  65.9 8.9 %collective-permute-start.18 = (f32[192,2048]{1,0:T(8,128)S(1)}, f32[192,2048]{1,0:T(8,128)S(1)}, u32[]{:S(2)}, u32[]{:S(2)}) collective-permute-start(f32[192,2048]{1,0:T(8,128)S(1)} %get-tuple-element.45), channel_id=1, source_target_pairs={{0,1},{1,0},{4,5},{5,4},{2,3},{3,2},{6,7},{7,6},{8,9},{9,8},{12,13... | collective-permute-start | bytes 4718600 | tf_op jit(solution)/shard_map/ppermute | solution.py:26
  66.4 16.2 %collective-permute-start.19 = (bf16[1024,256]{1,0:T(8,128)(2,1)}, bf16[1024,256]{1,0:T(8,128)(2,1)S(1)}, u32[]{:S(2)}, u32[]{:S(2)}) collective-permute-start(bf16[1024,256]{1,0:T(8,128)(2,1)} %get-tuple-element.46), channel_id=1, source_target_pairs={{0,3},{1,5},{4,2},{5,6},{2,1},{3,7},{6,0},{7,4},{8,11},{9,13},{12,... | collective-permute-start | bytes 1572872 | tf_op jit(solution)/shard_map/ppermute | solution.py:26
  66.4 26.9 %collective-permute-start.20 = (bf16[1024,256]{1,0:T(8,128)(2,1)}, bf16[1024,256]{1,0:T(8,128)(2,1)S(1)}, u32[]{:S(2)}, u32[]{:S(2)}) collective-permute-start(bf16[1024,256]{1,0:T(8,128)(2,1)} %get-tuple-element.47), channel_id=1, source_target_pairs={{0,2},{1,4},{4,3},{5,7},{2,0},{3,6},{6,1},{7,5},{8,10},{9,12},{12,... | collective-permute-start | bytes 1572872 | tf_op jit(solution)/shard_map/ppermute | solution.py:26
  68.8 24.5 %collective-permute-start.21 = (bf16[1024,256]{1,0:T(8,128)(2,1)}, bf16[1024,256]{1,0:T(8,128)(2,1)S(1)}, u32[]{:S(2)}, u32[]{:S(2)}) collective-permute-start(bf16[1024,256]{1,0:T(8,128)(2,1)} %get-tuple-element.48), channel_id=1, source_target_pairs={{0,1},{1,7},{4,0},{5,4},{2,3},{3,5},{6,2},{7,6},{8,9},{9,15},{12,8... | collective-permute-start | bytes 1572872 | tf_op jit(solution)/shard_map/ppermute | solution.py:26
  70.4 22.9 %collective-permute-start.22 = (bf16[1024,256]{1,0:T(8,128)(2,1)}, bf16[1024,256]{1,0:T(8,128)(2,1)S(1)}, u32[]{:S(2)}, u32[]{:S(2)}) collective-permute-start(bf16[1024,256]{1,0:T(8,128)(2,1)} %get-tuple-element.49), channel_id=1, source_target_pairs={{0,0},{1,6},{4,1},{5,5},{2,2},{3,4},{6,3},{7,7},{8,8},{9,14},{12,9... | collective-permute-start | bytes 1572872 | tf_op jit(solution)/shard_map/ppermute | solution.py:26
  76.5 18.4 %all-to-all-start = ((bf16[16,192,128]{2,1,0:T(8,128)(2,1)}), bf16[16,192,128]{2,1,0:T(8,128)(2,1)S(1)}, u32[]{:S(2)}, u32[]{:S(2)}) async-start(bf16[16,192,128]{2,1,0:T(8,128)(2,1)} %pack.1), calls=%async_computation | async-start | bytes 1572864 | tf_op jit(solution)/shard_map/all_to_all | solution.py:322
  82.6 12.3 %copy-start.1 = (bf16[192,1024]{1,0:T(8,128)(2,1)S(1)}, bf16[192,1024]{1,0:T(8,128)(2,1)}, u32[]{:S(2)}) copy-start(bf16[192,1024]{1,0:T(8,128)(2,1)} %dec_ref.1) | copy-start | bytes 1179652
